TPU v7x, 32 devices: a whole 2x2x4 slice. The times are simulated.
32 devices in a mesh: dx: 4 (over x, core), dy: 4 (over z), solid: 2 (over y).
Axes of the slice: x: 2, y: 2, z: 4, core: 2. Of those that a mesh axis runs over, the one named last changes fastest.
Arguments:
- velocity: float32 [3, 4, 4, 4, 4, 16, 256], P(None, None, None, None, 'dx', 'dy', 'solid'), may hold values from -6 to 6
- viscosity: float32 [4, 16, 256], P('dx', 'dy', 'solid'), may hold values from 0.5 to 4
- cell_config: int32 [4, 16, 256], P('dx', 'dy', 'solid'), may hold values from 0 to 7
- constraint_offsets: float32 [8, 64, 64], replicated, may hold values from -0.24 to 0.24
- slot_cells: int32 [4, 8, 64], P('dx', ('dy', 'solid')), may hold values from -1 to 511, as said below
- point_coords: float32 [3, 4, 8, 64], P(None, 'dx', ('dy', 'solid')), may hold values from 0 to 1
- strain_offsets: float32 [3, 3, 4, 8, 64], P(None, None, 'dx', ('dy', 'solid')), may hold values from -1.5 to 1.5
- solid_velocity: float32 [3, 4, 8, 64], P(None, 'dx', ('dy', 'solid')), may hold values from -6 to 6
Outputs:
- fluid_out: float32 [3, 4, 4, 4, 4, 16, 256], P(None, None, None, None, 'dx', 'dy', 'solid')
- new_deform: float32 [3, 3, 4, 8, 64], P(None, None, 'dx', ('dy', 'solid'))
Inputs may be any that keep to these rules, and one draw needn't show every extreme that they name: `slot_cells`: an entry is -1 for an empty slot, else a cell of the owner numbered with x slowest and z fastest. Slots h * 8 to (h + 1) * 8 - 1 of owner o hold the points that device h keeps.
All inputs are finite; a program needn't handle non-finite values.
Results may differ from a plain program's by a relative error of at most 0.0003.
Values sent between devices are 32-bit elements; how exact they have to be, the bound alone decides.
No kernel may reach another device: no remote copies, remote signals or barrier semaphores. Data moves between devices by JAX's collectives and lax.ppermute only.
A program may use at most 64 MiB of HBM per device.

v0:
```python
import jax
import jax.numpy as jnp
import numpy as np
from jax import lax
from jax.sharding import PartitionSpec as P

NCONF = 8


PRECISE = lax.Precision.HIGHEST
TIME_STEP = 0.05
SPRING_RATE = 2.0
PENALTY = 4.0
STIFFNESS = np.array(
    [[2.0, -1.0, 0.0, 0.0], [-1.0, 2.0, -1.0, 0.0], [0.0, -1.0, 2.0, -1.0], [0.0, 0.0, -1.0, 2.0]]
)
NODE_POINTS = (0.0, 1.0 / 3.0, 2.0 / 3.0, 1.0)


def extended(shard, sides, width):
    for axis, dim in sides:
        peers, length = (lax.axis_size(axis), shard.shape[dim])
        up = [(i, (i + 1) % peers) for i in range(peers - 1)]
        down = [(j, i) for i, j in up]
        last = lax.slice_in_dim(shard, length - width, length, axis=dim)
        initial = lax.slice_in_dim(shard, 0, width, axis=dim)
        before = lax.ppermute(last, axis, up)
        after = lax.ppermute(initial, axis, down)
        shard = jnp.concatenate([before, shard, after], axis=dim)
    return shard


def lagrange(coord):
    values = []
    slopes = []
    for which in range(4):
        others = [NODE_POINTS[j] for j in range(4) if j != which]
        denom = 1.0
        for other in others:
            denom = denom * (NODE_POINTS[which] - other)
        first = coord - others[0]
        second = coord - others[1]
        third = coord - others[2]
        values.append(first * second * third / denom)
        slopes.append((second * third + first * third + first * second) / denom)
    return (jnp.stack(values), jnp.stack(slopes))


def constrain(flat, config, offsets, transpose):
    eye = jnp.eye(64, dtype=flat.dtype)
    result = jnp.zeros_like(flat)
    for which in range(NCONF):
        matrix = eye + offsets[which]
        form = "ji,mjn->min" if transpose else "ij,mjn->min"
        product = jnp.einsum(form, matrix, flat, precision=PRECISE)
        result = result + jnp.where(config == which, product, 0.0)
    return result


def operate(field, planes, viscosity):
    lower_x, upper_x, lower_y, upper_y, lower_z, upper_z = planes
    stiff = jnp.asarray(STIFFNESS, field.dtype)
    lap = jnp.einsum("ia,kabcxyz->kibcxyz", stiff, field, precision=PRECISE)
    lap = lap + jnp.einsum("ib,kabcxyz->kaicxyz", stiff, field, precision=PRECISE)
    lap = lap + jnp.einsum("ic,kabcxyz->kabixyz", stiff, field, precision=PRECISE)
    result = field + viscosity * lap
    result = result.at[:, 0].add(PENALTY * (field[:, 0] - lower_x))
    result = result.at[:, 3].add(PENALTY * (field[:, 3] - upper_x))
    result = result.at[:, :, 0].add(PENALTY * (field[:, :, 0] - lower_y))
    result = result.at[:, :, 3].add(PENALTY * (field[:, :, 3] - upper_y))
    result = result.at[:, :, :, 0].add(PENALTY * (field[:, :, :, 0] - lower_z))
    result = result.at[:, :, :, 3].add(PENALTY * (field[:, :, :, 3] - upper_z))
    return result


def evaluate(gathered, coords):
    field = gathered.reshape(3, 4, 4, 4, -1)
    value_x, slope_x = lagrange(coords[0])
    value_y, slope_y = lagrange(coords[1])
    value_z, slope_z = lagrange(coords[2])
    along_zp = jnp.einsum("kabcs,cs->kabs", field, value_z, precision=PRECISE)
    along_zd = jnp.einsum("kabcs,cs->kabs", field, slope_z, precision=PRECISE)
    plain = jnp.einsum("kabs,bs->kas", along_zp, value_y, precision=PRECISE)
    dery = jnp.einsum("kabs,bs->kas", along_zp, slope_y, precision=PRECISE)
    derz = jnp.einsum("kabs,bs->kas", along_zd, value_y, precision=PRECISE)
    vel = jnp.einsum("kas,as->ks", plain, value_x, precision=PRECISE)
    grad_x = jnp.einsum("kas,as->ks", plain, slope_x, precision=PRECISE)
    grad_y = jnp.einsum("kas,as->ks", dery, value_x, precision=PRECISE)
    grad_z = jnp.einsum("kas,as->ks", derz, value_x, precision=PRECISE)
    return (vel, jnp.stack([grad_x, grad_y, grad_z], axis=1))


def solid_update(vel, grad, strain, motion):
    eye = jnp.eye(3, dtype=strain.dtype)[:, :, None]
    deform = eye + strain
    moved = deform + TIME_STEP * jnp.einsum("kjs,jls->kls", grad, deform, precision=PRECISE)
    stress = jnp.einsum("kls,mls->kms", moved, moved, precision=PRECISE) - eye
    drag = SPRING_RATE * (motion - vel)
    return (moved, stress, drag)


def spread_nodes(stress, drag, coords):
    value_x, slope_x = lagrange(coords[0])
    value_y, slope_y = lagrange(coords[1])
    value_z, slope_z = lagrange(coords[2])
    shape_x = jnp.einsum("as,bs,cs->abcs", slope_x, value_y, value_z, precision=PRECISE)
    shape_y = jnp.einsum("as,bs,cs->abcs", value_x, slope_y, value_z, precision=PRECISE)
    shape_z = jnp.einsum("as,bs,cs->abcs", value_x, value_y, slope_z, precision=PRECISE)
    whole = jnp.einsum("as,bs,cs->abcs", value_x, value_y, value_z, precision=PRECISE)
    nodal = jnp.einsum("ks,abcs->kabcs", stress[:, 0], shape_x, precision=PRECISE)
    nodal = nodal + jnp.einsum("ks,abcs->kabcs", stress[:, 1], shape_y, precision=PRECISE)
    nodal = nodal + jnp.einsum("ks,abcs->kabcs", stress[:, 2], shape_z, precision=PRECISE)
    nodal = jnp.einsum("ks,abcs->kabcs", drag, whole, precision=PRECISE) - nodal
    return nodal.reshape(192, -1)


def shards(
    velocity,
    viscosity,
    cell_config,
    constraint_offsets,
    slot_cells,
    point_coords,
    strain_offsets,
    solid_velocity,
):
    shape = velocity.shape
    count = shape[4] * shape[5] * shape[6]
    config = cell_config.reshape(count)
    flat = constrain(velocity.reshape(3, 64, count), config, constraint_offsets, False)
    constrained = flat.reshape(shape)
    sides_x = jnp.stack([constrained[:, 0], constrained[:, 3]], axis=1)
    sides_y = jnp.stack([constrained[:, :, 0], constrained[:, :, 3]], axis=1)
    sides_z = jnp.stack([constrained[:, :, :, 0], constrained[:, :, :, 3]], axis=1)
    wide_x = extended(sides_x, (("dx", 4),), 1)
    wide_y = extended(sides_y, (("dy", 5),), 1)
    wide_z = extended(sides_z, (("solid", 6),), 1)
    planes = (
        wide_x[:, 1, :, :, :-2],
        wide_x[:, 0, :, :, 2:],
        wide_y[:, 1, :, :, :, :-2],
        wide_y[:, 0, :, :, :, 2:],
        wide_z[:, 1, :, :, :, :, :-2],
        wide_z[:, 0, :, :, :, :, 2:],
    )
    applied = operate(constrained, planes, viscosity)
    block = flat.reshape(192, count)
    targets = slot_cells[0, 0]
    live = targets >= 0
    safe = jnp.where(live, targets, 0)
    coords = point_coords[:, 0, 0]
    strain = strain_offsets[:, :, 0, 0]
    motion = solid_velocity[:, 0, 0]
    gathered = jnp.where(live[None, :], jnp.take(block, safe, axis=1), 0.0)
    vel, grad = evaluate(gathered, coords)
    packed = jnp.concatenate([vel, grad.reshape(9, -1)], axis=0)
    received = lax.all_to_all(packed, ("dy", "solid"), split_axis=1, concat_axis=1, tiled=True)
    moved, stress, drag = solid_update(received[:3], received[3:].reshape(3, 3, -1), strain, motion)
    reply = jnp.concatenate([stress.reshape(9, -1), drag], axis=0)
    returned = lax.all_to_all(reply, ("dy", "solid"), split_axis=1, concat_axis=1, tiled=True)
    nodal = spread_nodes(returned[:9].reshape(3, 3, -1), returned[9:], coords)
    nodal = jnp.where(live[None, :], nodal, 0.0)
    force = jnp.zeros_like(block).at[:, safe].add(nodal)
    total = applied.reshape(3, 64, count) - force.reshape(3, 64, count)
    fluid_out = constrain(total, config, constraint_offsets, True).reshape(shape)
    return (fluid_out, moved[:, :, None, None, :])


def solution(mesh):
    return jax.shard_map(
        shards,
        mesh=mesh,
        in_specs=(
            P(None, None, None, None, "dx", "dy", "solid"),
            P("dx", "dy", "solid"),
            P("dx", "dy", "solid"),
            P(),
            P("dx", ("dy", "solid"), None),
            P(None, "dx", ("dy", "solid"), None),
            P(None, None, "dx", ("dy", "solid"), None),
            P(None, "dx", ("dy", "solid"), None),
        ),
        out_specs=(
            P(None, None, None, None, "dx", "dy", "solid"),
            P(None, None, "dx", ("dy", "solid"), None),
        ),
        check_vma=False,
    )
```

profile of v0, /device:TPU:6, one launch (start us, length us, event | category | flops | bytes accessed | tf_op | source)
XLA Modules:
  0.0 100.4 jit_solution(17596153238362744195)
XLA Ops:
  0.6 1.2 %reshape.1165 = f32[3,64,512]{2,1,0:T(8,128)S(1)} reshape(f32[3,4,4,4,1,4,128]{6,5,4,3,2,1,0:T(4,128)} %param.21) | data formatting | bytes 786432 | tf_op jit(solution)/shard_map/reshape | solution.py:130
  2.0 0.5 convolution_select_fusion.8
  2.5 0.5 convolution_select_fusion.9
  3.0 0.5 convolution_select_fusion.10
  3.5 0.5 convolution_select_fusion.11
  3.9 0.5 convolution_select_fusion.12
  4.4 0.5 convolution_select_fusion.13
  4.9 0.5 convolution_select_fusion.14
  5.4 0.6 fusion.6
  6.1 0.3 copy.91
  6.7 1.9 %collective-permute-start = (f32[3,2,4,4,1,4,128]{6,1,5,3,2,0,4:T(2,128)S(1)}, f32[3,2,4,4,1,4,128]{6,1,5,3,2,0,4:T(2,128)}, u32[]{:S(2)}, u32[]{:S(2)}) collective-permute-start(f32[3,2,4,4,1,4,128]{6,1,5,3,2,0,4:T(2,128)S(1)} %pad_maximum_fusion.1), channel_id=1, source_target_pairs={{0,8},{8,16},{16,24},{1,9},{9,17},{17,25},{2,10},{10,18},{18,26},{... | collective-permute-start | bytes 589832 | tf_op jit(solution)/shard_map/ppermute | solution.py:27
  8.7 3.6 %collective-permute-start.1 = (f32[3,2,4,4,1,4,128]{6,1,5,3,2,0,4:T(2,128)S(1)}, f32[3,2,4,4,1,4,128]{6,1,5,3,2,0,4:T(2,128)}, u32[]{:S(2)}, u32[]{:S(2)}) collective-permute-start(f32[3,2,4,4,1,4,128]{6,1,5,3,2,0,4:T(2,128)S(1)} %pad_maximum_fusion.1), channel_id=1, source_target_pairs={{8,0},{16,8},{24,16},{9,1},{17,9},{25,17},{10,2},{18,10},{26,18},{... | collective-permute-start | bytes 589832 | tf_op jit(solution)/shard_map/ppermute | solution.py:28
  12.4 0.7 pad_maximum_fusion.10
  13.1 4.1 %collective-permute-start.2 = (f32[3,2,4,4,1,1,128]{6,2,5,3,0,4,1:T(4,128)}, f32[3,2,4,4,1,1,128]{6,2,5,3,0,4,1:T(4,128)}, u32[]{:S(2)}, u32[]{:S(2)}) collective-permute-start(f32[3,2,4,4,1,1,128]{6,2,5,3,0,4,1:T(4,128)} %get-tuple-element.95), channel_id=1, source_target_pairs={{0,2},{2,4},{4,6},{1,3},{3,5},{5,7},{8,10},{10,12},{12,14},{9,11},... | collective-permute-start | bytes 147464 | tf_op jit(solution)/shard_map/ppermute | solution.py:27
  17.2 1.3 %collective-permute-start.3 = (f32[3,2,4,4,1,1,128]{6,2,5,3,0,4,1:T(4,128)}, f32[3,2,4,4,1,1,128]{6,2,5,3,0,4,1:T(4,128)}, u32[]{:S(2)}, u32[]{:S(2)}) collective-permute-start(f32[3,2,4,4,1,1,128]{6,2,5,3,0,4,1:T(4,128)} %get-tuple-element.94), channel_id=1, source_target_pairs={{2,0},{4,2},{6,4},{3,1},{5,3},{7,5},{10,8},{12,10},{14,12},{11,9},... | collective-permute-start | bytes 147464 | tf_op jit(solution)/shard_map/ppermute | solution.py:28
  18.6 0.8 pad_maximum_fusion
  19.5 1.6 %collective-permute-start.4 = (f32[3,2,4,4,1,4,1]{6,2,5,3,0,4,1:T(4,128)}, f32[3,2,4,4,1,4,1]{6,2,5,3,0,4,1:T(4,128)S(1)}, u32[]{:S(2)}, u32[]{:S(2)}) collective-permute-start(f32[3,2,4,4,1,4,1]{6,2,5,3,0,4,1:T(4,128)} %get-tuple-element.93), channel_id=1, source_target_pairs={{0,1},{2,3},{4,5},{6,7},{8,9},{10,11},{12,13},{14,15},{16,17},{18,... | collective-permute-start | bytes 4616 | tf_op jit(solution)/shard_map/ppermute | solution.py:27
  21.1 0.6 copy-done.28
  21.8 0.6 fusion.92
  22.7 0.7 gather_fusion
  23.5 0.8 multiply_reduce_fusion.1
  24.3 0.2 copy.137
  24.8 7.4 %fusion.26 = f32[64,1,3,4]{3,1,2,0:T(1,128)S(1)} fusion(f32[4,64,1,1]{0,2,3,1:T(1,128)S(1)} %copy.138, f32[64,3,4,4]{3,2,1,0:T(4,128)S(1)} %copy.137), kind=kOutput, calls=%fused_computation.47 | convolution fusion | flops 36864 | bytes 16384 | tf_op jit(solution)/shard_map/kabs,bs->kas/dot_general | solution.py:83
  32.2 7.4 %fusion.24 = f32[64,1,3,4]{3,1,2,0:T(1,128)S(1)} fusion(f32[4,64,1,1]{0,2,3,1:T(1,128)S(1)} %copy.152, f32[64,3,4,4]{3,2,1,0:T(4,128)S(1)} %copy.137), kind=kOutput, calls=%fused_computation.45 | convolution fusion | flops 36864 | bytes 16384 | tf_op jit(solution)/shard_map/kabs,bs->kas/dot_general | solution.py:84
  39.6 1.0 copy.166
  40.6 7.6 %fusion.22 = f32[64,1,3,4]{3,1,2,0:T(1,128)S(1)} fusion(f32[4,64,1,1]{0,2,3,1:T(1,128)S(1)} %copy.138, f32[64,3,4,4]{3,2,1,0:T(4,128)S(1)} %copy.166), kind=kOutput, calls=%fused_computation.43 | convolution fusion | flops 36864 | bytes 16384 | tf_op jit(solution)/shard_map/kabs,bs->kas/dot_general | solution.py:85
  48.2 0.4 fusion.37
  49.1 0.7 copy.106
  49.8 8.6 %all-to-all-start = ((f32[12,8,8]{0,2,1:T(8,128)}), f32[12,8,8]{0,2,1:T(8,128)S(1)}, u32[]{:S(2)}, u32[]{:S(2)}) async-start(f32[12,8,8]{0,2,1:T(8,128)} %copy.106), calls=%async_computation | async-start | bytes 65536 | tf_op jit(solution)/shard_map/all_to_all | solution.py:157
  58.6 0.5 copy-done.1
  59.1 0.8 fusion.28
  59.9 0.8 fusion.30
  60.8 0.7 copy-done.2
  61.5 1.6 %fusion.18 = f32[3,4,4,4,1,4,128]{6,1,5,3,2,0,4:T(4,128)S(1)} fusion(f32[4,4,1,1,1,1]{1,0,5,4,3,2:T(4,128)S(1)} %copy-done.1, f32[3,4,4,4,128,4]{4,5,3,2,1,0:T(4,128)S(1)} %fusion.28, f32[3,4,4,4,128,4]{4,5,3,2,1,0:T(4,128)S(1)} %fusion.30, f32[3,4,4,4,4,128]{5,4,3,2,1,0:T(4,128)S(1)} %reshape.1167, f32[4,128]{1,0:T(4,128)S(1)} %bitcast.560, ...), kind=kOutput, calls=%fused_computation.37 | convolution fusion | flops 5111808 | bytes 1968192 | tf_op jit(solution)/shard_map/ia,kabcxyz->kibcxyz/dot_general | solution.py:63
  63.1 0.7 copy-done.26
  63.9 0.6 copy-done.5
  65.0 0.6 fusion.21
  65.5 0.7 fusion.19
  66.5 0.7 copy.113
  67.2 6.0 %all-to-all-start.1 = ((f32[12,8,8]{0,2,1:T(8,128)}), f32[12,8,8]{0,2,1:T(8,128)S(1)}, u32[]{:S(2)}, u32[]{:S(2)}) async-start(f32[12,8,8]{0,2,1:T(8,128)} %copy.113), calls=%async_computation.1 | async-start | bytes 65536 | tf_op jit(solution)/shard_map/all_to_all | solution.py:160
  73.2 0.7 copy.129
  73.9 4.4 %all-to-all-done.1 = f32[12,8,8]{0,2,1:T(8,128)S(1)} async-done(((f32[12,8,8]{0,2,1:T(8,128)}), f32[12,8,8]{0,2,1:T(8,128)S(1)}, u32[]{:S(2)}, u32[]{:S(2)}) %all-to-all-start.1) | async-done | bytes 3104 | tf_op jit(solution)/shard_map/all_to_all | solution.py:160
  78.8 0.6 copy-done.23
  79.5 1.2 %scatter_custom_fusion = f32[192,512]{0,1:T(8,128)S(1)} fusion(s32[64]{0:T(128)} %copy-done.27, f32[64,192]{1,0:T(8,128)S(1)} %copy.116, f32[]{:T(128)} %constant.226.clone.1), kind=kCustom, calls=%fused_computation.55 | custom fusion | flops 12288 | bytes 393728 | tf_op jit(solution)/shard_map/scatter-add | solution.py:163
  81.0 3.7 %collective-permute-start.5 = (f32[3,2,4,4,1,4,1]{6,2,5,3,0,4,1:T(4,128)S(1)}, f32[3,2,4,4,1,4,1]{6,2,5,3,0,4,1:T(4,128)S(1)}, u32[]{:S(2)}, u32[]{:S(2)}) collective-permute-start(f32[3,2,4,4,1,4,1]{6,2,5,3,0,4,1:T(4,128)S(1)} %get-tuple-element.92), channel_id=1, source_target_pairs={{1,0},{3,2},{5,4},{7,6},{9,8},{11,10},{13,12},{15,14},{17,16},{19,... | collective-permute-start | bytes 4616 | tf_op jit(solution)/shard_map/ppermute | solution.py:28
  84.8 1.1 %fusion.64 = f32[3,1,4,4,1,4,128]{6,1,5,3,2,0,4:T(1,128)S(1)} fusion(f32[3,2,4,4,1,4,128]{6,1,5,3,2,0,4:T(2,128)} %collective-permute-done, f32[3,4,4,4,1,4,128]{6,1,5,3,2,0,4:T(4,128)S(1)} %fusion.18, f32[3,4,4,4,1,4,128]{6,1,5,3,2,0,4:T(4,128)S(1)} %copy.91), kind=kLoop, calls=%fused_computation.112 | loop fusion | flops 73728 | bytes 393216 | tf_op jit(solution)/shard_map/add | solution.py:67
  85.9 2.0 %scatter-add.26 = f32[3,4,4,4,1,4,128]{6,1,5,3,2,0,4:T(4,128)S(1)} dynamic-update-slice(f32[3,4,4,4,1,4,128]{6,1,5,3,2,0,4:T(4,128)S(1)} %fusion.18, f32[3,1,4,4,1,4,128]{6,1,5,3,2,0,4:T(1,128)S(1)} %fusion.64, s32[]{:T(128)} %constant.225.clone.1, s32[]{:T(128)} %constant.225.clone.1, s32[]{:T(128)} %constant.225.clone.1, s32[]{:T(128)} %constant.225.clone.1, s32[]{:T(128)} %constant.225.clone.1, ...) | dynamic-update-slice | bytes 196612 | tf_op jit(solution)/shard_map/scatter-add | solution.py:67
  87.9 1.2 %fusion.62 = f32[3,1,4,4,1,4,128]{6,1,5,3,2,0,4:T(1,128)S(1)} fusion(f32[3,2,4,4,1,4,128]{6,1,5,3,2,0,4:T(2,128)} %collective-permute-done.1, f32[3,4,4,4,1,4,128]{6,1,5,3,2,0,4:T(4,128)S(1)} %scatter-add.26, f32[3,4,4,4,1,4,128]{6,1,5,3,2,0,4:T(4,128)S(1)} %copy.91), kind=kLoop, calls=%fused_computation.109 | loop fusion | flops 73728 | bytes 393216 | tf_op jit(solution)/shard_map/add | solution.py:68
  89.1 2.0 %scatter-add.29 = f32[3,4,4,4,1,4,128]{6,1,5,3,2,0,4:T(4,128)S(1)} dynamic-update-slice(f32[3,4,4,4,1,4,128]{6,1,5,3,2,0,4:T(4,128)S(1)} %scatter-add.26, f32[3,1,4,4,1,4,128]{6,1,5,3,2,0,4:T(1,128)S(1)} %fusion.62, s32[]{:T(128)} %constant.225.clone.1, s32[]{:T(128)} %constant.229.clone.1, s32[]{:T(128)} %constant.225.clone.1, s32[]{:T(128)} %constant.225.clone.1, s32[]{:T(128)} %constant.225.clone.1, ...) | dynamic-update-slice | bytes 196612 | tf_op jit(solution)/shard_map/scatter-add | solution.py:68
  91.1 0.8 fusion.60
  91.9 0.8 fusion.55
  92.8 0.2 fusion.49
  93.0 0.3 fusion.44
  93.3 0.3 copy_subtract_fusion
  93.9 0.5 copy-done.19
  94.4 0.5 convolution_select_fusion
  95.0 0.5 convolution_select_fusion.1
  95.6 0.5 convolution_select_fusion.2
  96.3 0.5 convolution_select_fusion.3
  96.9 0.5 convolution_select_fusion.4
  97.6 0.5 convolution_select_fusion.5
  98.2 0.5 convolution_select_fusion.6
  98.8 0.7 fusion.14
  99.5 0.9 reshape.1173
  (117 shorter events, 4.7 us)
Async XLA Ops:
  0.6 1.2 %copy-start.24 = (s32[1,4,128]{2,1,0:T(4,128)S(1)}, s32[1,4,128]{2,1,0:T(4,128)}, u32[]{:S(2)}) copy-start(s32[1,4,128]{2,1,0:T(4,128)} %param.23) | copy-start | bytes 6148
  0.6 1.3 %copy-start = (f32[8,64,64]{2,1,0:T(8,128)S(1)}, f32[8,64,64]{2,1,0:T(8,128)}, u32[]{:S(2)}) copy-start(f32[8,64,64]{2,1,0:T(8,128)} %param.24) | copy-start | bytes 393220
  1.9 0.6 copy-start.18
  1.9 0.6 copy-start.16
  1.9 1.1 %copy-start.14 = (pred[512]{0:T(512)(128)(4,1)}, pred[512]{0:T(512)(128)(4,1)S(1)}, u32[]{:S(2)}) copy-start(pred[512]{0:T(512)(128)(4,1)S(1)} %get-tuple-element.111) | copy-start | bytes 1540
  1.9 1.5 %copy-start.12 = (pred[512]{0:T(512)(128)(4,1)}, pred[512]{0:T(512)(128)(4,1)S(1)}, u32[]{:S(2)}) copy-start(pred[512]{0:T(512)(128)(4,1)S(1)} %get-tuple-element.112) | copy-start | bytes 1540
  1.9 2.0 %copy-start.10 = (pred[512]{0:T(512)(128)(4,1)}, pred[512]{0:T(512)(128)(4,1)S(1)}, u32[]{:S(2)}) copy-start(pred[512]{0:T(512)(128)(4,1)S(1)} %get-tuple-element.113) | copy-start | bytes 1540
  1.9 2.5 %copy-start.8 = (pred[512]{0:T(512)(128)(4,1)}, pred[512]{0:T(512)(128)(4,1)S(1)}, u32[]{:S(2)}) copy-start(pred[512]{0:T(512)(128)(4,1)S(1)} %get-tuple-element.114) | copy-start | bytes 1540
  1.9 3.0 %copy-start.6 = (pred[512]{0:T(512)(128)(4,1)}, pred[512]{0:T(512)(128)(4,1)S(1)}, u32[]{:S(2)}) copy-start(pred[512]{0:T(512)(128)(4,1)S(1)} %get-tuple-element.115) | copy-start | bytes 1540
  1.9 3.5 %copy-start.20 = (pred[512]{0:T(512)(128)(4,1)}, pred[512]{0:T(512)(128)(4,1)S(1)}, u32[]{:S(2)}) copy-start(pred[512]{0:T(512)(128)(4,1)S(1)} %get-tuple-element.110) | copy-start | bytes 1540
  6.7 74.3 %collective-permute-start = (f32[3,2,4,4,1,4,128]{6,1,5,3,2,0,4:T(2,128)S(1)}, f32[3,2,4,4,1,4,128]{6,1,5,3,2,0,4:T(2,128)}, u32[]{:S(2)}, u32[]{:S(2)}) collective-permute-start(f32[3,2,4,4,1,4,128]{6,1,5,3,2,0,4:T(2,128)S(1)} %pad_maximum_fusion.1), channel_id=1, source_target_pairs={{0,8},{8,16},{16,24},{1,9},{9,17},{17,25},{2,10},{10,18},{18,26},{... | collective-permute-start | bytes 589832 | tf_op jit(solution)/shard_map/ppermute | solution.py:27
  8.7 79.3 %collective-permute-start.1 = (f32[3,2,4,4,1,4,128]{6,1,5,3,2,0,4:T(2,128)S(1)}, f32[3,2,4,4,1,4,128]{6,1,5,3,2,0,4:T(2,128)}, u32[]{:S(2)}, u32[]{:S(2)}) collective-permute-start(f32[3,2,4,4,1,4,128]{6,1,5,3,2,0,4:T(2,128)S(1)} %pad_maximum_fusion.1), channel_id=1, source_target_pairs={{8,0},{16,8},{24,16},{9,1},{17,9},{25,17},{10,2},{18,10},{26,18},{... | collective-permute-start | bytes 589832 | tf_op jit(solution)/shard_map/ppermute | solution.py:28
  13.1 78.0 %collective-permute-start.2 = (f32[3,2,4,4,1,1,128]{6,2,5,3,0,4,1:T(4,128)}, f32[3,2,4,4,1,1,128]{6,2,5,3,0,4,1:T(4,128)}, u32[]{:S(2)}, u32[]{:S(2)}) collective-permute-start(f32[3,2,4,4,1,1,128]{6,2,5,3,0,4,1:T(4,128)} %get-tuple-element.95), channel_id=1, source_target_pairs={{0,2},{2,4},{4,6},{1,3},{3,5},{5,7},{8,10},{10,12},{12,14},{9,11},... | collective-permute-start | bytes 147464 | tf_op jit(solution)/shard_map/ppermute | solution.py:27
  17.2 74.8 %collective-permute-start.3 = (f32[3,2,4,4,1,1,128]{6,2,5,3,0,4,1:T(4,128)}, f32[3,2,4,4,1,1,128]{6,2,5,3,0,4,1:T(4,128)}, u32[]{:S(2)}, u32[]{:S(2)}) collective-permute-start(f32[3,2,4,4,1,1,128]{6,2,5,3,0,4,1:T(4,128)} %get-tuple-element.94), channel_id=1, source_target_pairs={{2,0},{4,2},{6,4},{3,1},{5,3},{7,5},{10,8},{12,10},{14,12},{11,9},... | collective-permute-start | bytes 147464 | tf_op jit(solution)/shard_map/ppermute | solution.py:28
  19.5 1.6 %copy-start.4 = (f32[3,1,1,64]{3,2,1,0:T(1,128)S(1)}, f32[3,1,1,64]{3,2,1,0:T(1,128)}, u32[]{:S(2)}) copy-start(f32[3,1,1,64]{3,2,1,0:T(1,128)} %param.26) | copy-start | bytes 2308
  19.5 73.3 %collective-permute-start.4 = (f32[3,2,4,4,1,4,1]{6,2,5,3,0,4,1:T(4,128)}, f32[3,2,4,4,1,4,1]{6,2,5,3,0,4,1:T(4,128)S(1)}, u32[]{:S(2)}, u32[]{:S(2)}) collective-permute-start(f32[3,2,4,4,1,4,1]{6,2,5,3,0,4,1:T(4,128)} %get-tuple-element.93), channel_id=1, source_target_pairs={{0,1},{2,3},{4,5},{6,7},{8,9},{10,11},{12,13},{14,15},{16,17},{18,... | collective-permute-start | bytes 4616 | tf_op jit(solution)/shard_map/ppermute | solution.py:27
  21.1 0.7 copy-start.28
  21.8 0.9 copy-start.27
  21.8 1.7 %copy-start.22 = (pred[64]{0:T(512)(128)(4,1)}, pred[64]{0:T(512)(128)(4,1)S(1)}, u32[]{:S(2)}) copy-start(pred[64]{0:T(512)(128)(4,1)S(1)} %get-tuple-element.142) | copy-start | bytes 196
  49.8 14.8 %all-to-all-start = ((f32[12,8,8]{0,2,1:T(8,128)}), f32[12,8,8]{0,2,1:T(8,128)S(1)}, u32[]{:S(2)}, u32[]{:S(2)}) async-start(f32[12,8,8]{0,2,1:T(8,128)} %copy.106), calls=%async_computation | async-start | bytes 65536 | tf_op jit(solution)/shard_map/all_to_all | solution.py:157
  58.4 0.7 copy-start.1
  59.9 0.9 copy-start.3
  59.9 1.6 %copy-start.25 = (f32[1,4,128]{2,1,0:T(4,128)S(1)}, f32[1,4,128]{2,1,0:T(4,128)}, u32[]{:S(2)}) copy-start(f32[1,4,128]{2,1,0:T(4,128)} %param.22) | copy-start | bytes 6148
  60.8 0.7 copy-start.2
  63.1 0.7 copy-start.26
  63.8 0.7 copy-start.5
  67.2 11.1 %all-to-all-start.1 = ((f32[12,8,8]{0,2,1:T(8,128)}), f32[12,8,8]{0,2,1:T(8,128)S(1)}, u32[]{:S(2)}, u32[]{:S(2)}) async-start(f32[12,8,8]{0,2,1:T(8,128)} %copy.113), calls=%async_computation.1 | async-start | bytes 65536 | tf_op jit(solution)/shard_map/all_to_all | solution.py:160
  78.8 0.6 copy-start.23
  81.0 12.0 %collective-permute-start.5 = (f32[3,2,4,4,1,4,1]{6,2,5,3,0,4,1:T(4,128)S(1)}, f32[3,2,4,4,1,4,1]{6,2,5,3,0,4,1:T(4,128)S(1)}, u32[]{:S(2)}, u32[]{:S(2)}) collective-permute-start(f32[3,2,4,4,1,4,1]{6,2,5,3,0,4,1:T(4,128)S(1)} %get-tuple-element.92), channel_id=1, source_target_pairs={{1,0},{3,2},{5,4},{7,6},{9,8},{11,10},{13,12},{15,14},{17,16},{19,... | collective-permute-start | bytes 4616 | tf_op jit(solution)/shard_map/ppermute | solution.py:28
  93.8 0.6 copy-start.19
  94.4 0.6 copy-start.17
  95.0 0.6 copy-start.15
  95.6 0.7 copy-start.13
  96.3 0.6 copy-start.11
  96.9 0.7 copy-start.9
  97.6 0.6 copy-start.7
  98.2 0.6 copy-start.21
where the time goes:
time: 101 us; the launch traced here: 100 us
  matrix products  35.2 us (35%)
  starting transfers between devices  30.8 us (30%)
  local copies, waits for them, and re-layouts  18.8 us (19%)
  other arithmetic  9.66 us (10%)
  waiting for transfers between devices  4.44 us (4%)
  between operations  1.51 us (1%)
    ppermute x3, starting transfers between devices, extended(): after = lax.ppermute(initial, axis, down)  8.65 us
    all_to_all x1, starting transfers between devices, shards(): lax.all_to_all(packed, ('dy', 'solid'), split_axis=1, concat_axis=1, tile...  8.6 us
    dot_general x16, matrix products, constrain(): product = jnp.einsum(form, matrix, flat, precision=PRECISE)  8.25 us
    dot_general x1, matrix products, evaluate(): derz = jnp.einsum('kabs,bs->kas', along_zd, value_y, precision=PRECISE)  7.6 us
    ppermute x3, starting transfers between devices, extended(): before = lax.ppermute(last, axis, up)  7.59 us
    dot_general x1, matrix products, evaluate(): dery = jnp.einsum('kabs,bs->kas', along_zp, slope_y, precision=PRECISE)  7.41 us
    dot_general x1, matrix products, evaluate(): plain = jnp.einsum('kabs,bs->kas', along_zp, value_y, precision=PRECISE)  7.4 us
    unnamed x66, local copies, waits for them, and re-layouts  6.07 us
  transfers between devices with their start and end apart: 8, of which 1 were waited for; matrix products, arithmetic and copies ran while one was open for 47% of the time, Pallas kernels for 0%

commit v1 on v0

v1 whole, which is shorter than its diff:
```python
import functools

import jax
import jax.numpy as jnp
from jax import lax
from jax.experimental import pallas as pl
from jax.experimental.pallas import tpu as pltpu
from jax.sharding import PartitionSpec as P

TIME_STEP = 0.05
SPRING_RATE = 2.0
PENALTY = 4.0
NODE_POINTS = (0.0, 1.0 / 3.0, 2.0 / 3.0, 1.0)
F32, BF16 = jnp.float32, jnp.bfloat16
VMEM_LIMIT = 24 * 1024 * 1024


def iota(shape, dim):
    return lax.broadcasted_iota(jnp.int32, shape, dim)


def split(x):
    high = x.astype(BF16)
    low = (x - high.astype(F32)).astype(BF16)
    return high, low


def dot(a, b, dims=((1,), (0,))):
    return lax.dot_general(a, b, (dims, ((), ())), preferred_element_type=F32)


def lagrange(coord):
    values = []
    slopes = []
    for which in range(4):
        others = [NODE_POINTS[j] for j in range(4) if j != which]
        denom = 1.0
        for other in others:
            denom = denom * (NODE_POINTS[which] - other)
        scale = 1.0 / denom
        first = coord - others[0]
        second = coord - others[1]
        third = coord - others[2]
        values.append(first * second * third * scale)
        slopes.append((second * third + first * third + first * second) * scale)
    return values, slopes


def spread_rows(parts, dim, lanes):
    wide = [jnp.broadcast_to(p, (8, lanes)) for p in parts]
    if dim == 0:
        return jnp.concatenate([wide[a] for a in (0, 0, 1, 1, 2, 2, 3, 3)], axis=0)
    row = iota((8, lanes), 0)
    if dim == 1:
        even = jnp.where(row < 4, wide[0], wide[1])
        odd = jnp.where(row < 4, wide[2], wide[3])
        return jnp.concatenate([even, odd] * 4, axis=0)
    c = row & 3
    block = jnp.where(c == 0, wide[0], jnp.where(c == 1, wide[1], jnp.where(c == 2, wide[2], wide[3])))
    return jnp.concatenate([block] * 8, axis=0)


def shapes_of(xi, lanes):
    out = []
    for dim in range(3):
        values, slopes = lagrange(xi[dim])
        out.append((spread_rows(values, dim, lanes), spread_rows(slopes, dim, lanes)))
    return out


def one_hot(slots, cells):
    lanes = slots.shape[1]
    return jnp.where(iota((cells, lanes), 0) == slots, 1.0, 0.0).astype(BF16)


def configured(product, config, nconf):
    rows = product.shape[0] // nconf
    chosen = product[:rows]
    for which in range(1, nconf):
        chosen = jnp.where(config == which, product[which * rows : (which + 1) * rows], chosen)
    return chosen


def constrain(matrix, split_ref, config_rows, add, store, nconf, nodes, comps, blocks, lanes):
    step = 2 if blocks % 2 == 0 else 1
    for k in range(comps):
        for first in range(0, blocks, step):
            col = (k * blocks + first) * lanes
            product = dot(matrix, split_ref[:, col : col + step * lanes])
            for i in range(step):
                piece = product[:, i * lanes : (i + 1) * lanes]
                y = first + i
                store(k, y, add(k, y) + configured(piece, config_rows[y], nconf))


def put_split(ref, col, lanes, nodes, value):
    high, low = split(value)
    ref[0:nodes, col : col + lanes] = high
    ref[nodes : 2 * nodes, col : col + lanes] = low
    ref[2 * nodes : 3 * nodes, col : col + lanes] = high


def before(
    dims, axes,
    v_ref, config_ref, offset_ref, slot_ref, xi_ref, strain_ref, motion_ref,
    con_ref, talk_ref, xa_ref, xb_ref, ya_ref, yb_ref, zb_ref,
    rhs_ref, field_ref,
):
    comps, nodes, cx, cy, cz, nconf, slots, has_zb = dims
    blocks = cx * cy
    me_x, me_y, me_z = (lax.axis_index(a) for a in axes)
    even_x, even_y, even_z = (me_x % 2 == 0, me_y % 2 == 0, me_z % 2 == 0)
    high, low = split(offset_ref[...])
    matrix = jnp.concatenate([high, high, low], axis=1)
    config_rows = [config_ref[y : y + 1, :] for y in range(blocks)]

    def load(k, y):
        return v_ref[pl.ds(k * nodes * blocks + y, nodes, stride=blocks), :]

    for k in range(comps):
        for y in range(blocks):
            put_split(rhs_ref, (k * blocks + y) * cz, cz, nodes, load(k, y))

    def store(k, y, value):
        field_ref[(y * comps + k) * nodes : (y * comps + k + 1) * nodes, :] = value
        part, rest = split(value)
        row = 2 * k * nodes
        con_ref[row : row + nodes, y * cz : (y + 1) * cz] = part
        con_ref[row + nodes : row + 2 * nodes, y * cz : (y + 1) * cz] = rest

    constrain(matrix, rhs_ref, config_rows, load, store, nconf, nodes, comps, blocks, cz)

    face = nodes // 4
    for k in range(comps):
        for y in range(cy):
            low_row = (y * comps + k) * nodes
            up_row = (((cx - 1) * cy + y) * comps + k + 1) * nodes
            lower = field_ref[low_row : low_row + face, :]
            upper = field_ref[up_row - face : up_row, :]
            cells = slice(y * cz, (y + 1) * cz)
            xa_ref[k * face : (k + 1) * face, cells] = jnp.where(even_x, upper, lower)
            xb_ref[k * face : (k + 1) * face, cells] = jnp.where(even_x, lower, upper)
        for a in range(4):
            into = k * face + a * 4
            for x in range(cx):
                first = (x * cy * comps + k) * nodes + a * face
                last = ((x * cy + cy - 1) * comps + k) * nodes + a * face
                lower = field_ref[first : first + 4, :]
                upper = field_ref[last + 12 : last + 16, :]
                ya_ref[into : into + 4, x * cz : (x + 1) * cz] = jnp.where(even_y, upper, lower)
                yb_ref[into : into + 4, x * cz : (x + 1) * cz] = jnp.where(even_y, lower, upper)
    rows = comps * face
    lane = iota((rows, 128), 1)
    pack_a = jnp.zeros((rows, 128), F32)
    pack_b = jnp.zeros((rows, 128), F32)
    for y in range(blocks):
        first = y * comps * nodes
        lower = pltpu.roll(field_ref[pl.ds(first, rows, stride=4), :], y, axis=1)
        upper = pltpu.roll(field_ref[pl.ds(first + 3, rows, stride=4), :], (y + 1) % cz, axis=1)
        pack_a = jnp.where(lane == y, jnp.where(even_z, upper, lower), pack_a)
        if has_zb:
            pack_b = jnp.where(lane == y, jnp.where(even_z, lower, upper), pack_b)
    talk_ref[24 : 24 + rows, 0:128] = pack_a
    if has_zb:
        zb_ref[...] = pack_b
    else:
        zb_ref[...] = jnp.zeros_like(zb_ref)

    lanes = talk_ref.shape[1]
    repeat = lanes // slots
    targets = jnp.concatenate([slot_ref[...]] * repeat, axis=1)
    xi = [jnp.concatenate([xi_ref[j]] * repeat, axis=1) for j in range(3)]
    chosen = dot(con_ref[...], one_hot(targets, blocks * cz))
    (px, dx), (py, dy), (pz, dz) = shapes_of(xi, lanes)
    whole = py * pz
    along = (px * whole, dx * whole, px * dy * pz, px * py * dz)
    for k in range(comps):
        row = 2 * k * nodes
        local = chosen[row : row + nodes] + chosen[row + nodes : row + 2 * nodes]
        talk_ref[k : k + 1, :] = jnp.sum(local * along[0], axis=0, keepdims=True)
        for j in range(3):
            at = 3 + 3 * k + j
            talk_ref[at : at + 1, :] = jnp.sum(local * along[1 + j], axis=0, keepdims=True)
    for i in range(9):
        talk_ref[12 + i : 13 + i, :] = jnp.concatenate([strain_ref[i]] * repeat, axis=1)
    for i in range(3):
        talk_ref[21 + i : 22 + i, :] = jnp.concatenate([motion_ref[i]] * repeat, axis=1)


def solid(vel, grad, strain, motion):
    deform = [strain[3 * j + l] + (1.0 if j == l else 0.0) for j in range(3) for l in range(3)]
    moved = []
    for k in range(3):
        for l in range(3):
            change = sum(grad[3 * k + j] * deform[3 * j + l] for j in range(3))
            moved.append(deform[3 * k + l] + TIME_STEP * change)
    stress = [
        sum(moved[3 * k + l] * moved[3 * m + l] for l in range(3)) - (1.0 if k == m else 0.0)
        for k in range(3) for m in range(3)
    ]
    drag = [SPRING_RATE * (motion[k] - vel[k]) for k in range(3)]
    return moved, stress, drag


def node_tables():
    i, j = iota((64, 64), 0), iota((64, 64), 1)
    digits = [((i >> s) & 3, (j >> s) & 3) for s in (4, 2, 0)]
    same = [p == q for p, q in digits]
    lap = jnp.zeros((64, 64), F32)
    swaps = []
    for d in range(3):
        others = same[(d + 1) % 3] & same[(d + 2) % 3]
        p, q = digits[d]
        line = jnp.where(p == q, 2.0, jnp.where((p - q == 1) | (q - p == 1), -1.0, 0.0))
        lap = lap + jnp.where(others, line, 0.0)
        swaps.append(jnp.where(others & (((p == 0) & (q == 3)) | ((p == 3) & (q == 0))), 1.0, 0.0))
    return jnp.concatenate([lap, swaps[2], swaps[1]], axis=0).astype(BF16)


def after(
    dims, axes, sizes,
    con_ref, viscosity_ref, config_ref, offset_ref, slot_ref, xi_ref, strain_ref, motion_ref,
    talk_ref, parts_ref, xa_ref, xb_ref, ya_ref, yb_ref, za_ref, zb_ref,
    out_ref, deform_ref,
    rhs_ref, total_ref, z_ref,
):
    comps, nodes, cx, cy, cz, nconf, slots, has_zb = dims
    blocks = cx * cy
    face = nodes // 4
    row_x = cy * cz
    index = [lax.axis_index(a) for a in axes]
    even = [i % 2 == 0 for i in index]
    open_b = [jnp.where(e, i > 0, i < n - 1) for e, i, n in zip(even, index, sizes, strict=True)]
    open_b = [jnp.where(o, 1.0, 0.0) for o in open_b]

    def sides(d, a, b):
        b = b * open_b[d]
        return jnp.where(even[d], b, a), jnp.where(even[d], a, b)

    lanes = talk_ref.shape[1]
    repeat = lanes // slots
    targets = jnp.concatenate([slot_ref[...]] * repeat, axis=1)
    xi = [jnp.concatenate([xi_ref[j]] * repeat, axis=1) for j in range(3)]
    own = [talk_ref[i : i + 1, :] for i in range(24)]
    got = [parts_ref[i : i + 1, :] for i in range(24)]
    _, stress, drag = solid(own[0:3], own[3:12], got[12:21], got[21:24])
    moved, _, _ = solid(got[0:3], got[3:12], own[12:21], own[21:24])
    for i in range(9):
        deform_ref[i] = moved[i][:, :slots]
    (px, dx), (py, dy), (pz, dz) = shapes_of(xi, lanes)
    flat_yz, flat_dyz, flat_ydz = py * pz, dy * pz, py * dz
    basis = (px * flat_yz, dx * flat_yz, px * flat_dyz, px * flat_ydz)
    hot = one_hot(targets, blocks * cz)
    lane_half = iota((nodes, lanes), 1) < slots

    table = node_tables()
    table = jnp.concatenate([table, table], axis=1)
    row = iota((nodes, cz), 0)
    a, b, c = (row >> 4) & 3, (row >> 2) & 3, row & 3
    def ends(p):
        return jnp.where((p == 0) | (p == 3), PENALTY, 0.0)
    keep = 1.0 + ends(a) + ends(b) + ends(c)
    lane = iota((nodes, cz), 1)
    z_low, z_up = sides(2, za_ref[24 : 24 + comps * face, 0:128], zb_ref[...])
    z_ref[pl.ds(0, comps * face, stride=4), :] = z_low
    z_ref[pl.ds(3, comps * face, stride=4), :] = z_up

    for k in range(comps):
        force = drag[k] * basis[0]
        for j in range(3):
            force = force - stress[3 * k + j] * basis[1 + j]
        high, low = split(force)
        if repeat == 2:
            pieces = jnp.where(lane_half, high.astype(F32), low.astype(F32)).astype(BF16)
            spread = dot(pieces, hot, ((1,), (1,)))
        else:
            spread = dot(high, hot, ((1,), (1,))) + dot(low, hot, ((1,), (1,)))
        pair = con_ref[2 * k * nodes : 2 * (k + 1) * nodes, :]
        ops = dot(table, pair)
        y_low, y_up = sides(1, ya_ref[k * face : (k + 1) * face, :], yb_ref[k * face : (k + 1) * face, :])
        x_low, x_up = sides(0, xa_ref[k * face : (k + 1) * face, :], xb_ref[k * face : (k + 1) * face, :])
        z_face = z_ref[k * nodes : (k + 1) * nodes, :]
        for y in range(blocks):
            x_at, y_at = y // cy, y % cy
            cells = slice(y * cz, (y + 1) * cz)
            value = pair[:nodes, cells].astype(F32) + pair[nodes:, cells].astype(F32)
            total = keep * value + viscosity_ref[y : y + 1, :] * ops[0:nodes, cells] - spread[:, cells]
            moved_z = ops[nodes : 2 * nodes, cells]
            below = jnp.where(lane == 0, pltpu.roll(z_face, (cz - y) % cz, axis=1), pltpu.roll(moved_z, 1, axis=1))
            above = jnp.where(lane == cz - 1, pltpu.roll(z_face, (cz - 1 - y) % cz, axis=1), pltpu.roll(moved_z, cz - 1, axis=1))
            near = jnp.where(c == 0, below, jnp.where(c == 3, above, 0.0))
            if y_at > 0:
                below = ops[2 * nodes : 3 * nodes, (y - 1) * cz : y * cz]
            else:
                low_face = y_low[:, x_at * cz : (x_at + 1) * cz]
                below = jnp.concatenate([low_face[4 * (i // 4) : 4 * (i // 4) + 4] for i in range(16)], axis=0)
            if y_at < cy - 1:
                above = ops[2 * nodes : 3 * nodes, (y + 1) * cz : (y + 2) * cz]
            else:
                up_face = y_up[:, x_at * cz : (x_at + 1) * cz]
                above = jnp.concatenate([up_face[4 * (i // 4) : 4 * (i // 4) + 4] for i in range(16)], axis=0)
            near = near + jnp.where(b == 0, below, jnp.where(b == 3, above, 0.0))
            total = total - PENALTY * near
            plane = slice(y_at * cz, (y_at + 1) * cz)
            if x_at > 0:
                other = slice((y - cy) * cz, (y - cy + 1) * cz)
                below = pair[nodes - face : nodes, other].astype(F32) + pair[2 * nodes - face :, other].astype(F32)
            else:
                below = x_low[:, plane]
            if x_at < cx - 1:
                other = slice((y + cy) * cz, (y + cy + 1) * cz)
                above = pair[:face, other].astype(F32) + pair[nodes : nodes + face, other].astype(F32)
            else:
                above = x_up[:, plane]
            total = jnp.concatenate(
                [total[:face] - PENALTY * below, total[face : nodes - face], total[nodes - face :] - PENALTY * above],
                axis=0,
            )
            total_ref[k * nodes : (k + 1) * nodes, cells] = total
            put_split(rhs_ref, (k * blocks + y) * cz, cz, nodes, total)

    turned = jnp.concatenate([offset_ref[w * nodes : (w + 1) * nodes, :].T for w in range(nconf)], axis=0)
    high, low = split(turned)
    matrix = jnp.concatenate([high, high, low], axis=1)
    config_rows = [config_ref[y : y + 1, :] for y in range(blocks)]

    def add(k, y):
        return total_ref[k * nodes : (k + 1) * nodes, y * cz : (y + 1) * cz]

    def store(k, y, value):
        out_ref[pl.ds(k * nodes * blocks + y, nodes, stride=blocks), :] = value

    constrain(matrix, rhs_ref, config_rows, add, store, nconf, nodes, comps, blocks, cz)


def swap(x, axis, stage):
    n = lax.axis_size(axis)
    pairs = [(i, i + 1) for i in range(stage, n - 1, 2)]
    if not pairs:
        return jnp.zeros_like(x)
    return lax.ppermute(x, axis, pairs + [(j, i) for i, j in pairs])


def shards(
    mesh_sizes,
    velocity,
    viscosity,
    cell_config,
    constraint_offsets,
    slot_cells,
    point_coords,
    strain_offsets,
    solid_velocity,
):
    axes = ("dx", "dy", "solid")
    comps, cx, cy, cz = velocity.shape[0], *velocity.shape[4:]
    nodes = velocity.shape[1] * velocity.shape[2] * velocity.shape[3]
    blocks = cx * cy
    nconf = constraint_offsets.shape[0]
    slots = slot_cells.shape[-1]
    n_dx, n_dy, n_solid = mesh_sizes
    has_zb = n_solid > 2
    dims = (comps, nodes, cx, cy, cz, nconf, slots, has_zb)
    face_rows = comps * nodes // 4
    lanes = max(slots, 128)

    v = velocity.reshape(comps * nodes * blocks, cz)
    visc = viscosity.reshape(blocks, cz)
    config = cell_config.reshape(blocks, cz)
    offsets = constraint_offsets.reshape(nconf * nodes, nodes)
    targets = slot_cells.reshape(1, slots)
    xi = point_coords.reshape(3, 1, slots)
    strain = strain_offsets.reshape(9, 1, slots)
    motion = solid_velocity.reshape(3, 1, slots)

    vmem = pl.BlockSpec(memory_space=pltpu.VMEM)
    params = pltpu.CompilerParams(vmem_limit_bytes=VMEM_LIMIT)
    face_z = jax.ShapeDtypeStruct((face_rows, 128), F32)
    face_y = jax.ShapeDtypeStruct((face_rows, cx * cz), F32)
    face_x = jax.ShapeDtypeStruct((face_rows, cy * cz), F32)
    con, talk, xa, xb, ya, yb, zb = pl.pallas_call(
        functools.partial(before, dims, axes),
        out_shape=(
            jax.ShapeDtypeStruct((2 * comps * nodes, blocks * cz), BF16),
            jax.ShapeDtypeStruct((24 + face_rows, lanes), F32),
            face_x, face_x, face_y, face_y, face_z,
        ),
        in_specs=[vmem] * 7,
        out_specs=(vmem,) * 7,
        scratch_shapes=[
            pltpu.VMEM((3 * nodes, comps * blocks * cz), BF16),
            pltpu.VMEM((blocks * comps * nodes, cz), F32),
        ],
        compiler_params=params,
        name="before",
    )(v, config, offsets, targets, xi, strain, motion)

    if (n_dy, n_solid, slots) == (4, 2, 64):
        got_s = swap(talk, "solid", 0)
        got_xa = swap(xa, "dx", 0)
        pair = jnp.where(iota((24, 128), 1) < 64, talk[:24], got_s[:24])
        send_a = jnp.concatenate([ya, pair], axis=0)
        got_a = swap(send_a, "dy", 0)
        got_xb = swap(xb, "dx", 1)
        send_b = jnp.concatenate([yb, pair, got_a[face_rows:]], axis=0)
        got_b = lax.ppermute(send_b, "dy", [(i, 3 - i) for i in range(4)])
        four = [pair, got_a[face_rows:], got_b[face_rows : face_rows + 24], got_b[face_rows + 24 :]]
        me_y, me_s = lax.axis_index("dy"), lax.axis_index("solid")
        me = me_y * 2 + me_s
        parts = jnp.zeros((24, 8, 8), F32)
        for flip, block in zip((0, 1, 3, 2), four, strict=True):
            for half in range(2):
                source = (me_y ^ flip) * 2 + (me_s ^ half)
                piece = lax.dynamic_slice(block, (0, half * 64 + me * 8), (24, 8))
                parts = lax.dynamic_update_slice(parts, piece[:, None, :], (0, source, 0))
        parts = parts.reshape(24, 64)
        parts = jnp.concatenate([parts, parts], axis=1)
        got_ya, got_yb = got_a[:face_rows], got_b[:face_rows]
        got_za, got_zb = got_s, zb
    else:
        got_xa, got_xb = swap(xa, "dx", 0), swap(xb, "dx", 1)
        got_ya, got_yb = swap(ya, "dy", 0), swap(yb, "dy", 1)
        got_za, got_zb = swap(talk, "solid", 0), swap(zb, "solid", 1)
        parts = lax.all_to_all(talk[:24, :slots], ("dy", "solid"), split_axis=1, concat_axis=1, tiled=True)
        parts = jnp.concatenate([parts] * (lanes // slots), axis=1)

    out, deform = pl.pallas_call(
        functools.partial(after, dims, axes, mesh_sizes),
        out_shape=(
            jax.ShapeDtypeStruct(v.shape, F32),
            jax.ShapeDtypeStruct((9, 1, slots), F32),
        ),
        in_specs=[vmem] * 16,
        out_specs=(vmem,) * 2,
        scratch_shapes=[
            pltpu.VMEM((3 * nodes, comps * blocks * cz), BF16),
            pltpu.VMEM((comps * nodes, blocks * cz), F32),
            pltpu.VMEM((comps * nodes, 128), F32),
        ],
        compiler_params=params,
        name="after",
    )(con, visc, config, offsets, targets, xi, strain, motion,
      talk, parts, got_xa, got_xb, got_ya, got_yb, got_za, got_zb)
    return out.reshape(velocity.shape), deform.reshape(strain_offsets.shape)


def solution(mesh):
    sizes = tuple(mesh.shape[a] for a in ("dx", "dy", "solid"))
    return jax.shard_map(
        functools.partial(shards, sizes),
        mesh=mesh,
        in_specs=(
            P(None, None, None, None, "dx", "dy", "solid"),
            P("dx", "dy", "solid"),
            P("dx", "dy", "solid"),
            P(),
            P("dx", ("dy", "solid"), None),
            P(None, "dx", ("dy", "solid"), None),
            P(None, None, "dx", ("dy", "solid"), None),
            P(None, "dx", ("dy", "solid"), None),
        ),
        out_specs=(
            P(None, None, None, None, "dx", "dy", "solid"),
            P(None, None, "dx", ("dy", "solid"), None),
        ),
        check_vma=False,
    )
```

time: 101 us -> 23.6 us (0.23)
  the two profiles are of different devices: /device:TPU:6 before, /device:TPU:0 now
where the time goes in v1:
time: 23.6 us; the launch traced here: 23.3 us
  starting transfers between devices  10 us (42%)
  waiting for transfers between devices  5.26 us (22%)
  local copies, waits for them, and re-layouts  4.18 us (18%)
  Pallas kernels  2.94 us (12%)
  between operations  0.8 us (3%)
    ppermute x4, starting transfers between devices, swap(): return lax.ppermute(x, axis, pairs + [(j, i) for i, j in pairs])  5.78 us
    ppermute x1, starting transfers between devices, shards(): got_b = lax.ppermute(send_b, 'dy', [(i, 3 - i) for i in range(4)])  4.25 us
    unnamed x18, local copies, waits for them, and re-layouts  3.32 us
    ppermute x4, waiting for transfers between devices, swap(): return lax.ppermute(x, axis, pairs + [(j, i) for i, j in pairs])  3.14 us
    ppermute x1, waiting for transfers between devices, shards(): got_b = lax.ppermute(send_b, 'dy', [(i, 3 - i) for i in range(4)])  2.12 us
    pallas_call x1, Pallas kernels, shards(): pl.pallas_call(functools.partial(after, dims, axes, mesh_sizes), out_shap...  2 us
    pallas_call x1, Pallas kernels, shards(): pl.pallas_call(functools.partial(before, dims, axes), out_shape=(jax.Shap...  0.94 us
    dynamic_slice x11, local copies, waits for them, and re-layouts, shards(): piece = lax.dynamic_slice(block, (0, half * 64 + me * 8), (24, 8))  0.77 us
  transfers between devices with their start and end apart: 5, of which 3 were waited for; matrix products, arithmetic and copies ran while one was open for 4% of the time, Pallas kernels for 0%

profile of v1, /device:TPU:0, one launch (start us, length us, event | category | flops | bytes accessed | tf_op | source)
XLA Modules:
  0.0 23.3 jit_solution(17067973344367360809)
XLA Ops:
  0.6 0.0 copy-start.6
  0.6 0.0 copy-start.3
  0.7 0.0 copy-start.8
  0.7 0.0 copy-start.4
  0.7 0.0 copy-start.5
  0.7 0.6 %copy-done.6 = f32[3,1,1,64]{3,2,1,0:T(1,128)S(1)} copy-done((f32[3,1,1,64]{3,2,1,0:T(1,128)S(1)}, f32[3,1,1,64]{3,2,1,0:T(1,128)}, u32[]{:S(2)}) %copy-start.6) | copy-done | bytes 792
  1.3 0.0 copy-done.3
  1.3 0.0 copy-done.8
  1.3 0.0 copy-done.4
  1.4 0.0 copy-done.5
  1.4 0.0 copy-start
  1.4 0.9 %copy-done = f32[8,64,64]{2,1,0:T(8,128)S(1)} copy-done((f32[8,64,64]{2,1,0:T(8,128)S(1)}, f32[8,64,64]{2,1,0:T(8,128)}, u32[]{:S(2)}) %copy-start) | copy-done | bytes 131096
  2.3 0.0 copy-start.2
  2.3 1.0 %copy-done.2 = f32[3,4,4,4,1,4,128]{6,5,4,3,2,1,0:T(4,128)S(1)} copy-done((f32[3,4,4,4,1,4,128]{6,5,4,3,2,1,0:T(4,128)S(1)}, f32[3,4,4,4,1,4,128]{6,5,4,3,2,1,0:T(4,128)}, u32[]{:S(2)}) %copy-start.2) | copy-done | bytes 393240
  3.3 0.9 %before.1 = (bf16[384,512]{1,0:T(8,128)(2,1)S(1)}, f32[72,128]{1,0:T(8,128)S(1)}, f32[48,512]{1,0:T(8,128)S(1)}, f32[48,512]{1,0:T(8,128)S(1)}, f32[48,128]{1,0:...) custom-call(f32[768,128]{1,0:T(8,128)S(1)} %bitcast.33, s32[4,128]{1,0:T(4,128)S(1)} %bitcast.36, ...), custom_call_target="tpu_custom_call" | custom-call | tf_op jit(solution)/shard_map/before/pallas_call | solution.py:381
  4.3 3.0 %collective-permute-start = (f32[72,128]{1,0:T(8,128)S(1)}, f32[72,128]{1,0:T(8,128)S(1)}, u32[]{:S(2)}, u32[]{:S(2)}) collective-permute-start(f32[72,128]{1,0:T(8,128)S(1)} %get-tuple-element.12.talk_ref), channel_id=1, source_target_pairs={{0,1},{1,0},{2,3},{3,2},{4,5},{5,4},{6,7},{7,6},{8,9},{9,8},{10,11... | collective-permute-start | bytes 110600 | tf_op jit(solution)/shard_map/ppermute | solution.py:341
  7.3 0.0 collective-permute-start.3
  7.3 0.7 %collective-permute-start.4 = (f32[48,512]{1,0:T(8,128)S(1)}, f32[48,512]{1,0:T(8,128)S(1)}, u32[]{:S(2)}, u32[]{:S(2)}) collective-permute-start(f32[48,512]{1,0:T(8,128)S(1)} %get-tuple-element.16), channel_id=1, source_target_pairs={{8,16},{16,8},{9,17},{17,9},{10,18},{18,10},{11,19},{19,11},{12,20... | collective-permute-start | bytes 294920 | tf_op jit(solution)/shard_map/ppermute | solution.py:341
  8.0 1.2 %collective-permute-done.za_ref = f32[72,128]{1,0:T(8,128)S(1)} collective-permute-done((f32[72,128]{1,0:T(8,128)S(1)}, f32[72,128]{1,0:T(8,128)S(1)}, u32[]{:S(2)}, u32[]{:S(2)}) %collective-permute-start) | collective-permute-done | bytes 36896 | tf_op jit(solution)/shard_map/ppermute | solution.py:341
  9.3 0.1 constant_dynamic-slice_fusion.6
  9.3 0.1 copy.17
  9.4 0.1 copy.16
  9.5 2.1 %collective-permute-start.1 = (f32[72,128]{1,0:T(8,128)S(1)}, f32[72,128]{1,0:T(8,128)S(1)}, u32[]{:S(2)}, u32[]{:S(2)}) collective-permute-start(f32[72,128]{1,0:T(8,128)S(1)} %pad_maximum_fusion.1), channel_id=1, source_target_pairs={{0,2},{4,6},{2,0},{6,4},{1,3},{5,7},{3,1},{7,5},{8,10},{12,14},{10... | collective-permute-start | bytes 110600 | tf_op jit(solution)/shard_map/ppermute | solution.py:341
  11.6 1.9 %collective-permute-done.1 = f32[72,128]{1,0:T(8,128)S(1)} collective-permute-done((f32[72,128]{1,0:T(8,128)S(1)}, f32[72,128]{1,0:T(8,128)S(1)}, u32[]{:S(2)}, u32[]{:S(2)}) %collective-permute-start.1) | collective-permute-done | bytes 36896 | tf_op jit(solution)/shard_map/ppermute | solution.py:341
  13.5 0.1 constant_dynamic-slice_fusion.4
  13.6 0.0 copy-start.1
  13.6 0.1 copy.19
  13.6 0.1 copy.18
  13.7 4.2 %collective-permute-start.2 = (f32[96,128]{1,0:T(8,128)S(1)}, f32[96,128]{1,0:T(8,128)S(1)}, u32[]{:S(2)}, u32[]{:S(2)}) collective-permute-start(f32[96,128]{1,0:T(8,128)S(1)} %pad_maximum_fusion), channel_id=1, source_target_pairs={{0,6},{2,4},{4,2},{6,0},{1,7},{3,5},{5,3},{7,1},{8,14},{10,12},{12... | collective-permute-start | bytes 147464 | tf_op jit(solution)/shard_map/ppermute | solution.py:406
  18.0 2.1 %collective-permute-done.2 = f32[96,128]{1,0:T(8,128)S(1)} collective-permute-done((f32[96,128]{1,0:T(8,128)S(1)}, f32[96,128]{1,0:T(8,128)S(1)}, u32[]{:S(2)}, u32[]{:S(2)}) %collective-permute-start.2) | collective-permute-done | bytes 49184 | tf_op jit(solution)/shard_map/ppermute | solution.py:406
  20.1 0.1 constant_dynamic-slice_fusion
  20.2 0.1 copy.23
  20.2 0.1 copy.22
  20.3 0.1 copy.20
  20.4 0.1 copy.21
  20.5 0.1 copy.24
  20.5 0.1 pad_maximum_fusion.2.parts_ref
  20.6 0.0 collective-permute-done.3.xa_ref
  20.6 0.0 collective-permute-done.4.xb_ref
  20.6 0.0 copy-start.7
  20.6 0.0 copy-done.1
  20.6 0.7 %copy-done.7 = f32[1,4,128]{2,1,0:T(4,128)S(1)} copy-done((f32[1,4,128]{2,1,0:T(4,128)S(1)}, f32[1,4,128]{2,1,0:T(4,128)}, u32[]{:S(2)}) %copy-start.7) | copy-done | bytes 2072
  21.3 2.0 %after.1 = (f32[768,128]{1,0:T(8,128)}, f32[9,1,64]{2,1,0:T(1,128)}) custom-call(bf16[384,512]{1,0:T(8,128)(2,1)S(1)} %get-tuple-element.11.con_ref, f32[4,128]{1,0:T(4,128)S(1)} %bitcast.42, s32[4,128]{1,0:T(4,128)S(1)} %bitcast.37, f32[512,64]{1,0:T(8,128)S(1)} %bitcast.32, s32[1,64]{1,0:T(1,128)S(1)} %bitcast.44, f32[3,1,64]{2,1,0:T(1,128)S(1)} %bitcast.39, ...), custom_call_target="tpu_custom_call" | custom-call | tf_op jit(solution)/shard_map/after/pallas_call | solution.py:427
  (17 shorter events, 0.0 us)
Async XLA Ops:
  0.6 0.7 %copy-start.6 = (f32[3,1,1,64]{3,2,1,0:T(1,128)S(1)}, f32[3,1,1,64]{3,2,1,0:T(1,128)}, u32[]{:S(2)}) copy-start(f32[3,1,1,64]{3,2,1,0:T(1,128)} %param.15) | copy-start | bytes 2308
  0.6 0.7 %copy-start.3 = (f32[3,3,1,1,64]{4,3,2,1,0:T(1,128)S(1)}, f32[3,3,1,1,64]{4,3,2,1,0:T(1,128)}, u32[]{:S(2)}) copy-start(f32[3,3,1,1,64]{4,3,2,1,0:T(1,128)} %param.14) | copy-start | bytes 6916
  0.7 0.7 %copy-start.8 = (s32[1,1,64]{2,1,0:T(1,128)S(1)}, s32[1,1,64]{2,1,0:T(1,128)}, u32[]{:S(2)}) copy-start(s32[1,1,64]{2,1,0:T(1,128)} %param.12) | copy-start | bytes 772
  0.7 0.7 %copy-start.4 = (s32[1,4,128]{2,1,0:T(4,128)S(1)}, s32[1,4,128]{2,1,0:T(4,128)}, u32[]{:S(2)}) copy-start(s32[1,4,128]{2,1,0:T(4,128)} %param.10) | copy-start | bytes 6148
  0.7 0.7 %copy-start.5 = (f32[3,1,1,64]{3,2,1,0:T(1,128)S(1)}, f32[3,1,1,64]{3,2,1,0:T(1,128)}, u32[]{:S(2)}) copy-start(f32[3,1,1,64]{3,2,1,0:T(1,128)} %param.13) | copy-start | bytes 2308
  1.4 0.9 %copy-start = (f32[8,64,64]{2,1,0:T(8,128)S(1)}, f32[8,64,64]{2,1,0:T(8,128)}, u32[]{:S(2)}) copy-start(f32[8,64,64]{2,1,0:T(8,128)} %param.11) | copy-start | bytes 393220
  2.3 1.0 %copy-start.2 = (f32[3,4,4,4,1,4,128]{6,5,4,3,2,1,0:T(4,128)S(1)}, f32[3,4,4,4,1,4,128]{6,5,4,3,2,1,0:T(4,128)}, u32[]{:S(2)}) copy-start(f32[3,4,4,4,1,4,128]{6,5,4,3,2,1,0:T(4,128)} %param.8) | copy-start | bytes 1179652
  4.3 5.0 %collective-permute-start = (f32[72,128]{1,0:T(8,128)S(1)}, f32[72,128]{1,0:T(8,128)S(1)}, u32[]{:S(2)}, u32[]{:S(2)}) collective-permute-start(f32[72,128]{1,0:T(8,128)S(1)} %get-tuple-element.12.talk_ref), channel_id=1, source_target_pairs={{0,1},{1,0},{2,3},{3,2},{4,5},{5,4},{6,7},{7,6},{8,9},{9,8},{10,11... | collective-permute-start | bytes 110600 | tf_op jit(solution)/shard_map/ppermute | solution.py:341
  7.3 13.3 %collective-permute-start.3 = (f32[48,512]{1,0:T(8,128)S(1)}, f32[48,512]{1,0:T(8,128)S(1)}, u32[]{:S(2)}, u32[]{:S(2)}) collective-permute-start(f32[48,512]{1,0:T(8,128)S(1)} %get-tuple-element.15), channel_id=1, source_target_pairs={{0,8},{16,24},{8,0},{24,16},{1,9},{17,25},{9,1},{25,17},{2,10},{18... | collective-permute-start | bytes 294920 | tf_op jit(solution)/shard_map/ppermute | solution.py:341
  7.3 13.3 %collective-permute-start.4 = (f32[48,512]{1,0:T(8,128)S(1)}, f32[48,512]{1,0:T(8,128)S(1)}, u32[]{:S(2)}, u32[]{:S(2)}) collective-permute-start(f32[48,512]{1,0:T(8,128)S(1)} %get-tuple-element.16), channel_id=1, source_target_pairs={{8,16},{16,8},{9,17},{17,9},{10,18},{18,10},{11,19},{19,11},{12,20... | collective-permute-start | bytes 294920 | tf_op jit(solution)/shard_map/ppermute | solution.py:341
  9.5 4.0 %collective-permute-start.1 = (f32[72,128]{1,0:T(8,128)S(1)}, f32[72,128]{1,0:T(8,128)S(1)}, u32[]{:S(2)}, u32[]{:S(2)}) collective-permute-start(f32[72,128]{1,0:T(8,128)S(1)} %pad_maximum_fusion.1), channel_id=1, source_target_pairs={{0,2},{4,6},{2,0},{6,4},{1,3},{5,7},{3,1},{7,5},{8,10},{12,14},{10... | collective-permute-start | bytes 110600 | tf_op jit(solution)/shard_map/ppermute | solution.py:341
  13.6 7.1 %copy-start.1 = (f32[8,64,64]{2,1,0:T(8,128)S(1)}, f32[8,64,64]{2,1,0:T(8,128)}, u32[]{:S(2)}) copy-start(f32[8,64,64]{2,1,0:T(8,128)} %param.11) | copy-start | bytes 393220
  13.7 6.4 %collective-permute-start.2 = (f32[96,128]{1,0:T(8,128)S(1)}, f32[96,128]{1,0:T(8,128)S(1)}, u32[]{:S(2)}, u32[]{:S(2)}) collective-permute-start(f32[96,128]{1,0:T(8,128)S(1)} %pad_maximum_fusion), channel_id=1, source_target_pairs={{0,6},{2,4},{4,2},{6,0},{1,7},{3,5},{5,3},{7,1},{8,14},{10,12},{12... | collective-permute-start | bytes 147464 | tf_op jit(solution)/shard_map/ppermute | solution.py:406
  20.6 0.7 %copy-start.7 = (f32[1,4,128]{2,1,0:T(4,128)S(1)}, f32[1,4,128]{2,1,0:T(4,128)}, u32[]{:S(2)}) copy-start(f32[1,4,128]{2,1,0:T(4,128)} %param.9) | copy-start | bytes 6148

commit v2 on v1

v2 whole, which is shorter than its diff:
```python
import functools

import jax
import jax.numpy as jnp
from jax import lax
from jax.experimental import pallas as pl
from jax.experimental.pallas import tpu as pltpu
from jax.sharding import PartitionSpec as P

TIME_STEP = 0.05
SPRING_RATE = 2.0
PENALTY = 4.0
NODE_POINTS = (0.0, 1.0 / 3.0, 2.0 / 3.0, 1.0)
F32, BF16 = jnp.float32, jnp.bfloat16
VMEM_LIMIT = 24 * 1024 * 1024


def iota(shape, dim):
    return lax.broadcasted_iota(jnp.int32, shape, dim)


def split(x):
    high = x.astype(BF16)
    low = (x - high.astype(F32)).astype(BF16)
    return high, low


def dot(a, b, dims=((1,), (0,))):
    return lax.dot_general(a, b, (dims, ((), ())), preferred_element_type=F32)


def lagrange(coord):
    values = []
    slopes = []
    for which in range(4):
        others = [NODE_POINTS[j] for j in range(4) if j != which]
        denom = 1.0
        for other in others:
            denom = denom * (NODE_POINTS[which] - other)
        scale = 1.0 / denom
        first = coord - others[0]
        second = coord - others[1]
        third = coord - others[2]
        values.append(first * second * third * scale)
        slopes.append((second * third + first * third + first * second) * scale)
    return values, slopes


def spread_rows(parts, dim, lanes):
    wide = [jnp.broadcast_to(p, (8, lanes)) for p in parts]
    if dim == 0:
        return jnp.concatenate([wide[a] for a in (0, 0, 1, 1, 2, 2, 3, 3)], axis=0)
    row = iota((8, lanes), 0)
    if dim == 1:
        even = jnp.where(row < 4, wide[0], wide[1])
        odd = jnp.where(row < 4, wide[2], wide[3])
        return jnp.concatenate([even, odd] * 4, axis=0)
    c = row & 3
    block = jnp.where(c == 0, wide[0], jnp.where(c == 1, wide[1], jnp.where(c == 2, wide[2], wide[3])))
    return jnp.concatenate([block] * 8, axis=0)


def shapes_of(xi, lanes):
    out = []
    for dim in range(3):
        values, slopes = lagrange(xi[dim])
        out.append((spread_rows(values, dim, lanes), spread_rows(slopes, dim, lanes)))
    return out


def one_hot(slots, cells):
    lanes = slots.shape[1]
    return jnp.where(iota((cells, lanes), 0) == slots, 1.0, 0.0).astype(BF16)


def configured(product, config, nconf):
    rows = product.shape[0] // nconf
    chosen = product[:rows]
    for which in range(1, nconf):
        chosen = jnp.where(config == which, product[which * rows : (which + 1) * rows], chosen)
    return chosen


def constrain(matrix, split_ref, config_rows, add, store, nconf, nodes, comps, blocks, lanes):
    step = 2 if blocks % 2 == 0 else 1
    for k in range(comps):
        for first in range(0, blocks, step):
            col = (k * blocks + first) * lanes
            product = dot(matrix, split_ref[:, col : col + step * lanes])
            for i in range(step):
                piece = product[:, i * lanes : (i + 1) * lanes]
                y = first + i
                store(k, y, add(k, y) + configured(piece, config_rows[y], nconf))


def put_split(ref, col, lanes, nodes, value):
    high, low = split(value)
    ref[0:nodes, col : col + lanes] = high
    ref[nodes : 2 * nodes, col : col + lanes] = low
    ref[2 * nodes : 3 * nodes, col : col + lanes] = high


def fetch(pairs, sems):
    copies = [pltpu.make_async_copy(src, dst, sems.at[i]) for i, (src, dst) in enumerate(pairs)]
    for copy in copies:
        copy.start()
    return copies


def begin(
    dims,
    v_hbm, config_hbm, offset_hbm, slot_hbm, xi_hbm, strain_hbm, motion_hbm, viscosity_hbm,
    talk_ref, rhs_ref, matrix_ref, hot_ref, basis_ref, config_ref, offset_ref, viscosity_ref,
    v_ref, slot_ref, xi_ref, strain_ref, motion_ref, column_ref, end_ref, sems,
):
    comps, nodes, cx, cy, cz, nconf, slots, lanes = dims
    blocks = cx * cy
    cells = blocks * cz
    face = nodes // 4
    copies = fetch(
        [(slot_hbm, slot_ref), (xi_hbm, xi_ref), (strain_hbm, strain_ref), (motion_hbm, motion_ref),
         (config_hbm, config_ref), (offset_hbm, offset_ref), (v_hbm, v_ref), (viscosity_hbm, viscosity_ref)],
        sems,
    )
    for copy in copies:
        copy.wait()

    lane = iota((1, lanes), 1)
    targets = jnp.concatenate([slot_ref[...], jnp.full((1, lanes - slots), -1, jnp.int32)], axis=1)
    for y in range(blocks):
        targets = jnp.where(lane == lanes - 2 * blocks + y, y * cz, targets)
        targets = jnp.where(lane == lanes - blocks + y, (y + 1) * cz - 1, targets)
    hot = one_hot(targets, cells)
    hot_ref[...] = hot
    high, low = split(offset_ref[...])
    matrix = jnp.concatenate([high, high, low], axis=1)
    matrix_ref[...] = matrix
    for k in range(comps):
        for y in range(blocks):
            value = v_ref[pl.ds(k * nodes * blocks + y, nodes, stride=blocks), :]
            put_split(rhs_ref, (k * blocks + y) * cz, cz, nodes, value)
    config = jnp.concatenate([config_ref[y : y + 1, :] for y in range(blocks)], axis=1)
    config = dot(jnp.broadcast_to(config.astype(F32), (16, cells)).astype(BF16), hot)[0:1, :]

    raw = []
    for k in range(comps):
        both = dot(rhs_ref[0 : 2 * nodes, k * cells : (k + 1) * cells], hot)
        raw.append(both[:nodes] + both[nodes:])
        put_split(column_ref, k * lanes, lanes, nodes, raw[k])
    product = dot(matrix, column_ref[...])

    xi = [jnp.concatenate([xi_ref[j], jnp.zeros((1, lanes - slots), F32)], axis=1) for j in range(3)]
    (px, dx), (py, dy), (pz, dz) = shapes_of(xi, lanes)
    whole = py * pz
    along = (px * whole, dx * whole, px * dy * pz, px * py * dz)
    for j in range(4):
        basis_ref[j * nodes : (j + 1) * nodes, :] = along[j]
    for k in range(comps):
        piece = product[:, k * lanes : (k + 1) * lanes]
        local = raw[k] + configured(piece, config, nconf)
        talk_ref[k : k + 1, :] = jnp.sum(local * along[0], axis=0, keepdims=True)
        for j in range(3):
            at = 3 + 3 * k + j
            talk_ref[at : at + 1, :] = jnp.sum(local * along[1 + j], axis=0, keepdims=True)
        ends = local[:, lanes - 128 :]
        ends = jnp.where(iota((nodes, 128), 1) < 128 - blocks, ends, pltpu.roll(ends, nodes - 3, axis=0))
        end_ref[k * nodes : (k + 1) * nodes, :] = ends
    talk_ref[24 : 24 + comps * face, lanes - 128 :] = end_ref[pl.ds(0, comps * face, stride=4), :]
    for i in range(9):
        talk_ref[12 + i : 13 + i, 0:slots] = strain_ref[i]
    for i in range(3):
        talk_ref[21 + i : 22 + i, 0:slots] = motion_ref[i]
    if 2 * slots == lanes:
        twice = talk_ref[0:24, :]
        talk_ref[0:24, :] = jnp.where(iota((24, lanes), 1) < slots, twice, pltpu.roll(twice, slots, axis=1))


def local(
    dims, axes,
    rhs_ref, matrix_ref, config_ref,
    con_ref, xa_ref, xb_ref, ya_ref, yb_ref,
    field_ref,
):
    comps, nodes, cx, cy, cz, nconf, slots, lanes = dims
    blocks = cx * cy
    me_x, me_y = lax.axis_index(axes[0]), lax.axis_index(axes[1])
    even_x, even_y = me_x % 2 == 0, me_y % 2 == 0
    config_rows = [config_ref[y : y + 1, :] for y in range(blocks)]

    def load(k, y):
        cells = slice((k * blocks + y) * cz, (k * blocks + y + 1) * cz)
        return rhs_ref[0:nodes, cells].astype(F32) + rhs_ref[nodes : 2 * nodes, cells].astype(F32)

    def store(k, y, value):
        field_ref[(y * comps + k) * nodes : (y * comps + k + 1) * nodes, :] = value
        part, rest = split(value)
        row = 2 * k * nodes
        con_ref[row : row + nodes, y * cz : (y + 1) * cz] = part
        con_ref[row + nodes : row + 2 * nodes, y * cz : (y + 1) * cz] = rest

    constrain(matrix_ref[...], rhs_ref, config_rows, load, store, nconf, nodes, comps, blocks, cz)

    face = nodes // 4
    for k in range(comps):
        for y in range(cy):
            low_row = (y * comps + k) * nodes
            up_row = (((cx - 1) * cy + y) * comps + k + 1) * nodes
            lower = field_ref[low_row : low_row + face, :]
            upper = field_ref[up_row - face : up_row, :]
            cells = slice(y * cz, (y + 1) * cz)
            xa_ref[k * face : (k + 1) * face, cells] = jnp.where(even_x, upper, lower)
            xb_ref[k * face : (k + 1) * face, cells] = jnp.where(even_x, lower, upper)
        for a in range(4):
            into = k * face + a * 4
            for x in range(cx):
                first = (x * cy * comps + k) * nodes + a * face
                last = ((x * cy + cy - 1) * comps + k) * nodes + a * face
                lower = field_ref[first : first + 4, :]
                upper = field_ref[last + 12 : last + 16, :]
                ya_ref[into : into + 4, x * cz : (x + 1) * cz] = jnp.where(even_y, upper, lower)
                yb_ref[into : into + 4, x * cz : (x + 1) * cz] = jnp.where(even_y, lower, upper)


def solid(vel, grad, strain, motion):
    deform = [strain[3 * j + l] + (1.0 if j == l else 0.0) for j in range(3) for l in range(3)]
    moved = []
    for k in range(3):
        for l in range(3):
            change = sum(grad[3 * k + j] * deform[3 * j + l] for j in range(3))
            moved.append(deform[3 * k + l] + TIME_STEP * change)
    stress = [
        sum(moved[3 * k + l] * moved[3 * m + l] for l in range(3)) - (1.0 if k == m else 0.0)
        for k in range(3) for m in range(3)
    ]
    drag = [SPRING_RATE * (motion[k] - vel[k]) for k in range(3)]
    return moved, stress, drag


def node_tables():
    i, j = iota((64, 64), 0), iota((64, 64), 1)
    digits = [((i >> s) & 3, (j >> s) & 3) for s in (4, 2, 0)]
    same = [p == q for p, q in digits]
    lap = jnp.zeros((64, 64), F32)
    swaps = []
    for d in range(3):
        others = same[(d + 1) % 3] & same[(d + 2) % 3]
        p, q = digits[d]
        line = jnp.where(p == q, 2.0, jnp.where((p - q == 1) | (q - p == 1), -1.0, 0.0))
        lap = lap + jnp.where(others, line, 0.0)
        swaps.append(jnp.where(others & (((p == 0) & (q == 3)) | ((p == 3) & (q == 0))), 1.0, 0.0))
    return jnp.concatenate([lap, swaps[2], swaps[1]], axis=0).astype(BF16)


def sides(even, open_b, a, b):
    b = jnp.where(open_b, b, 0.0)
    return jnp.where(even, b, a), jnp.where(even, a, b)


def place(axis, n):
    index = lax.axis_index(axis)
    even = index % 2 == 0
    return even, jnp.where(even, index, n - 1 - index) > 0


def middle(
    dims, axes, sizes,
    con_ref, viscosity_ref, offset_ref, xa_ref, xb_ref, za_ref, zb_ref,
    total_ref, matrix_ref,
    z_ref,
):
    comps, nodes, cx, cy, cz, nconf, slots, lanes = dims
    blocks = cx * cy
    face = nodes // 4
    even_x, open_x = place(axes[0], sizes[0])
    even_z, open_z = place(axes[2], sizes[2])

    table = node_tables()
    table = jnp.concatenate([table, table], axis=1)
    row = iota((nodes, cz), 0)
    a, b, c = (row >> 4) & 3, (row >> 2) & 3, row & 3

    def ends(p):
        return jnp.where((p == 0) | (p == 3), PENALTY, 0.0)

    keep = 1.0 + ends(a) + ends(b) + ends(c)
    lane = iota((nodes, cz), 1)
    ends_at = slice(za_ref.shape[1] - 128, za_ref.shape[1])
    z_low, z_up = sides(even_z, open_z, za_ref[24 : 24 + comps * face, ends_at], zb_ref[24 : 24 + comps * face, ends_at])
    z_ref[pl.ds(0, comps * face, stride=4), :] = z_low
    z_ref[pl.ds(3, comps * face, stride=4), :] = z_up

    for k in range(comps):
        pair = con_ref[2 * k * nodes : 2 * (k + 1) * nodes, :]
        ops = dot(table, pair)
        rows = slice(k * face, (k + 1) * face)
        x_low, x_up = sides(even_x, open_x, xa_ref[rows, :], xb_ref[rows, :])
        z_face = z_ref[k * nodes : (k + 1) * nodes, :]
        for y in range(blocks):
            x_at, y_at = y // cy, y % cy
            cells = slice(y * cz, (y + 1) * cz)
            value = pair[:nodes, cells].astype(F32) + pair[nodes:, cells].astype(F32)
            total = keep * value + viscosity_ref[y : y + 1, :] * ops[0:nodes, cells]
            moved_z = ops[nodes : 2 * nodes, cells]
            below = jnp.where(lane == 0, pltpu.roll(z_face, (blocks - y) % cz, axis=1), pltpu.roll(moved_z, 1, axis=1))
            above = jnp.where(
                lane == cz - 1, pltpu.roll(z_face, (2 * blocks - 1 - y) % cz, axis=1), pltpu.roll(moved_z, cz - 1, axis=1)
            )
            near = jnp.where(c == 0, below, jnp.where(c == 3, above, 0.0))
            if y_at > 0:
                near = near + jnp.where(b == 0, ops[2 * nodes : 3 * nodes, (y - 1) * cz : y * cz], 0.0)
            if y_at < cy - 1:
                near = near + jnp.where(b == 3, ops[2 * nodes : 3 * nodes, (y + 1) * cz : (y + 2) * cz], 0.0)
            total = total - PENALTY * near
            plane = slice(y_at * cz, (y_at + 1) * cz)
            if x_at > 0:
                other = slice((y - cy) * cz, (y - cy + 1) * cz)
                below = pair[nodes - face : nodes, other].astype(F32) + pair[2 * nodes - face :, other].astype(F32)
            else:
                below = x_low[:, plane]
            if x_at < cx - 1:
                other = slice((y + cy) * cz, (y + cy + 1) * cz)
                above = pair[:face, other].astype(F32) + pair[nodes : nodes + face, other].astype(F32)
            else:
                above = x_up[:, plane]
            total_ref[k * nodes : (k + 1) * nodes, cells] = jnp.concatenate(
                [total[:face] - PENALTY * below, total[face : nodes - face], total[nodes - face :] - PENALTY * above],
                axis=0,
            )

    turned = jnp.concatenate([offset_ref[w * nodes : (w + 1) * nodes, :].T for w in range(nconf)], axis=0)
    high, low = split(turned)
    matrix_ref[...] = jnp.concatenate([high, high, low], axis=1)


def widen(face, nodes):
    return jnp.concatenate([face[4 * (i // 4) : 4 * (i // 4) + 4] for i in range(nodes // 4)], axis=0)


def gather_parts(refs, axes):
    me_y, me_s = lax.axis_index(axes[1]), lax.axis_index(axes[2])
    me = me_y * 2 + me_s
    lane = iota((24, 128), 1) >> 3
    parts = jnp.zeros((24, 128), F32)
    for flip, ref in enumerate(refs):
        block = ref[0:24, :]
        for half in range(2):
            source = (me_y ^ flip) * 2 + (me_s ^ half)
            shift = (source - me) * 8 + (128 - 64 * half)
            parts = jnp.where(lane == source, pltpu.roll(block, shift & 127, axis=1), parts)
    return parts + pltpu.roll(parts, 64, axis=1)


def after(
    dims, axes, sizes, fast,
    total_ref, matrix_ref, config_ref, hot_ref, basis_ref, talk_ref, ya_ref, yb_ref, *refs,
):
    if fast:
        refs = (refs[0], ya_ref, refs[1], yb_ref, *refs[2:])
        ya_ref, yb_ref = ya_ref.at[24:, :], yb_ref.at[24:, :]
    *part_refs, out_hbm, deform_ref, rhs_ref, total2_ref, out_ref, sems = refs
    comps, nodes, cx, cy, cz, nconf, slots, lanes = dims
    blocks = cx * cy
    face = nodes // 4
    even_y, open_y = place(axes[1], sizes[1])

    parts = gather_parts(part_refs, axes) if fast else part_refs[0][...]
    own = [talk_ref[i : i + 1, :] for i in range(24)]
    got = [parts[i : i + 1, :] for i in range(24)]
    _, stress, drag = solid(own[0:3], own[3:12], got[12:21], got[21:24])
    moved, _, _ = solid(got[0:3], got[3:12], own[12:21], own[21:24])
    for i in range(9):
        deform_ref[i] = moved[i][:, :slots]
    hot = hot_ref[...]
    basis = [basis_ref[j * nodes : (j + 1) * nodes, :] for j in range(4)]
    row = iota((nodes, cz), 0)
    b = (row >> 2) & 3
    live = iota((nodes, lanes), 1) < slots
    highs, lows = [], []
    for k in range(comps):
        force = drag[k] * basis[0]
        for j in range(3):
            force = force - stress[3 * k + j] * basis[1 + j]
        high, low = split(jnp.where(live, force, 0.0))
        highs.append(high)
        lows.append(low)
    spreads = dot(jnp.concatenate(highs + lows, axis=0), hot, ((1,), (1,)))

    for k in range(comps):
        other = (comps + k) * nodes
        spread = spreads[k * nodes : (k + 1) * nodes] + spreads[other : other + nodes]
        rows = slice(k * face, (k + 1) * face)
        y_low, y_up = sides(even_y, open_y, ya_ref[rows, :], yb_ref[rows, :])
        for y in range(blocks):
            x_at, y_at = y // cy, y % cy
            cells = slice(y * cz, (y + 1) * cz)
            total = total_ref[k * nodes : (k + 1) * nodes, cells] - spread[:, cells]
            plane = slice(x_at * cz, (x_at + 1) * cz)
            if y_at == 0:
                total = total - jnp.where(b == 0, PENALTY * widen(y_low[:, plane], nodes), 0.0)
            if y_at == cy - 1:
                total = total - jnp.where(b == 3, PENALTY * widen(y_up[:, plane], nodes), 0.0)
            total2_ref[k * nodes : (k + 1) * nodes, cells] = total
            put_split(rhs_ref, (k * blocks + y) * cz, cz, nodes, total)

    config_rows = [config_ref[y : y + 1, :] for y in range(blocks)]

    def add(k, y):
        return total2_ref[k * nodes : (k + 1) * nodes, y * cz : (y + 1) * cz]

    copies = []

    def store(k, y, value):
        out_ref[pl.ds(k * nodes * blocks + y, nodes, stride=blocks), :] = value
        if y == blocks - 1:
            done = slice(k * nodes * blocks, (k + 1) * nodes * blocks)
            copies.append(pltpu.make_async_copy(out_ref.at[done, :], out_hbm.at[done, :], sems.at[k]))
            copies[-1].start()

    constrain(matrix_ref[...], rhs_ref, config_rows, add, store, nconf, nodes, comps, blocks, cz)
    for copy in copies:
        copy.wait()


def swap(x, axis, stage):
    n = lax.axis_size(axis)
    pairs = [(i, i + 1) for i in range(stage, n - 1, 2)]
    if not pairs:
        return jnp.zeros_like(x)
    return lax.ppermute(x, axis, pairs + [(j, i) for i, j in pairs])


def flip(x, axis, bits):
    return lax.ppermute(x, axis, [(i, i ^ bits) for i in range(lax.axis_size(axis))])


def shards(
    mesh_sizes,
    velocity,
    viscosity,
    cell_config,
    constraint_offsets,
    slot_cells,
    point_coords,
    strain_offsets,
    solid_velocity,
):
    axes = ("dx", "dy", "solid")
    comps, cx, cy, cz = velocity.shape[0], *velocity.shape[4:]
    nodes = velocity.shape[1] * velocity.shape[2] * velocity.shape[3]
    blocks = cx * cy
    nconf = constraint_offsets.shape[0]
    slots = slot_cells.shape[-1]
    n_dx, n_dy, n_solid = mesh_sizes
    face_rows = comps * nodes // 4
    lanes = pl.cdiv(slots + 2 * blocks, 128) * 128
    dims = (comps, nodes, cx, cy, cz, nconf, slots, lanes)

    v = velocity.reshape(comps * nodes * blocks, cz)
    visc = viscosity.reshape(blocks, cz)
    config = cell_config.reshape(blocks, cz)
    offsets = constraint_offsets.reshape(nconf * nodes, nodes)
    targets = slot_cells.reshape(1, slots)
    xi = point_coords.reshape(3, 1, slots)
    strain = strain_offsets.reshape(9, 1, slots)
    motion = solid_velocity.reshape(3, 1, slots)

    vmem = pl.BlockSpec(memory_space=pltpu.VMEM)
    hbm = pl.BlockSpec(memory_space=pltpu.HBM)
    params = pltpu.CompilerParams(vmem_limit_bytes=VMEM_LIMIT)
    cells = blocks * cz
    face_y = jax.ShapeDtypeStruct((face_rows, cx * cz), F32)
    face_x = jax.ShapeDtypeStruct((face_rows, cy * cz), F32)
    def shape(*size, dtype=F32):
        return jax.ShapeDtypeStruct(size, dtype)

    def estimate(columns):
        return pl.CostEstimate(flops=2 * 6 * nconf * nodes * nodes * columns, bytes_accessed=1_000_000, transcendentals=0)

    talk, rhs, matrix, hot, basis, config, offsets, visc = pl.pallas_call(
        functools.partial(begin, dims),
        out_shape=(
            shape(24 + face_rows, lanes),
            shape(3 * nodes, comps * cells, dtype=BF16),
            shape(nconf * nodes, 3 * nodes, dtype=BF16),
            shape(cells, lanes, dtype=BF16),
            shape(4 * nodes, lanes),
            shape(*config.shape, dtype=config.dtype),
            shape(*offsets.shape),
            shape(*visc.shape),
        ),
        in_specs=[hbm] * 8,
        out_specs=(vmem,) * 8,
        scratch_shapes=[
            pltpu.VMEM(v.shape, F32),
            pltpu.VMEM(targets.shape, targets.dtype),
            pltpu.VMEM(xi.shape, F32),
            pltpu.VMEM(strain.shape, F32),
            pltpu.VMEM(motion.shape, F32),
            pltpu.VMEM((3 * nodes, comps * lanes), BF16),
            pltpu.VMEM((comps * nodes, 128), F32),
            pltpu.SemaphoreType.DMA((8,)),
        ],
        compiler_params=params,
        name="begin",
    )(*(pltpu.with_memory_space_constraint(x, pltpu.HBM) for x in (v, config, offsets, targets, xi, strain, motion, visc)))

    con, xa, xb, ya, yb = pl.pallas_call(
        functools.partial(local, dims, axes),
        out_shape=(shape(2 * comps * nodes, cells, dtype=BF16), face_x, face_x, face_y, face_y),
        in_specs=[vmem] * 3,
        out_specs=(vmem,) * 5,
        scratch_shapes=[pltpu.VMEM((blocks * comps * nodes, cz), F32)],
        compiler_params=params,
        cost_estimate=estimate(comps * cells),
        name="local",
    )(rhs, matrix, config)

    fast = (n_dx, n_dy, n_solid, slots) == (4, 4, 2, 64)
    if fast:
        got_s = swap(talk, "solid", 0)
        got_xa = swap(xa, "dx", 0)
        got_xb = flip(xb, "dx", 3)
        pair = jnp.where(iota((24, 128), 1) < 64, talk[:24], got_s[:24])
        got_3 = flip(jnp.concatenate([pair, yb, pair[:8]], axis=0), "dy", 3)
        got_2 = flip(pair, "dy", 2)
        got_1 = flip(jnp.concatenate([pair, ya], axis=0), "dy", 1)
        parts = [pair, got_2]
        got_ya, got_yb = got_1, got_3
        got_za, got_zb = got_s, got_s
    else:
        got_xa, got_xb = swap(xa, "dx", 0), swap(xb, "dx", 1)
        got_ya, got_yb = swap(ya, "dy", 0), swap(yb, "dy", 1)
        got_za, got_zb = swap(talk, "solid", 0), swap(talk, "solid", 1)
        parts = lax.all_to_all(talk[:24, :slots], ("dy", "solid"), split_axis=1, concat_axis=1, tiled=True)
        parts = [jnp.pad(parts, ((0, 0), (0, lanes - slots)))]

    total, matrix = pl.pallas_call(
        functools.partial(middle, dims, axes, mesh_sizes),
        out_shape=(
            jax.ShapeDtypeStruct((comps * nodes, cells), F32),
            jax.ShapeDtypeStruct((nconf * nodes, 3 * nodes), BF16),
        ),
        in_specs=[vmem] * 7,
        out_specs=(vmem,) * 2,
        scratch_shapes=[pltpu.VMEM((comps * nodes, 128), F32)],
        compiler_params=params,
        cost_estimate=estimate(comps * cells),
        name="middle",
    )(con, visc, offsets, got_xa, got_xb, got_za, got_zb)

    out, deform = pl.pallas_call(
        functools.partial(after, dims, axes, mesh_sizes, fast),
        out_shape=(
            jax.ShapeDtypeStruct(v.shape, F32),
            jax.ShapeDtypeStruct((9, 1, slots), F32),
        ),
        in_specs=[vmem] * (8 + len(parts)),
        out_specs=(hbm, vmem),
        scratch_shapes=[
            pltpu.VMEM((3 * nodes, comps * cells), BF16),
            pltpu.VMEM((comps * nodes, cells), F32),
            pltpu.VMEM(v.shape, F32),
            pltpu.SemaphoreType.DMA((comps,)),
        ],
        compiler_params=params,
        name="after",
    )(total, matrix, config, hot, basis, talk, got_ya, got_yb, *parts)
    return out.reshape(velocity.shape), deform.reshape(strain_offsets.shape)


def solution(mesh):
    sizes = tuple(mesh.shape[a] for a in ("dx", "dy", "solid"))
    return jax.shard_map(
        functools.partial(shards, sizes),
        mesh=mesh,
        in_specs=(
            P(None, None, None, None, "dx", "dy", "solid"),
            P("dx", "dy", "solid"),
            P("dx", "dy", "solid"),
            P(),
            P("dx", ("dy", "solid"), None),
            P(None, "dx", ("dy", "solid"), None),
            P(None, None, "dx", ("dy", "solid"), None),
            P(None, "dx", ("dy", "solid"), None),
        ),
        out_specs=(
            P(None, None, None, None, "dx", "dy", "solid"),
            P(None, None, "dx", ("dy", "solid"), None),
        ),
        check_vma=False,
    )
```

time: 23.6 us -> 18.9 us (0.80)
  local copies, waits for them, and re-layouts: 4.18 us -> 0.01 us
  Pallas kernels: 2.94 us -> 5.65 us
  waiting for transfers between devices: 5.26 us -> 3.32 us
  starting transfers between devices: 10 us -> 9.09 us
    unnamed x18 -> x0, local copies, waits for them, and re-layouts: 3.32 us -> none
    ppermute x4 -> x2, waiting for transfers between devices: 3.14 us -> 0.01 us  [swap(): return lax.ppermute(x, axis, pairs + [(j, i) for i, j in pairs])]
    pallas_call x2 -> x4, Pallas kernels: 2.94 us -> 5.65 us  [the longest x1 2.27 us: shards(): pl.pallas_call(functools.partial(after, dims, axes, mesh_sizes, fast), ou...]
    ppermute x4 -> x2, starting transfers between devices: 5.78 us -> 3.1 us  [swap(): return lax.ppermute(x, axis, pairs + [(j, i) for i, j in pairs])]
    ppermute x1 -> x4, starting transfers between devices: 4.25 us -> 5.99 us  [flip(): lax.ppermute(x, axis, [(i, i ^ bits) for i in range(lax.axis_size(axis))])]
    ppermute x1 -> x4, waiting for transfers between devices: 2.12 us -> 3.31 us  [flip(): lax.ppermute(x, axis, [(i, i ^ bits) for i in range(lax.axis_size(axis))])]
    dynamic_slice x11 -> x0, local copies, waits for them, and re-layouts: 0.77 us -> none  [shards(): piece = lax.dynamic_slice(block, (0, half * 64 + me * 8), (24, 8))]
  transfers between devices with their start and end apart: 5 -> 6, of which waited for: 3 -> 2; matrix products, arithmetic and copies ran while one was open for 4% -> 0% of each run, Pallas kernels for 0% -> 8%
where the time goes in v2:
time: 18.9 us; the launch traced here: 18.8 us
  starting transfers between devices  9.09 us (48%)
  Pallas kernels  5.65 us (30%)
  waiting for transfers between devices  3.32 us (18%)
  between operations  0.68 us (4%)
    ppermute x4, starting transfers between devices, flip(): lax.ppermute(x, axis, [(i, i ^ bits) for i in range(lax.axis_size(axis))])  5.99 us
    ppermute x4, waiting for transfers between devices, flip(): lax.ppermute(x, axis, [(i, i ^ bits) for i in range(lax.axis_size(axis))])  3.31 us
    ppermute x2, starting transfers between devices, swap(): return lax.ppermute(x, axis, pairs + [(j, i) for i, j in pairs])  3.1 us
    pallas_call x1, Pallas kernels, shards(): pl.pallas_call(functools.partial(after, dims, axes, mesh_sizes, fast), ou...  2.27 us
    pallas_call x1, Pallas kernels, shards(): pl.pallas_call(functools.partial(begin, dims), out_shape=(shape(24 + face...  1.94 us
    pallas_call x1, Pallas kernels, shards(): pl.pallas_call(functools.partial(middle, dims, axes, mesh_sizes), out_sha...  0.82 us
    pallas_call x1, Pallas kernels, shards(): pl.pallas_call(functools.partial(local, dims, axes), out_shape=(shape(2 *...  0.61 us
  transfers between devices with their start and end apart: 6, of which 2 were waited for; matrix products, arithmetic and copies ran while one was open for 0% of the time, Pallas kernels for 8%

profile of v2, /device:TPU:0, one launch (start us, length us, event | category | flops | bytes accessed | tf_op | source)
XLA Modules:
  0.0 18.8 jit_solution(17849699044449493944)
XLA Ops:
  0.6 1.9 %begin.1 = (f32[72,128]{1,0:T(8,128)S(1)}, bf16[192,1536]{1,0:T(8,128)(2,1)S(1)}, bf16[512,192]{1,0:T(8,128)(2,1)S(1)}, bf16[512,128]{1,0:T(8,128)(2,1)S(1)}, f3...) custom-call(f32[768,128]{1,0:T(8,128)} %bitcast.14, ...), custom_call_target="tpu_custom_call" | custom-call | tf_op jit(solution)/shard_map/begin/pallas_call | solution.py:479
  2.6 3.0 %collective-permute-start.2 = (f32[72,128]{1,0:T(8,128)S(1)}, f32[72,128]{1,0:T(8,128)S(1)}, u32[]{:S(2)}, u32[]{:S(2)}) collective-permute-start(f32[72,128]{1,0:T(8,128)S(1)} %get-tuple-element.27.talk_ref), channel_id=1, source_target_pairs={{0,1},{1,0},{2,3},{3,2},{4,5},{5,4},{6,7},{7,6},{8,9},{9,8},{10,11... | collective-permute-start | bytes 110600 | tf_op jit(solution)/shard_map/ppermute | solution.py:429
  5.6 0.6 %local.1 = (bf16[384,512]{1,0:T(8,128)(2,1)S(1)}, f32[48,512]{1,0:T(8,128)S(1)}, f32[48,512]{1,0:T(8,128)S(1)}, f32[48,128]{1,0:T(8,128)S(1)}, f32[48,128]{1,0:T(8,128)S(1)}) custom-call(bf16[192,1536]{1,0:T(8,128)(2,1)S(1)} %get-tuple-element.19.rhs_ref, bf16[512,192]{1,0:T(8,128)(2,1)S(1)} %get-tuple-element.20.matrix_ref, ...), custom_call_target="tpu_custom_call" | custom-call | flops 603979776 | bytes 1000000 | tf_op jit(solution)/shard_map/local/pallas_call | solution.py:507
  6.2 0.1 collective-permute-start
  6.3 1.6 %collective-permute-start.1 = (f32[48,512]{1,0:T(8,128)S(1)}, f32[48,512]{1,0:T(8,128)S(1)}, u32[]{:S(2)}, u32[]{:S(2)}) collective-permute-start(f32[48,512]{1,0:T(8,128)S(1)} %get-tuple-element.26), channel_id=1, source_target_pairs={{0,24},{8,16},{16,8},{24,0},{1,25},{9,17},{17,9},{25,1},{2,26},{10... | collective-permute-start | bytes 294920 | tf_op jit(solution)/shard_map/ppermute | solution.py:433
  7.9 0.0 collective-permute-done.2.za_ref.zb_ref
  7.9 2.7 %collective-permute-start.5 = (f32[24,128]{1,0:T(8,128)S(1)}, f32[24,128]{1,0:T(8,128)S(1)}, u32[]{:S(2)}, u32[]{:S(2)}) collective-permute-start(f32[24,128]{1,0:T(8,128)S(1)} %slice_select_fusion.refs_0_), channel_id=1, source_target_pairs={{0,4},{2,6},{4,0},{6,2},{1,5},{3,7},{5,1},{7,3},{8,12},{10,14},{12... | collective-permute-start | bytes 36872 | tf_op jit(solution)/shard_map/ppermute | solution.py:433
  10.7 1.4 %collective-permute-start.4 = (f32[80,128]{1,0:T(8,128)S(1)}, f32[80,128]{1,0:T(8,128)S(1)}, u32[]{:S(2)}, u32[]{:S(2)}) collective-permute-start(f32[80,128]{1,0:T(8,128)S(1)} %pad_maximum_fusion), channel_id=1, source_target_pairs={{0,6},{2,4},{4,2},{6,0},{1,7},{3,5},{5,3},{7,1},{8,14},{10,12},{12... | collective-permute-start | bytes 122888 | tf_op jit(solution)/shard_map/ppermute | solution.py:433
  12.0 0.3 %collective-permute-start.3 = (f32[72,128]{1,0:T(8,128)S(1)}, f32[72,128]{1,0:T(8,128)S(1)}, u32[]{:S(2)}, u32[]{:S(2)}) collective-permute-start(f32[72,128]{1,0:T(8,128)S(1)} %pad_maximum_fusion.1), channel_id=1, source_target_pairs={{0,2},{2,0},{4,6},{6,4},{1,3},{3,1},{5,7},{7,5},{8,10},{10,8},{12,... | collective-permute-start | bytes 110600 | tf_op jit(solution)/shard_map/ppermute | solution.py:433
  12.3 0.0 collective-permute-done.xa_ref
  12.3 0.0 collective-permute-done.1.xb_ref
  12.3 0.8 %middle.1 = (f32[192,512]{1,0:T(8,128)S(1)}, bf16[512,192]{1,0:T(8,128)(2,1)S(1)}) custom-call(bf16[384,512]{1,0:T(8,128)(2,1)S(1)} %get-tuple-element.22.con_ref, f32[4,128]{1,0:T(4,128)S(1)} %get-tuple-element.23.viscosity_ref, f32[512,64]{1,0:T(8,128)S(1)} %get-tuple-element.24.offset_ref, f32[48,512]{1,0:T(8,128)S(1)} %collective-permute-done.xa_ref, ...), custom_call_target="tpu_custom_call" | custom-call | flops 603979776 | bytes 1000000 | tf_op jit(solution)/shard_map/middle/pallas_call | solution.py:537
  13.2 0.0 collective-permute-done.5.refs_1_
  13.2 2.8 %collective-permute-done.3.ya_ref = f32[72,128]{1,0:T(8,128)S(1)} collective-permute-done((f32[72,128]{1,0:T(8,128)S(1)}, f32[72,128]{1,0:T(8,128)S(1)}, u32[]{:S(2)}, u32[]{:S(2)}) %collective-permute-start.3) | collective-permute-done | bytes 36896 | tf_op jit(solution)/shard_map/ppermute | solution.py:433
  16.0 0.5 %collective-permute-done.4.yb_ref = f32[80,128]{1,0:T(8,128)S(1)} collective-permute-done((f32[80,128]{1,0:T(8,128)S(1)}, f32[80,128]{1,0:T(8,128)S(1)}, u32[]{:S(2)}, u32[]{:S(2)}) %collective-permute-start.4) | collective-permute-done | bytes 40992 | tf_op jit(solution)/shard_map/ppermute | solution.py:433
  16.5 2.3 %after.1 = (f32[768,128]{1,0:T(8,128)}, f32[9,1,64]{2,1,0:T(1,128)}) custom-call(f32[192,512]{1,0:T(8,128)S(1)} %get-tuple-element.28.total_ref, bf16[512,192]{1,0:T(8,128)(2,1)S(1)} %get-tuple-element.29.matrix_ref, s32[4,128]{1,0:T(4,128)S(1)} %get-tuple-element.21.config_ref, bf16[512,128]{1,0:T(8,128)(2,1)S(1)} %get-tuple-element.30.hot_ref, ...), custom_call_target="tpu_custom_call" | custom-call | tf_op jit(solution)/shard_map/after/pallas_call | solution.py:551
  (5 shorter events, 0.0 us)
Async XLA Ops:
  2.6 5.3 %collective-permute-start.2 = (f32[72,128]{1,0:T(8,128)S(1)}, f32[72,128]{1,0:T(8,128)S(1)}, u32[]{:S(2)}, u32[]{:S(2)}) collective-permute-start(f32[72,128]{1,0:T(8,128)S(1)} %get-tuple-element.27.talk_ref), channel_id=1, source_target_pairs={{0,1},{1,0},{2,3},{3,2},{4,5},{5,4},{6,7},{7,6},{8,9},{9,8},{10,11... | collective-permute-start | bytes 110600 | tf_op jit(solution)/shard_map/ppermute | solution.py:429
  6.2 6.1 %collective-permute-start = (f32[48,512]{1,0:T(8,128)S(1)}, f32[48,512]{1,0:T(8,128)S(1)}, u32[]{:S(2)}, u32[]{:S(2)}) collective-permute-start(f32[48,512]{1,0:T(8,128)S(1)} %get-tuple-element.25), channel_id=1, source_target_pairs={{0,8},{16,24},{8,0},{24,16},{1,9},{17,25},{9,1},{25,17},{2,10},{18... | collective-permute-start | bytes 294920 | tf_op jit(solution)/shard_map/ppermute | solution.py:429
  6.3 6.0 %collective-permute-start.1 = (f32[48,512]{1,0:T(8,128)S(1)}, f32[48,512]{1,0:T(8,128)S(1)}, u32[]{:S(2)}, u32[]{:S(2)}) collective-permute-start(f32[48,512]{1,0:T(8,128)S(1)} %get-tuple-element.26), channel_id=1, source_target_pairs={{0,24},{8,16},{16,8},{24,0},{1,25},{9,17},{17,9},{25,1},{2,26},{10... | collective-permute-start | bytes 294920 | tf_op jit(solution)/shard_map/ppermute | solution.py:433
  7.9 5.2 %collective-permute-start.5 = (f32[24,128]{1,0:T(8,128)S(1)}, f32[24,128]{1,0:T(8,128)S(1)}, u32[]{:S(2)}, u32[]{:S(2)}) collective-permute-start(f32[24,128]{1,0:T(8,128)S(1)} %slice_select_fusion.refs_0_), channel_id=1, source_target_pairs={{0,4},{2,6},{4,0},{6,2},{1,5},{3,7},{5,1},{7,3},{8,12},{10,14},{12... | collective-permute-start | bytes 36872 | tf_op jit(solution)/shard_map/ppermute | solution.py:433
  10.7 5.8 %collective-permute-start.4 = (f32[80,128]{1,0:T(8,128)S(1)}, f32[80,128]{1,0:T(8,128)S(1)}, u32[]{:S(2)}, u32[]{:S(2)}) collective-permute-start(f32[80,128]{1,0:T(8,128)S(1)} %pad_maximum_fusion), channel_id=1, source_target_pairs={{0,6},{2,4},{4,2},{6,0},{1,7},{3,5},{5,3},{7,1},{8,14},{10,12},{12... | collective-permute-start | bytes 122888 | tf_op jit(solution)/shard_map/ppermute | solution.py:433
  12.0 4.0 %collective-permute-start.3 = (f32[72,128]{1,0:T(8,128)S(1)}, f32[72,128]{1,0:T(8,128)S(1)}, u32[]{:S(2)}, u32[]{:S(2)}) collective-permute-start(f32[72,128]{1,0:T(8,128)S(1)} %pad_maximum_fusion.1), channel_id=1, source_target_pairs={{0,2},{2,0},{4,6},{6,4},{1,3},{3,1},{5,7},{7,5},{8,10},{10,8},{12,... | collective-permute-start | bytes 110600 | tf_op jit(solution)/shard_map/ppermute | solution.py:433

commit v3 on v2

--- a/solution.py
+++ b/solution.py
@@ -108,23 +108,25 @@
 
 
 def begin(
-    dims,
+    dims, axes, fast,
     v_hbm, config_hbm, offset_hbm, slot_hbm, xi_hbm, strain_hbm, motion_hbm, viscosity_hbm,
-    talk_ref, rhs_ref, matrix_ref, hot_ref, basis_ref, config_ref, offset_ref, viscosity_ref,
+    talk_ref, own_ref, rhs_ref, matrix_ref, hot_ref, basis_ref, config_ref, offset_ref, viscosity_ref,
     v_ref, slot_ref, xi_ref, strain_ref, motion_ref, column_ref, end_ref, sems,
 ):
     comps, nodes, cx, cy, cz, nconf, slots, lanes = dims
     blocks = cx * cy
     cells = blocks * cz
     face = nodes // 4
-    copies = fetch(
-        [(slot_hbm, slot_ref), (xi_hbm, xi_ref), (strain_hbm, strain_ref), (motion_hbm, motion_ref),
-         (config_hbm, config_ref), (offset_hbm, offset_ref), (v_hbm, v_ref), (viscosity_hbm, viscosity_ref)],
-        sems,
-    )
-    for copy in copies:
-        copy.wait()
-
+    small = [(slot_hbm, slot_ref), (config_hbm, config_ref), (xi_hbm, xi_ref)]
+    late = [(strain_hbm, strain_ref), (motion_hbm, motion_ref), (viscosity_hbm, viscosity_ref)]
+    pairs = small + [(v_hbm, v_ref)] + [(offset_hbm, offset_ref)] + late
+    copies = fetch(pairs, sems)
+
+    def wait(count):
+        for _ in range(count):
+            copies.pop(0).wait()
+
+    wait(3)
     lane = iota((1, lanes), 1)
     targets = jnp.concatenate([slot_ref[...], jnp.full((1, lanes - slots), -1, jnp.int32)], axis=1)
     for y in range(blocks):
@@ -132,18 +134,17 @@
         targets = jnp.where(lane == lanes - blocks + y, (y + 1) * cz - 1, targets)
     hot = one_hot(targets, cells)
     hot_ref[...] = hot
+    wait(len(copies))
+    config = jnp.concatenate([config_ref[y : y + 1, :] for y in range(blocks)], axis=1)
+    config = dot(jnp.broadcast_to(config.astype(F32), (16, cells)).astype(BF16), hot)[0:1, :]
     high, low = split(offset_ref[...])
     matrix = jnp.concatenate([high, high, low], axis=1)
     matrix_ref[...] = matrix
+    raw = []
     for k in range(comps):
         for y in range(blocks):
             value = v_ref[pl.ds(k * nodes * blocks + y, nodes, stride=blocks), :]
             put_split(rhs_ref, (k * blocks + y) * cz, cz, nodes, value)
-    config = jnp.concatenate([config_ref[y : y + 1, :] for y in range(blocks)], axis=1)
-    config = dot(jnp.broadcast_to(config.astype(F32), (16, cells)).astype(BF16), hot)[0:1, :]
-
-    raw = []
-    for k in range(comps):
         both = dot(rhs_ref[0 : 2 * nodes, k * cells : (k + 1) * cells], hot)
         raw.append(both[:nodes] + both[nodes:])
         put_split(column_ref, k * lanes, lanes, nodes, raw[k])
@@ -158,21 +159,28 @@
     for k in range(comps):
         piece = product[:, k * lanes : (k + 1) * lanes]
         local = raw[k] + configured(piece, config, nconf)
-        talk_ref[k : k + 1, :] = jnp.sum(local * along[0], axis=0, keepdims=True)
+        own_ref[k : k + 1, :] = jnp.sum(local * along[0], axis=0, keepdims=True)
         for j in range(3):
             at = 3 + 3 * k + j
-            talk_ref[at : at + 1, :] = jnp.sum(local * along[1 + j], axis=0, keepdims=True)
+            own_ref[at : at + 1, :] = jnp.sum(local * along[1 + j], axis=0, keepdims=True)
         ends = local[:, lanes - 128 :]
         ends = jnp.where(iota((nodes, 128), 1) < 128 - blocks, ends, pltpu.roll(ends, nodes - 3, axis=0))
         end_ref[k * nodes : (k + 1) * nodes, :] = ends
-    talk_ref[24 : 24 + comps * face, lanes - 128 :] = end_ref[pl.ds(0, comps * face, stride=4), :]
     for i in range(9):
-        talk_ref[12 + i : 13 + i, 0:slots] = strain_ref[i]
+        own_ref[12 + i : 13 + i, 0:slots] = strain_ref[i]
     for i in range(3):
-        talk_ref[21 + i : 22 + i, 0:slots] = motion_ref[i]
-    if 2 * slots == lanes:
-        twice = talk_ref[0:24, :]
-        talk_ref[0:24, :] = jnp.where(iota((24, lanes), 1) < slots, twice, pltpu.roll(twice, slots, axis=1))
+        own_ref[21 + i : 22 + i, 0:slots] = motion_ref[i]
+
+    half = comps * face // 2
+    ends = end_ref[pl.ds(0, 2 * half, stride=4), :]
+    lane = iota((half, 128), 1)
+    ends = jnp.where(lane < 128 - 2 * blocks, pltpu.roll(ends[:half], 128 - 2 * blocks, axis=1), ends[half:])
+    last = jnp.where(lane < 128 - 4 * blocks, own_ref[:, lanes - 128 :], ends)
+    if fast:
+        last = pltpu.roll(last, lax.axis_index(axes[2]) * slots, axis=1)
+    elif lanes > 128:
+        talk_ref[:, : lanes - 128] = own_ref[:, : lanes - 128]
+    talk_ref[:, lanes - 128 :] = last
 
 
 def local(
@@ -263,7 +271,7 @@
 
 
 def middle(
-    dims, axes, sizes,
+    dims, axes, sizes, fast,
     con_ref, viscosity_ref, offset_ref, xa_ref, xb_ref, za_ref, zb_ref,
     total_ref, matrix_ref,
     z_ref,
@@ -284,8 +292,15 @@
 
     keep = 1.0 + ends(a) + ends(b) + ends(c)
     lane = iota((nodes, cz), 1)
-    ends_at = slice(za_ref.shape[1] - 128, za_ref.shape[1])
-    z_low, z_up = sides(even_z, open_z, za_ref[24 : 24 + comps * face, ends_at], zb_ref[24 : 24 + comps * face, ends_at])
+
+    def ends_of(ref):
+        last = ref[:, lanes - 128 :]
+        if fast:
+            last = pltpu.roll(last, (lax.axis_index(axes[2]) + 1) % 2 * slots, axis=1)
+        return jnp.concatenate([pltpu.roll(last, 2 * blocks, axis=1), last], axis=0)
+
+    z_a = ends_of(za_ref)
+    z_low, z_up = sides(even_z, open_z, z_a, z_a if fast else ends_of(zb_ref))
     z_ref[pl.ds(0, comps * face, stride=4), :] = z_low
     z_ref[pl.ds(3, comps * face, stride=4), :] = z_up
 
@@ -344,7 +359,7 @@
     for flip, ref in enumerate(refs):
         block = ref[0:24, :]
         for half in range(2):
-            source = (me_y ^ flip) * 2 + (me_s ^ half)
+            source = (me_y ^ flip) * 2 + half
             shift = (source - me) * 8 + (128 - 64 * half)
             parts = jnp.where(lane == source, pltpu.roll(block, shift & 127, axis=1), parts)
     return parts + pltpu.roll(parts, 64, axis=1)
@@ -352,24 +367,26 @@
 
 def after(
     dims, axes, sizes, fast,
-    total_ref, matrix_ref, config_ref, hot_ref, basis_ref, talk_ref, ya_ref, yb_ref, *refs,
+    total_ref, matrix_ref, config_ref, hot_ref, basis_ref, own_ref, ya_ref, yb_ref, *refs,
 ):
     if fast:
         refs = (refs[0], ya_ref, refs[1], yb_ref, *refs[2:])
         ya_ref, yb_ref = ya_ref.at[24:, :], yb_ref.at[24:, :]
-    *part_refs, out_hbm, deform_ref, rhs_ref, total2_ref, out_ref, sems = refs
+    *part_refs, out_hbm, deform_hbm, rhs_ref, total2_ref, out_ref, deform_ref, sems = refs
     comps, nodes, cx, cy, cz, nconf, slots, lanes = dims
     blocks = cx * cy
     face = nodes // 4
     even_y, open_y = place(axes[1], sizes[1])
 
     parts = gather_parts(part_refs, axes) if fast else part_refs[0][...]
-    own = [talk_ref[i : i + 1, :] for i in range(24)]
+    own = [own_ref[i : i + 1, :] for i in range(24)]
     got = [parts[i : i + 1, :] for i in range(24)]
     _, stress, drag = solid(own[0:3], own[3:12], got[12:21], got[21:24])
     moved, _, _ = solid(got[0:3], got[3:12], own[12:21], own[21:24])
     for i in range(9):
         deform_ref[i] = moved[i][:, :slots]
+    copies = [pltpu.make_async_copy(deform_ref, deform_hbm, sems.at[4 * comps])]
+    copies[0].start()
     hot = hot_ref[...]
     basis = [basis_ref[j * nodes : (j + 1) * nodes, :] for j in range(4)]
     row = iota((nodes, cz), 0)
@@ -407,14 +424,14 @@
     def add(k, y):
         return total2_ref[k * nodes : (k + 1) * nodes, y * cz : (y + 1) * cz]
 
-    copies = []
-
     def store(k, y, value):
         out_ref[pl.ds(k * nodes * blocks + y, nodes, stride=blocks), :] = value
         if y == blocks - 1:
-            done = slice(k * nodes * blocks, (k + 1) * nodes * blocks)
-            copies.append(pltpu.make_async_copy(out_ref.at[done, :], out_hbm.at[done, :], sems.at[k]))
-            copies[-1].start()
+            step = nodes * blocks // 4
+            for i in range(4 * k, 4 * k + 4):
+                done = slice(i * step, (i + 1) * step)
+                copies.append(pltpu.make_async_copy(out_ref.at[done, :], out_hbm.at[done, :], sems.at[i]))
+                copies[-1].start()
 
     constrain(matrix_ref[...], rhs_ref, config_rows, add, store, nconf, nodes, comps, blocks, cz)
     for copy in copies:
@@ -452,7 +469,7 @@
     slots = slot_cells.shape[-1]
     n_dx, n_dy, n_solid = mesh_sizes
     face_rows = comps * nodes // 4
-    lanes = pl.cdiv(slots + 2 * blocks, 128) * 128
+    lanes = pl.cdiv(slots + 4 * blocks, 128) * 128
     dims = (comps, nodes, cx, cy, cz, nconf, slots, lanes)
 
     v = velocity.reshape(comps * nodes * blocks, cz)
@@ -476,10 +493,12 @@
     def estimate(columns):
         return pl.CostEstimate(flops=2 * 6 * nconf * nodes * nodes * columns, bytes_accessed=1_000_000, transcendentals=0)
 
-    talk, rhs, matrix, hot, basis, config, offsets, visc = pl.pallas_call(
-        functools.partial(begin, dims),
+    fast = (n_dx, n_dy, n_solid, slots, lanes) == (4, 4, 2, 64, 128)
+    talk, own, rhs, matrix, hot, basis, config, offsets, visc = pl.pallas_call(
+        functools.partial(begin, dims, axes, fast),
         out_shape=(
-            shape(24 + face_rows, lanes),
+            shape(24, lanes),
+            shape(24, lanes),
             shape(3 * nodes, comps * cells, dtype=BF16),
             shape(nconf * nodes, 3 * nodes, dtype=BF16),
             shape(cells, lanes, dtype=BF16),
@@ -489,7 +508,7 @@
             shape(*visc.shape),
         ),
         in_specs=[hbm] * 8,
-        out_specs=(vmem,) * 8,
+        out_specs=(vmem,) * 9,
         scratch_shapes=[
             pltpu.VMEM(v.shape, F32),
             pltpu.VMEM(targets.shape, targets.dtype),
@@ -515,14 +534,14 @@
         name="local",
     )(rhs, matrix, config)
 
-    fast = (n_dx, n_dy, n_solid, slots) == (4, 4, 2, 64)
     if fast:
         got_s = swap(talk, "solid", 0)
         got_xa = swap(xa, "dx", 0)
         got_xb = flip(xb, "dx", 3)
-        pair = jnp.where(iota((24, 128), 1) < 64, talk[:24], got_s[:24])
+        mine = (iota((24, 128), 1) >= 64) == (lax.axis_index("solid") == 1)
+        pair = jnp.where(mine, talk, got_s)
         got_3 = flip(jnp.concatenate([pair, yb, pair[:8]], axis=0), "dy", 3)
-        got_2 = flip(pair, "dy", 2)
+        got_2 = flip(jnp.concatenate([pair, yb[:8]], axis=0), "dy", 2)
         got_1 = flip(jnp.concatenate([pair, ya], axis=0), "dy", 1)
         parts = [pair, got_2]
         got_ya, got_yb = got_1, got_3
@@ -531,11 +550,11 @@
         got_xa, got_xb = swap(xa, "dx", 0), swap(xb, "dx", 1)
         got_ya, got_yb = swap(ya, "dy", 0), swap(yb, "dy", 1)
         got_za, got_zb = swap(talk, "solid", 0), swap(talk, "solid", 1)
-        parts = lax.all_to_all(talk[:24, :slots], ("dy", "solid"), split_axis=1, concat_axis=1, tiled=True)
+        parts = lax.all_to_all(talk[:, :slots], ("dy", "solid"), split_axis=1, concat_axis=1, tiled=True)
         parts = [jnp.pad(parts, ((0, 0), (0, lanes - slots)))]
 
     total, matrix = pl.pallas_call(
-        functools.partial(middle, dims, axes, mesh_sizes),
+        functools.partial(middle, dims, axes, mesh_sizes, fast),
         out_shape=(
             jax.ShapeDtypeStruct((comps * nodes, cells), F32),
             jax.ShapeDtypeStruct((nconf * nodes, 3 * nodes), BF16),
@@ -555,16 +574,17 @@
             jax.ShapeDtypeStruct((9, 1, slots), F32),
         ),
         in_specs=[vmem] * (8 + len(parts)),
-        out_specs=(hbm, vmem),
+        out_specs=(hbm, hbm),
         scratch_shapes=[
             pltpu.VMEM((3 * nodes, comps * cells), BF16),
             pltpu.VMEM((comps * nodes, cells), F32),
             pltpu.VMEM(v.shape, F32),
-            pltpu.SemaphoreType.DMA((comps,)),
+            pltpu.VMEM(strain.shape, F32),
+            pltpu.SemaphoreType.DMA((4 * comps + 1,)),
         ],
         compiler_params=params,
         name="after",
-    )(total, matrix, config, hot, basis, talk, got_ya, got_yb, *parts)
+    )(total, matrix, config, hot, basis, own, got_ya, got_yb, *parts)
     return out.reshape(velocity.shape), deform.reshape(strain_offsets.shape)
 
 

time: 18.9 us -> 18.2 us (0.963)
  Pallas kernels: 5.65 us -> 5.07 us
  waiting for transfers between devices: 3.32 us -> 3.08 us
    pallas_call x1, Pallas kernels: 2.27 us -> 1.76 us  [shards(): pl.pallas_call(functools.partial(after, dims, axes, mesh_sizes, fast), ou...]
    ppermute x4, waiting for transfers between devices: 3.31 us -> 3.07 us  [flip(): lax.ppermute(x, axis, [(i, i ^ bits) for i in range(lax.axis_size(axis))])]
  transfers between devices with their start and end apart: 6 -> 6, of which waited for: 2 -> 1; matrix products, arithmetic and copies ran while one was open for 0% -> 0% of each run, Pallas kernels for 8% -> 8%
where the time goes in v3:
time: 18.2 us; the launch traced here: 18 us
  starting transfers between devices  9.16 us (50%)
  Pallas kernels  5.07 us (28%)
  waiting for transfers between devices  3.08 us (17%)
  between operations  0.69 us (4%)
    ppermute x4, starting transfers between devices, flip(): lax.ppermute(x, axis, [(i, i ^ bits) for i in range(lax.axis_size(axis))])  6.06 us
    ppermute x2, starting transfers between devices, swap(): return lax.ppermute(x, axis, pairs + [(j, i) for i, j in pairs])  3.1 us
    ppermute x4, waiting for transfers between devices, flip(): lax.ppermute(x, axis, [(i, i ^ bits) for i in range(lax.axis_size(axis))])  3.07 us
    pallas_call x1, Pallas kernels, shards(): pl.pallas_call(functools.partial(begin, dims, axes, fast), out_shape=(sha...  1.93 us
    pallas_call x1, Pallas kernels, shards(): pl.pallas_call(functools.partial(after, dims, axes, mesh_sizes, fast), ou...  1.76 us
    pallas_call x1, Pallas kernels, shards(): pl.pallas_call(functools.partial(middle, dims, axes, mesh_sizes, fast), o...  0.77 us
    pallas_call x1, Pallas kernels, shards(): pl.pallas_call(functools.partial(local, dims, axes), out_shape=(shape(2 *...  0.62 us
  transfers between devices with their start and end apart: 6, of which 1 were waited for; matrix products, arithmetic and copies ran while one was open for 0% of the time, Pallas kernels for 8%

profile of v3, /device:TPU:0, one launch (start us, length us, event | category | flops | bytes accessed | tf_op | source)
XLA Modules:
  0.0 18.0 jit_solution(11730123728960504115)
XLA Ops:
  0.6 1.9 %begin.1 = (f32[24,128]{1,0:T(8,128)S(1)}, f32[24,128]{1,0:T(8,128)S(1)}, bf16[192,1536]{1,0:T(8,128)(2,1)S(1)}, bf16[512,192]{1,0:T(8,128)(2,1)S(1)}, bf16[512,...) custom-call(f32[768,128]{1,0:T(8,128)} %bitcast.14, ...), custom_call_target="tpu_custom_call" | custom-call | tf_op jit(solution)/shard_map/begin/pallas_call | solution.py:497
  2.6 3.0 %collective-permute-start.2 = (f32[24,128]{1,0:T(8,128)S(1)}, f32[24,128]{1,0:T(8,128)S(1)}, u32[]{:S(2)}, u32[]{:S(2)}) collective-permute-start(f32[24,128]{1,0:T(8,128)S(1)} %get-tuple-element.28), channel_id=1, source_target_pairs={{0,1},{1,0},{2,3},{3,2},{4,5},{5,4},{6,7},{7,6},{8,9},{9,8},{10,11... | collective-permute-start | bytes 36872 | tf_op jit(solution)/shard_map/ppermute | solution.py:446
  5.6 0.6 %local.1 = (bf16[384,512]{1,0:T(8,128)(2,1)S(1)}, f32[48,512]{1,0:T(8,128)S(1)}, f32[48,512]{1,0:T(8,128)S(1)}, f32[48,128]{1,0:T(8,128)S(1)}, f32[48,128]{1,0:T(8,128)S(1)}) custom-call(bf16[192,1536]{1,0:T(8,128)(2,1)S(1)} %get-tuple-element.20.rhs_ref, bf16[512,192]{1,0:T(8,128)(2,1)S(1)} %get-tuple-element.21.matrix_ref, ...), custom_call_target="tpu_custom_call" | custom-call | flops 603979776 | bytes 1000000 | tf_op jit(solution)/shard_map/local/pallas_call | solution.py:526
  6.2 0.1 collective-permute-start
  6.3 1.6 %collective-permute-start.1 = (f32[48,512]{1,0:T(8,128)S(1)}, f32[48,512]{1,0:T(8,128)S(1)}, u32[]{:S(2)}, u32[]{:S(2)}) collective-permute-start(f32[48,512]{1,0:T(8,128)S(1)} %get-tuple-element.27), channel_id=1, source_target_pairs={{0,24},{8,16},{16,8},{24,0},{1,25},{9,17},{17,9},{25,1},{2,26},{10... | collective-permute-start | bytes 294920 | tf_op jit(solution)/shard_map/ppermute | solution.py:450
  7.9 0.0 collective-permute-done.2.za_ref.zb_ref
  8.0 3.7 %collective-permute-start.4 = (f32[80,128]{1,0:T(8,128)S(1)}, f32[80,128]{1,0:T(8,128)S(1)}, u32[]{:S(2)}, u32[]{:S(2)}) collective-permute-start(f32[80,128]{1,0:T(8,128)S(1)} %pad_maximum_fusion), channel_id=1, source_target_pairs={{0,6},{2,4},{4,2},{6,0},{1,7},{3,5},{5,3},{7,1},{8,14},{10,12},{12... | collective-permute-start | bytes 122888 | tf_op jit(solution)/shard_map/ppermute | solution.py:450
  11.6 0.0 collective-permute-start.5
  11.6 0.8 %collective-permute-start.3 = (f32[72,128]{1,0:T(8,128)S(1)}, f32[72,128]{1,0:T(8,128)S(1)}, u32[]{:S(2)}, u32[]{:S(2)}) collective-permute-start(f32[72,128]{1,0:T(8,128)S(1)} %pad_maximum_fusion.1), channel_id=1, source_target_pairs={{0,2},{2,0},{4,6},{6,4},{1,3},{3,1},{5,7},{7,5},{8,10},{10,8},{12,... | collective-permute-start | bytes 110600 | tf_op jit(solution)/shard_map/ppermute | solution.py:450
  12.4 0.0 collective-permute-done.xa_ref
  12.4 0.0 collective-permute-done.1.xb_ref
  12.4 0.8 %middle.1 = (f32[192,512]{1,0:T(8,128)S(1)}, bf16[512,192]{1,0:T(8,128)(2,1)S(1)}) custom-call(bf16[384,512]{1,0:T(8,128)(2,1)S(1)} %get-tuple-element.23.con_ref, f32[4,128]{1,0:T(4,128)S(1)} %get-tuple-element.24.viscosity_ref, f32[512,64]{1,0:T(8,128)S(1)} %get-tuple-element.25.offset_ref, f32[48,512]{1,0:T(8,128)S(1)} %collective-permute-done.xa_ref, ...), custom_call_target="tpu_custom_call" | custom-call | flops 603979776 | bytes 1000000 | tf_op jit(solution)/shard_map/middle/pallas_call | solution.py:556
  13.2 3.1 %collective-permute-done.5.refs_1_ = f32[32,128]{1,0:T(8,128)S(1)} collective-permute-done((f32[32,128]{1,0:T(8,128)S(1)}, f32[32,128]{1,0:T(8,128)S(1)}, u32[]{:S(2)}, u32[]{:S(2)}) %collective-permute-start.5) | collective-permute-done | bytes 16416 | tf_op jit(solution)/shard_map/ppermute | solution.py:450
  16.3 0.0 collective-permute-done.3.ya_ref
  16.3 0.0 collective-permute-done.4.yb_ref
  16.3 1.8 %after.1 = (f32[768,128]{1,0:T(8,128)}, f32[9,1,64]{2,1,0:T(1,128)}) custom-call(f32[192,512]{1,0:T(8,128)S(1)} %get-tuple-element.29.total_ref, bf16[512,192]{1,0:T(8,128)(2,1)S(1)} %get-tuple-element.30.matrix_ref, s32[4,128]{1,0:T(4,128)S(1)} %get-tuple-element.22.config_ref, bf16[512,128]{1,0:T(8,128)(2,1)S(1)} %get-tuple-element.31.hot_ref, ...), custom_call_target="tpu_custom_call" | custom-call | tf_op jit(solution)/shard_map/after/pallas_call | solution.py:570
  (7 shorter events, 0.0 us)
Async XLA Ops:
  2.6 5.4 %collective-permute-start.2 = (f32[24,128]{1,0:T(8,128)S(1)}, f32[24,128]{1,0:T(8,128)S(1)}, u32[]{:S(2)}, u32[]{:S(2)}) collective-permute-start(f32[24,128]{1,0:T(8,128)S(1)} %get-tuple-element.28), channel_id=1, source_target_pairs={{0,1},{1,0},{2,3},{3,2},{4,5},{5,4},{6,7},{7,6},{8,9},{9,8},{10,11... | collective-permute-start | bytes 36872 | tf_op jit(solution)/shard_map/ppermute | solution.py:446
  6.2 6.2 %collective-permute-start = (f32[48,512]{1,0:T(8,128)S(1)}, f32[48,512]{1,0:T(8,128)S(1)}, u32[]{:S(2)}, u32[]{:S(2)}) collective-permute-start(f32[48,512]{1,0:T(8,128)S(1)} %get-tuple-element.26), channel_id=1, source_target_pairs={{0,8},{16,24},{8,0},{24,16},{1,9},{17,25},{9,1},{25,17},{2,10},{18... | collective-permute-start | bytes 294920 | tf_op jit(solution)/shard_map/ppermute | solution.py:446
  6.3 6.1 %collective-permute-start.1 = (f32[48,512]{1,0:T(8,128)S(1)}, f32[48,512]{1,0:T(8,128)S(1)}, u32[]{:S(2)}, u32[]{:S(2)}) collective-permute-start(f32[48,512]{1,0:T(8,128)S(1)} %get-tuple-element.27), channel_id=1, source_target_pairs={{0,24},{8,16},{16,8},{24,0},{1,25},{9,17},{17,9},{25,1},{2,26},{10... | collective-permute-start | bytes 294920 | tf_op jit(solution)/shard_map/ppermute | solution.py:450
  8.0 8.3 %collective-permute-start.4 = (f32[80,128]{1,0:T(8,128)S(1)}, f32[80,128]{1,0:T(8,128)S(1)}, u32[]{:S(2)}, u32[]{:S(2)}) collective-permute-start(f32[80,128]{1,0:T(8,128)S(1)} %pad_maximum_fusion), channel_id=1, source_target_pairs={{0,6},{2,4},{4,2},{6,0},{1,7},{3,5},{5,3},{7,1},{8,14},{10,12},{12... | collective-permute-start | bytes 122888 | tf_op jit(solution)/shard_map/ppermute | solution.py:450
  11.6 4.6 %collective-permute-start.5 = (f32[32,128]{1,0:T(8,128)S(1)}, f32[32,128]{1,0:T(8,128)S(1)}, u32[]{:S(2)}, u32[]{:S(2)}) collective-permute-start(f32[32,128]{1,0:T(8,128)S(1)} %pad_maximum_fusion.2), channel_id=1, source_target_pairs={{0,4},{2,6},{4,0},{6,2},{1,5},{3,7},{5,1},{7,3},{8,12},{10,14},{12... | collective-permute-start | bytes 49160 | tf_op jit(solution)/shard_map/ppermute | solution.py:450
  11.6 4.6 %collective-permute-start.3 = (f32[72,128]{1,0:T(8,128)S(1)}, f32[72,128]{1,0:T(8,128)S(1)}, u32[]{:S(2)}, u32[]{:S(2)}) collective-permute-start(f32[72,128]{1,0:T(8,128)S(1)} %pad_maximum_fusion.1), channel_id=1, source_target_pairs={{0,2},{2,0},{4,6},{6,4},{1,3},{3,1},{5,7},{7,5},{8,10},{10,8},{12,... | collective-permute-start | bytes 110600 | tf_op jit(solution)/shard_map/ppermute | solution.py:450

commit v4 on v3

--- a/solution.py
+++ b/solution.py
@@ -81,23 +81,19 @@
     return chosen
 
 
-def constrain(matrix, split_ref, config_rows, add, store, nconf, nodes, comps, blocks, lanes):
+def tripled(high, low):
+    return jnp.concatenate([high, low, high], axis=0)
+
+
+def constrain(matrix, columns, config_rows, store, nconf, comps, blocks, lanes):
     step = 2 if blocks % 2 == 0 else 1
     for k in range(comps):
         for first in range(0, blocks, step):
-            col = (k * blocks + first) * lanes
-            product = dot(matrix, split_ref[:, col : col + step * lanes])
+            values, parts = columns(k, range(first, first + step))
+            product = dot(matrix, parts)
             for i in range(step):
                 piece = product[:, i * lanes : (i + 1) * lanes]
-                y = first + i
-                store(k, y, add(k, y) + configured(piece, config_rows[y], nconf))
-
-
-def put_split(ref, col, lanes, nodes, value):
-    high, low = split(value)
-    ref[0:nodes, col : col + lanes] = high
-    ref[nodes : 2 * nodes, col : col + lanes] = low
-    ref[2 * nodes : 3 * nodes, col : col + lanes] = high
+                store(k, first + i, values[i] + configured(piece, config_rows[first + i], nconf))
 
 
 def fetch(pairs, sems):
@@ -107,26 +103,34 @@
     return copies
 
 
+def plain_matrix(offsets):
+    high, low = split(offsets)
+    return jnp.concatenate([high, high, low], axis=1)
+
+
+def turned_matrix(offsets, nconf, nodes):
+    turned = jnp.concatenate([offsets[w * nodes : (w + 1) * nodes, :].T for w in range(nconf)], axis=0)
+    high, low = split(turned)
+    return jnp.concatenate([high, high, low], axis=1)
+
+
 def begin(
     dims, axes, fast,
     v_hbm, config_hbm, offset_hbm, slot_hbm, xi_hbm, strain_hbm, motion_hbm, viscosity_hbm,
-    talk_ref, own_ref, rhs_ref, matrix_ref, hot_ref, basis_ref, config_ref, offset_ref, viscosity_ref,
-    v_ref, slot_ref, xi_ref, strain_ref, motion_ref, column_ref, end_ref, sems,
+    talk_ref, own_ref, split_ref, matrix_ref, hot_ref, weight_ref, config_ref, offset_ref, viscosity_ref,
+    v_ref, slot_ref, xi_ref, strain_ref, motion_ref, sems,
 ):
     comps, nodes, cx, cy, cz, nconf, slots, lanes = dims
     blocks = cx * cy
     cells = blocks * cz
-    face = nodes // 4
-    small = [(slot_hbm, slot_ref), (config_hbm, config_ref), (xi_hbm, xi_ref)]
-    late = [(strain_hbm, strain_ref), (motion_hbm, motion_ref), (viscosity_hbm, viscosity_ref)]
-    pairs = small + [(v_hbm, v_ref)] + [(offset_hbm, offset_ref)] + late
-    copies = fetch(pairs, sems)
-
-    def wait(count):
-        for _ in range(count):
-            copies.pop(0).wait()
-
-    wait(3)
+    copies = fetch(
+        [(v_hbm, v_ref), (offset_hbm, offset_ref), (slot_hbm, slot_ref), (config_hbm, config_ref), (xi_hbm, xi_ref),
+         (strain_hbm, strain_ref), (motion_hbm, motion_ref), (viscosity_hbm, viscosity_ref)],
+        sems,
+    )
+
+    for copy in copies[2:5]:
+        copy.wait()
     lane = iota((1, lanes), 1)
     targets = jnp.concatenate([slot_ref[...], jnp.full((1, lanes - slots), -1, jnp.int32)], axis=1)
     for y in range(blocks):
@@ -134,58 +138,63 @@
         targets = jnp.where(lane == lanes - blocks + y, (y + 1) * cz - 1, targets)
     hot = one_hot(targets, cells)
     hot_ref[...] = hot
-    wait(len(copies))
     config = jnp.concatenate([config_ref[y : y + 1, :] for y in range(blocks)], axis=1)
     config = dot(jnp.broadcast_to(config.astype(F32), (16, cells)).astype(BF16), hot)[0:1, :]
-    high, low = split(offset_ref[...])
-    matrix = jnp.concatenate([high, high, low], axis=1)
-    matrix_ref[...] = matrix
-    raw = []
-    for k in range(comps):
-        for y in range(blocks):
-            value = v_ref[pl.ds(k * nodes * blocks + y, nodes, stride=blocks), :]
-            put_split(rhs_ref, (k * blocks + y) * cz, cz, nodes, value)
-        both = dot(rhs_ref[0 : 2 * nodes, k * cells : (k + 1) * cells], hot)
-        raw.append(both[:nodes] + both[nodes:])
-        put_split(column_ref, k * lanes, lanes, nodes, raw[k])
-    product = dot(matrix, column_ref[...])
 
     xi = [jnp.concatenate([xi_ref[j], jnp.zeros((1, lanes - slots), F32)], axis=1) for j in range(3)]
     (px, dx), (py, dy), (pz, dz) = shapes_of(xi, lanes)
     whole = py * pz
-    along = (px * whole, dx * whole, px * dy * pz, px * py * dz)
+    basis = (px * whole, dx * whole, px * dy * pz, px * py * dz)
+    for copy in copies[:2] + copies[5:]:
+        copy.wait()
+    raw = []
+    for k in range(comps):
+        row = 2 * k * nodes
+        for y in range(blocks):
+            high, low = split(v_ref[pl.ds(k * nodes * blocks + y, nodes, stride=blocks), :])
+            at = slice(y * cz, (y + 1) * cz)
+            split_ref[row : row + nodes, at] = high
+            split_ref[row + nodes : row + 2 * nodes, at] = low
+        both = dot(split_ref[row : row + 2 * nodes, :], hot)
+        raw.append(both[:nodes] + both[nodes:])
+    matrix = turned_matrix(offset_ref[...], nconf, nodes)
+    matrix_ref[...] = matrix
+    product = dot(matrix, jnp.concatenate([tripled(*split(p)) for p in basis], axis=1))
+    weights = []
     for j in range(4):
-        basis_ref[j * nodes : (j + 1) * nodes, :] = along[j]
+        weights.append(basis[j] + configured(product[:, j * lanes : (j + 1) * lanes], config, nconf))
+        weight_ref[j * nodes : (j + 1) * nodes, :] = weights[j]
+
     for k in range(comps):
-        piece = product[:, k * lanes : (k + 1) * lanes]
-        local = raw[k] + configured(piece, config, nconf)
-        own_ref[k : k + 1, :] = jnp.sum(local * along[0], axis=0, keepdims=True)
+        own_ref[k : k + 1, :] = jnp.sum(raw[k] * weights[0], axis=0, keepdims=True)
         for j in range(3):
             at = 3 + 3 * k + j
-            own_ref[at : at + 1, :] = jnp.sum(local * along[1 + j], axis=0, keepdims=True)
-        ends = local[:, lanes - 128 :]
-        ends = jnp.where(iota((nodes, 128), 1) < 128 - blocks, ends, pltpu.roll(ends, nodes - 3, axis=0))
-        end_ref[k * nodes : (k + 1) * nodes, :] = ends
+            own_ref[at : at + 1, :] = jnp.sum(raw[k] * weights[1 + j], axis=0, keepdims=True)
     for i in range(9):
         own_ref[12 + i : 13 + i, 0:slots] = strain_ref[i]
     for i in range(3):
         own_ref[21 + i : 22 + i, 0:slots] = motion_ref[i]
 
-    half = comps * face // 2
-    ends = end_ref[pl.ds(0, 2 * half, stride=4), :]
-    lane = iota((half, 128), 1)
-    ends = jnp.where(lane < 128 - 2 * blocks, pltpu.roll(ends[:half], 128 - 2 * blocks, axis=1), ends[half:])
-    last = jnp.where(lane < 128 - 4 * blocks, own_ref[:, lanes - 128 :], ends)
+    count = comps * nodes // 24
+    wide = 2 * blocks
+    ends = jnp.concatenate([r[:, lanes - 128 :] for r in raw], axis=0)
+    lane = iota((24, 128), 1)
+    last = own_ref[:, lanes - 128 :]
+    for g in range(count):
+        start = 128 - (count - g) * wide
+        group = pltpu.roll(ends[24 * g : 24 * (g + 1)], (start + wide) % 128, axis=1)
+        last = jnp.where(lane >= start, group, last)
+    last = jnp.concatenate([last, jnp.broadcast_to(config[:, lanes - 128 :], (8, 128))], axis=0)
     if fast:
         last = pltpu.roll(last, lax.axis_index(axes[2]) * slots, axis=1)
     elif lanes > 128:
-        talk_ref[:, : lanes - 128] = own_ref[:, : lanes - 128]
+        talk_ref[0:24, : lanes - 128] = own_ref[:, : lanes - 128]
     talk_ref[:, lanes - 128 :] = last
 
 
 def local(
     dims, axes,
-    rhs_ref, matrix_ref, config_ref,
+    split_ref, offset_ref, config_ref,
     con_ref, xa_ref, xb_ref, ya_ref, yb_ref,
     field_ref,
 ):
@@ -195,9 +204,12 @@
     even_x, even_y = me_x % 2 == 0, me_y % 2 == 0
     config_rows = [config_ref[y : y + 1, :] for y in range(blocks)]
 
-    def load(k, y):
-        cells = slice((k * blocks + y) * cz, (k * blocks + y + 1) * cz)
-        return rhs_ref[0:nodes, cells].astype(F32) + rhs_ref[nodes : 2 * nodes, cells].astype(F32)
+    def columns(k, ys):
+        at = slice(ys[0] * cz, (ys[-1] + 1) * cz)
+        high = split_ref[2 * k * nodes : (2 * k + 1) * nodes, at]
+        low = split_ref[(2 * k + 1) * nodes : (2 * k + 2) * nodes, at]
+        value = high.astype(F32) + low.astype(F32)
+        return [value[:, i * cz : (i + 1) * cz] for i in range(len(ys))], tripled(high, low)
 
     def store(k, y, value):
         field_ref[(y * comps + k) * nodes : (y * comps + k + 1) * nodes, :] = value
@@ -206,7 +218,7 @@
         con_ref[row : row + nodes, y * cz : (y + 1) * cz] = part
         con_ref[row + nodes : row + 2 * nodes, y * cz : (y + 1) * cz] = rest
 
-    constrain(matrix_ref[...], rhs_ref, config_rows, load, store, nconf, nodes, comps, blocks, cz)
+    constrain(plain_matrix(offset_ref[...]), columns, config_rows, store, nconf, comps, blocks, cz)
 
     face = nodes // 4
     for k in range(comps):
@@ -272,9 +284,8 @@
 
 def middle(
     dims, axes, sizes, fast,
-    con_ref, viscosity_ref, offset_ref, xa_ref, xb_ref, za_ref, zb_ref,
-    total_ref, matrix_ref,
-    z_ref,
+    za_ref, con_ref, viscosity_ref, offset_ref, matrix_ref, config_ref, xa_ref, xb_ref, zb_ref,
+    total_ref,
 ):
     comps, nodes, cx, cy, cz, nconf, slots, lanes = dims
     blocks = cx * cy
@@ -292,33 +303,47 @@
 
     keep = 1.0 + ends(a) + ends(b) + ends(c)
     lane = iota((nodes, cz), 1)
+    count = comps * nodes // 24
+    wide = 2 * blocks
+    plain = plain_matrix(offset_ref[...])
 
     def ends_of(ref):
         last = ref[:, lanes - 128 :]
         if fast:
             last = pltpu.roll(last, (lax.axis_index(axes[2]) + 1) % 2 * slots, axis=1)
-        return jnp.concatenate([pltpu.roll(last, 2 * blocks, axis=1), last], axis=0)
+        config = pltpu.roll(last[24:32], wide, axis=1)
+        groups = [pltpu.roll(last[0:24], (count - g) * wide, axis=1) for g in range(count)]
+        rows = jnp.concatenate(groups, axis=0)
+        raw = rows[:nodes]
+        spread_config = config[0:1]
+        for k in range(1, comps):
+            here = lane >= k * wide
+            raw = jnp.where(here, pltpu.roll(rows[k * nodes : (k + 1) * nodes], k * wide, axis=1), raw)
+            spread_config = jnp.where(here[0:1], pltpu.roll(config, k * wide, axis=1)[0:1], spread_config)
+        raw = jnp.where(lane < comps * wide, raw, 0.0)
+        return raw + configured(dot(plain, tripled(*split(raw))), spread_config, nconf)
 
     z_a = ends_of(za_ref)
     z_low, z_up = sides(even_z, open_z, z_a, z_a if fast else ends_of(zb_ref))
-    z_ref[pl.ds(0, comps * face, stride=4), :] = z_low
-    z_ref[pl.ds(3, comps * face, stride=4), :] = z_up
+    z_low, z_up = pltpu.roll(z_low, nodes - 3, axis=0), pltpu.roll(z_up, 3, axis=0)
+    config_rows = [config_ref[y : y + 1, :] for y in range(blocks)]
+    matrix = matrix_ref[...]
 
     for k in range(comps):
         pair = con_ref[2 * k * nodes : 2 * (k + 1) * nodes, :]
         ops = dot(table, pair)
         rows = slice(k * face, (k + 1) * face)
         x_low, x_up = sides(even_x, open_x, xa_ref[rows, :], xb_ref[rows, :])
-        z_face = z_ref[k * nodes : (k + 1) * nodes, :]
+        values = []
         for y in range(blocks):
             x_at, y_at = y // cy, y % cy
             cells = slice(y * cz, (y + 1) * cz)
             value = pair[:nodes, cells].astype(F32) + pair[nodes:, cells].astype(F32)
             total = keep * value + viscosity_ref[y : y + 1, :] * ops[0:nodes, cells]
             moved_z = ops[nodes : 2 * nodes, cells]
-            below = jnp.where(lane == 0, pltpu.roll(z_face, (blocks - y) % cz, axis=1), pltpu.roll(moved_z, 1, axis=1))
+            below = jnp.where(lane == 0, pltpu.roll(z_low, cz - k * wide - blocks - y, axis=1), pltpu.roll(moved_z, 1, axis=1))
             above = jnp.where(
-                lane == cz - 1, pltpu.roll(z_face, (2 * blocks - 1 - y) % cz, axis=1), pltpu.roll(moved_z, cz - 1, axis=1)
+                lane == cz - 1, pltpu.roll(z_up, cz - 1 - k * wide - y, axis=1), pltpu.roll(moved_z, cz - 1, axis=1)
             )
             near = jnp.where(c == 0, below, jnp.where(c == 3, above, 0.0))
             if y_at > 0:
@@ -337,14 +362,18 @@
                 above = pair[:face, other].astype(F32) + pair[nodes : nodes + face, other].astype(F32)
             else:
                 above = x_up[:, plane]
-            total_ref[k * nodes : (k + 1) * nodes, cells] = jnp.concatenate(
+            total = jnp.concatenate(
                 [total[:face] - PENALTY * below, total[face : nodes - face], total[nodes - face :] - PENALTY * above],
                 axis=0,
             )
-
-    turned = jnp.concatenate([offset_ref[w * nodes : (w + 1) * nodes, :].T for w in range(nconf)], axis=0)
-    high, low = split(turned)
-    matrix_ref[...] = jnp.concatenate([high, high, low], axis=1)
+            values.append(total)
+        inner = [y for y in range(blocks) if 0 < y % cy < cy - 1]
+        if inner:
+            product = dot(matrix, tripled(*split(jnp.concatenate([values[y] for y in inner], axis=1))))
+            for i, y in enumerate(inner):
+                values[y] = values[y] + configured(product[:, i * cz : (i + 1) * cz], config_rows[y], nconf)
+        for y in range(blocks):
+            total_ref[k * nodes : (k + 1) * nodes, y * cz : (y + 1) * cz] = values[y]
 
 
 def widen(face, nodes):
@@ -367,12 +396,18 @@
 
 def after(
     dims, axes, sizes, fast,
-    total_ref, matrix_ref, config_ref, hot_ref, basis_ref, own_ref, ya_ref, yb_ref, *refs,
+    total_ref, yb_ref, *refs,
 ):
     if fast:
-        refs = (refs[0], ya_ref, refs[1], yb_ref, *refs[2:])
+        got_2, ya_ref, pair_ref, *refs = refs
+        refs = (*refs[:5], pair_ref, ya_ref, got_2, yb_ref, *refs[5:])
+    else:
+        ya_ref, parts_ref, *refs = refs
+        refs = (*refs[:5], parts_ref, *refs[5:])
+    matrix_ref, config_ref, hot_ref, weight_ref, own_ref, *refs = refs
+    if fast:
         ya_ref, yb_ref = ya_ref.at[24:, :], yb_ref.at[24:, :]
-    *part_refs, out_hbm, deform_hbm, rhs_ref, total2_ref, out_ref, deform_ref, sems = refs
+    *part_refs, out_hbm, deform_hbm, out_ref, deform_ref, sems = refs
     comps, nodes, cx, cy, cz, nconf, slots, lanes = dims
     blocks = cx * cy
     face = nodes // 4
@@ -388,7 +423,7 @@
     copies = [pltpu.make_async_copy(deform_ref, deform_hbm, sems.at[4 * comps])]
     copies[0].start()
     hot = hot_ref[...]
-    basis = [basis_ref[j * nodes : (j + 1) * nodes, :] for j in range(4)]
+    basis = [weight_ref[j * nodes : (j + 1) * nodes, :] for j in range(4)]
     row = iota((nodes, cz), 0)
     b = (row >> 2) & 3
     live = iota((nodes, lanes), 1) < slots
@@ -402,38 +437,32 @@
         lows.append(low)
     spreads = dot(jnp.concatenate(highs + lows, axis=0), hot, ((1,), (1,)))
 
+    config_rows = [config_ref[y : y + 1, :] for y in range(blocks)]
+    matrix = matrix_ref[...]
+    step = nodes * blocks // 4
+    outer = [y for y in range(blocks) if y % cy in (0, cy - 1)]
     for k in range(comps):
-        other = (comps + k) * nodes
-        spread = spreads[k * nodes : (k + 1) * nodes] + spreads[other : other + nodes]
         rows = slice(k * face, (k + 1) * face)
         y_low, y_up = sides(even_y, open_y, ya_ref[rows, :], yb_ref[rows, :])
+        values = [total_ref[k * nodes : (k + 1) * nodes, y * cz : (y + 1) * cz] for y in range(blocks)]
+        for y in outer:
+            plane = slice(y // cy * cz, (y // cy + 1) * cz)
+            if y % cy == 0:
+                values[y] = values[y] - jnp.where(b == 0, PENALTY * widen(y_low[:, plane], nodes), 0.0)
+            if y % cy == cy - 1:
+                values[y] = values[y] - jnp.where(b == 3, PENALTY * widen(y_up[:, plane], nodes), 0.0)
+        product = dot(matrix, tripled(*split(jnp.concatenate([values[y] for y in outer], axis=1))))
+        for i, y in enumerate(outer):
+            values[y] = values[y] + configured(product[:, i * cz : (i + 1) * cz], config_rows[y], nconf)
         for y in range(blocks):
-            x_at, y_at = y // cy, y % cy
             cells = slice(y * cz, (y + 1) * cz)
-            total = total_ref[k * nodes : (k + 1) * nodes, cells] - spread[:, cells]
-            plane = slice(x_at * cz, (x_at + 1) * cz)
-            if y_at == 0:
-                total = total - jnp.where(b == 0, PENALTY * widen(y_low[:, plane], nodes), 0.0)
-            if y_at == cy - 1:
-                total = total - jnp.where(b == 3, PENALTY * widen(y_up[:, plane], nodes), 0.0)
-            total2_ref[k * nodes : (k + 1) * nodes, cells] = total
-            put_split(rhs_ref, (k * blocks + y) * cz, cz, nodes, total)
-
-    config_rows = [config_ref[y : y + 1, :] for y in range(blocks)]
-
-    def add(k, y):
-        return total2_ref[k * nodes : (k + 1) * nodes, y * cz : (y + 1) * cz]
-
-    def store(k, y, value):
-        out_ref[pl.ds(k * nodes * blocks + y, nodes, stride=blocks), :] = value
-        if y == blocks - 1:
-            step = nodes * blocks // 4
-            for i in range(4 * k, 4 * k + 4):
-                done = slice(i * step, (i + 1) * step)
-                copies.append(pltpu.make_async_copy(out_ref.at[done, :], out_hbm.at[done, :], sems.at[i]))
-                copies[-1].start()
-
-    constrain(matrix_ref[...], rhs_ref, config_rows, add, store, nconf, nodes, comps, blocks, cz)
+            for part in (k, comps + k):
+                values[y] = values[y] - spreads[part * nodes : (part + 1) * nodes, cells]
+            out_ref[pl.ds(k * nodes * blocks + y, nodes, stride=blocks), :] = values[y]
+        for i in range(4 * k, 4 * k + 4):
+            done = slice(i * step, (i + 1) * step)
+            copies.append(pltpu.make_async_copy(out_ref.at[done, :], out_hbm.at[done, :], sems.at[i]))
+            copies[-1].start()
     for copy in copies:
         copy.wait()
 
@@ -469,7 +498,7 @@
     slots = slot_cells.shape[-1]
     n_dx, n_dy, n_solid = mesh_sizes
     face_rows = comps * nodes // 4
-    lanes = pl.cdiv(slots + 4 * blocks, 128) * 128
+    lanes = pl.cdiv(slots + comps * nodes // 24 * 2 * blocks, 128) * 128
     dims = (comps, nodes, cx, cy, cz, nconf, slots, lanes)
 
     v = velocity.reshape(comps * nodes * blocks, cz)
@@ -494,12 +523,12 @@
         return pl.CostEstimate(flops=2 * 6 * nconf * nodes * nodes * columns, bytes_accessed=1_000_000, transcendentals=0)
 
     fast = (n_dx, n_dy, n_solid, slots, lanes) == (4, 4, 2, 64, 128)
-    talk, own, rhs, matrix, hot, basis, config, offsets, visc = pl.pallas_call(
+    talk, own, parted, matrix, hot, weights, config, offsets, visc = pl.pallas_call(
         functools.partial(begin, dims, axes, fast),
         out_shape=(
+            shape(32, lanes),
             shape(24, lanes),
-            shape(24, lanes),
-            shape(3 * nodes, comps * cells, dtype=BF16),
+            shape(2 * comps * nodes, cells, dtype=BF16),
             shape(nconf * nodes, 3 * nodes, dtype=BF16),
             shape(cells, lanes, dtype=BF16),
             shape(4 * nodes, lanes),
@@ -515,8 +544,6 @@
             pltpu.VMEM(xi.shape, F32),
             pltpu.VMEM(strain.shape, F32),
             pltpu.VMEM(motion.shape, F32),
-            pltpu.VMEM((3 * nodes, comps * lanes), BF16),
-            pltpu.VMEM((comps * nodes, 128), F32),
             pltpu.SemaphoreType.DMA((8,)),
         ],
         compiler_params=params,
@@ -532,40 +559,36 @@
         compiler_params=params,
         cost_estimate=estimate(comps * cells),
         name="local",
-    )(rhs, matrix, config)
+    )(parted, offsets, config)
 
     if fast:
         got_s = swap(talk, "solid", 0)
         got_xa = swap(xa, "dx", 0)
         got_xb = flip(xb, "dx", 3)
         mine = (iota((24, 128), 1) >= 64) == (lax.axis_index("solid") == 1)
-        pair = jnp.where(mine, talk, got_s)
+        pair = jnp.where(mine, talk[:24], got_s[:24])
         got_3 = flip(jnp.concatenate([pair, yb, pair[:8]], axis=0), "dy", 3)
         got_2 = flip(jnp.concatenate([pair, yb[:8]], axis=0), "dy", 2)
         got_1 = flip(jnp.concatenate([pair, ya], axis=0), "dy", 1)
-        parts = [pair, got_2]
-        got_ya, got_yb = got_1, got_3
+        parts = [got_2, got_1, pair]
+        got_yb = got_3
         got_za, got_zb = got_s, got_s
     else:
         got_xa, got_xb = swap(xa, "dx", 0), swap(xb, "dx", 1)
         got_ya, got_yb = swap(ya, "dy", 0), swap(yb, "dy", 1)
         got_za, got_zb = swap(talk, "solid", 0), swap(talk, "solid", 1)
-        parts = lax.all_to_all(talk[:, :slots], ("dy", "solid"), split_axis=1, concat_axis=1, tiled=True)
-        parts = [jnp.pad(parts, ((0, 0), (0, lanes - slots)))]
-
-    total, matrix = pl.pallas_call(
+        got_parts = lax.all_to_all(talk[:24, :slots], ("dy", "solid"), split_axis=1, concat_axis=1, tiled=True)
+        parts = [got_ya, jnp.pad(got_parts, ((0, 0), (0, lanes - slots)))]
+
+    total = pl.pallas_call(
         functools.partial(middle, dims, axes, mesh_sizes, fast),
-        out_shape=(
-            jax.ShapeDtypeStruct((comps * nodes, cells), F32),
-            jax.ShapeDtypeStruct((nconf * nodes, 3 * nodes), BF16),
-        ),
-        in_specs=[vmem] * 7,
-        out_specs=(vmem,) * 2,
-        scratch_shapes=[pltpu.VMEM((comps * nodes, 128), F32)],
+        out_shape=shape(comps * nodes, cells),
+        in_specs=[vmem] * 9,
+        out_specs=vmem,
         compiler_params=params,
         cost_estimate=estimate(comps * cells),
         name="middle",
-    )(con, visc, offsets, got_xa, got_xb, got_za, got_zb)
+    )(got_za, con, visc, offsets, matrix, config, got_xa, got_xb, got_zb)
 
     out, deform = pl.pallas_call(
         functools.partial(after, dims, axes, mesh_sizes, fast),
@@ -573,18 +596,16 @@
             jax.ShapeDtypeStruct(v.shape, F32),
             jax.ShapeDtypeStruct((9, 1, slots), F32),
         ),
-        in_specs=[vmem] * (8 + len(parts)),
+        in_specs=[vmem] * (7 + len(parts)),
         out_specs=(hbm, hbm),
         scratch_shapes=[
-            pltpu.VMEM((3 * nodes, comps * cells), BF16),
-            pltpu.VMEM((comps * nodes, cells), F32),
             pltpu.VMEM(v.shape, F32),
             pltpu.VMEM(strain.shape, F32),
             pltpu.SemaphoreType.DMA((4 * comps + 1,)),
         ],
         compiler_params=params,
         name="after",
-    )(total, matrix, config, hot, basis, own, got_ya, got_yb, *parts)
+    )(total, got_yb, *parts, matrix, config, hot, weights, own)
     return out.reshape(velocity.shape), deform.reshape(strain_offsets.shape)
 
 

time: 18.2 us -> 17.9 us (0.984)
  waiting for transfers between devices: 3.08 us -> 2.67 us
    ppermute x4, waiting for transfers between devices: 3.07 us -> 2.66 us  [flip(): lax.ppermute(x, axis, [(i, i ^ bits) for i in range(lax.axis_size(axis))])]
    pallas_call x1, Pallas kernels: 0.77 us -> 1.16 us  [shards(): pl.pallas_call(functools.partial(middle, dims, axes, mesh_sizes, fast), o...]
    pallas_call x1, Pallas kernels: 1.76 us -> 1.46 us  [shards(): pl.pallas_call(functools.partial(after, dims, axes, mesh_sizes, fast), ou...]
  transfers between devices with their start and end apart: 6 -> 6, of which waited for: 1 -> 1; matrix products, arithmetic and copies ran while one was open for 0% -> 0% of each run, Pallas kernels for 8% -> 10%
where the time goes in v4:
time: 17.9 us; the launch traced here: 17.7 us
  starting transfers between devices  9.16 us (51%)
  Pallas kernels  5.15 us (29%)
  waiting for transfers between devices  2.67 us (15%)
  between operations  0.69 us (4%)
    ppermute x4, starting transfers between devices, flip(): lax.ppermute(x, axis, [(i, i ^ bits) for i in range(lax.axis_size(axis))])  6.06 us
    ppermute x2, starting transfers between devices, swap(): return lax.ppermute(x, axis, pairs + [(j, i) for i, j in pairs])  3.1 us
    ppermute x4, waiting for transfers between devices, flip(): lax.ppermute(x, axis, [(i, i ^ bits) for i in range(lax.axis_size(axis))])  2.66 us
    pallas_call x1, Pallas kernels, shards(): pl.pallas_call(functools.partial(begin, dims, axes, fast), out_shape=(sha...  1.87 us
    pallas_call x1, Pallas kernels, shards(): pl.pallas_call(functools.partial(after, dims, axes, mesh_sizes, fast), ou...  1.46 us
    pallas_call x1, Pallas kernels, shards(): pl.pallas_call(functools.partial(middle, dims, axes, mesh_sizes, fast), o...  1.16 us
    pallas_call x1, Pallas kernels, shards(): pl.pallas_call(functools.partial(local, dims, axes), out_shape=(shape(2 *...  0.66 us
  transfers between devices with their start and end apart: 6, of which 1 were waited for; matrix products, arithmetic and copies ran while one was open for 0% of the time, Pallas kernels for 10%

profile of v4, /device:TPU:0, one launch (start us, length us, event | category | flops | bytes accessed | tf_op | source)
XLA Modules:
  0.0 17.7 jit_solution(1244907524202733496)
XLA Ops:
  0.6 1.9 %begin.1 = (f32[32,128]{1,0:T(8,128)S(1)}, f32[24,128]{1,0:T(8,128)S(1)}, bf16[384,512]{1,0:T(8,128)(2,1)S(1)}, bf16[512,192]{1,0:T(8,128)(2,1)S(1)}, bf16[512,1...) custom-call(f32[768,128]{1,0:T(8,128)} %bitcast.14, ...), custom_call_target="tpu_custom_call" | custom-call | tf_op jit(solution)/shard_map/begin/pallas_call | solution.py:526
  2.5 3.0 %collective-permute-start = (f32[32,128]{1,0:T(8,128)S(1)}, f32[32,128]{1,0:T(8,128)S(1)}, u32[]{:S(2)}, u32[]{:S(2)}) collective-permute-start(f32[32,128]{1,0:T(8,128)S(1)} %get-tuple-element.18), channel_id=1, source_target_pairs={{0,1},{1,0},{2,3},{3,2},{4,5},{5,4},{6,7},{7,6},{8,9},{9,8},{10,11... | collective-permute-start | bytes 49160 | tf_op jit(solution)/shard_map/ppermute | solution.py:475
  5.5 0.7 %local.1 = (bf16[384,512]{1,0:T(8,128)(2,1)S(1)}, f32[48,512]{1,0:T(8,128)S(1)}, f32[48,512]{1,0:T(8,128)S(1)}, f32[48,128]{1,0:T(8,128)S(1)}, f32[48,128]{1,0:T(8,128)S(1)}) custom-call(bf16[384,512]{1,0:T(8,128)(2,1)S(1)} %get-tuple-element.19.split_ref, f32[512,64]{1,0:T(8,128)S(1)} %get-tuple-element.20.offset_ref, ...), custom_call_target="tpu_custom_call" | custom-call | flops 603979776 | bytes 1000000 | tf_op jit(solution)/shard_map/local/pallas_call | solution.py:553
  6.2 0.1 collective-permute-start.1
  6.3 1.6 %collective-permute-start.2 = (f32[48,512]{1,0:T(8,128)S(1)}, f32[48,512]{1,0:T(8,128)S(1)}, u32[]{:S(2)}, u32[]{:S(2)}) collective-permute-start(f32[48,512]{1,0:T(8,128)S(1)} %get-tuple-element.26), channel_id=1, source_target_pairs={{0,24},{8,16},{16,8},{24,0},{1,25},{9,17},{17,9},{25,1},{2,26},{10... | collective-permute-start | bytes 294920 | tf_op jit(solution)/shard_map/ppermute | solution.py:479
  7.9 0.0 collective-permute-done.za_ref.zb_ref
  8.0 3.6 %collective-permute-start.3 = (f32[80,128]{1,0:T(8,128)S(1)}, f32[80,128]{1,0:T(8,128)S(1)}, u32[]{:S(2)}, u32[]{:S(2)}) collective-permute-start(f32[80,128]{1,0:T(8,128)S(1)} %pad_maximum_fusion), channel_id=1, source_target_pairs={{0,6},{2,4},{4,2},{6,0},{1,7},{3,5},{5,3},{7,1},{8,14},{10,12},{12... | collective-permute-start | bytes 122888 | tf_op jit(solution)/shard_map/ppermute | solution.py:479
  11.6 0.0 collective-permute-start.4
  11.6 0.8 %collective-permute-start.5 = (f32[72,128]{1,0:T(8,128)S(1)}, f32[72,128]{1,0:T(8,128)S(1)}, u32[]{:S(2)}, u32[]{:S(2)}) collective-permute-start(f32[72,128]{1,0:T(8,128)S(1)} %pad_maximum_fusion.1), channel_id=1, source_target_pairs={{0,2},{2,0},{4,6},{6,4},{1,3},{3,1},{5,7},{7,5},{8,10},{10,8},{12,... | collective-permute-start | bytes 110600 | tf_op jit(solution)/shard_map/ppermute | solution.py:479
  12.4 0.0 collective-permute-done.1.xa_ref
  12.4 0.0 collective-permute-done.2.xb_ref
  12.4 1.2 %middle.1.total_ref = f32[192,512]{1,0:T(8,128)S(1)} custom-call(f32[32,128]{1,0:T(8,128)S(1)} %collective-permute-done.za_ref.zb_ref, bf16[384,512]{1,0:T(8,128)(2,1)S(1)} %get-tuple-element.22.con_ref, f32[4,128]{1,0:T(4,128)S(1)} %get-tuple-element.23.viscosity_ref, f32[512,64]{1,0:T(8,128)S(1)} %get-tuple-element.20.offset_ref, ...), custom_call_target="tpu_custom_call" | custom-call | flops 603979776 | bytes 1000000 | tf_op jit(solution)/shard_map/middle/pallas_call | solution.py:583
  13.6 2.7 %collective-permute-done.4.refs_0_ = f32[32,128]{1,0:T(8,128)S(1)} collective-permute-done((f32[32,128]{1,0:T(8,128)S(1)}, f32[32,128]{1,0:T(8,128)S(1)}, u32[]{:S(2)}, u32[]{:S(2)}) %collective-permute-start.4) | collective-permute-done | bytes 16416 | tf_op jit(solution)/shard_map/ppermute | solution.py:479
  16.2 0.0 collective-permute-done.5.refs_1_
  16.2 0.0 collective-permute-done.3.yb_ref
  16.2 1.5 %after.1 = (f32[768,128]{1,0:T(8,128)}, f32[9,1,64]{2,1,0:T(1,128)}) custom-call(f32[192,512]{1,0:T(8,128)S(1)} %middle.1.total_ref, f32[80,128]{1,0:T(8,128)S(1)} %collective-permute-done.3.yb_ref, f32[32,128]{1,0:T(8,128)S(1)} %collective-permute-done.4.refs_0_, f32[72,128]{1,0:T(8,128)S(1)} %collective-permute-done.5.refs_1_, ...), custom_call_target="tpu_custom_call" | custom-call | tf_op jit(solution)/shard_map/after/pallas_call | solution.py:593
  (7 shorter events, 0.0 us)
Async XLA Ops:
  2.5 5.4 %collective-permute-start = (f32[32,128]{1,0:T(8,128)S(1)}, f32[32,128]{1,0:T(8,128)S(1)}, u32[]{:S(2)}, u32[]{:S(2)}) collective-permute-start(f32[32,128]{1,0:T(8,128)S(1)} %get-tuple-element.18), channel_id=1, source_target_pairs={{0,1},{1,0},{2,3},{3,2},{4,5},{5,4},{6,7},{7,6},{8,9},{9,8},{10,11... | collective-permute-start | bytes 49160 | tf_op jit(solution)/shard_map/ppermute | solution.py:475
  6.2 6.2 %collective-permute-start.1 = (f32[48,512]{1,0:T(8,128)S(1)}, f32[48,512]{1,0:T(8,128)S(1)}, u32[]{:S(2)}, u32[]{:S(2)}) collective-permute-start(f32[48,512]{1,0:T(8,128)S(1)} %get-tuple-element.25), channel_id=1, source_target_pairs={{0,8},{16,24},{8,0},{24,16},{1,9},{17,25},{9,1},{25,17},{2,10},{18... | collective-permute-start | bytes 294920 | tf_op jit(solution)/shard_map/ppermute | solution.py:475
  6.3 6.1 %collective-permute-start.2 = (f32[48,512]{1,0:T(8,128)S(1)}, f32[48,512]{1,0:T(8,128)S(1)}, u32[]{:S(2)}, u32[]{:S(2)}) collective-permute-start(f32[48,512]{1,0:T(8,128)S(1)} %get-tuple-element.26), channel_id=1, source_target_pairs={{0,24},{8,16},{16,8},{24,0},{1,25},{9,17},{17,9},{25,1},{2,26},{10... | collective-permute-start | bytes 294920 | tf_op jit(solution)/shard_map/ppermute | solution.py:479
  8.0 8.3 %collective-permute-start.3 = (f32[80,128]{1,0:T(8,128)S(1)}, f32[80,128]{1,0:T(8,128)S(1)}, u32[]{:S(2)}, u32[]{:S(2)}) collective-permute-start(f32[80,128]{1,0:T(8,128)S(1)} %pad_maximum_fusion), channel_id=1, source_target_pairs={{0,6},{2,4},{4,2},{6,0},{1,7},{3,5},{5,3},{7,1},{8,14},{10,12},{12... | collective-permute-start | bytes 122888 | tf_op jit(solution)/shard_map/ppermute | solution.py:479
  11.6 4.6 %collective-permute-start.4 = (f32[32,128]{1,0:T(8,128)S(1)}, f32[32,128]{1,0:T(8,128)S(1)}, u32[]{:S(2)}, u32[]{:S(2)}) collective-permute-start(f32[32,128]{1,0:T(8,128)S(1)} %pad_maximum_fusion.2), channel_id=1, source_target_pairs={{0,4},{2,6},{4,0},{6,2},{1,5},{3,7},{5,1},{7,3},{8,12},{10,14},{12... | collective-permute-start | bytes 49160 | tf_op jit(solution)/shard_map/ppermute | solution.py:479
  11.6 4.6 %collective-permute-start.5 = (f32[72,128]{1,0:T(8,128)S(1)}, f32[72,128]{1,0:T(8,128)S(1)}, u32[]{:S(2)}, u32[]{:S(2)}) collective-permute-start(f32[72,128]{1,0:T(8,128)S(1)} %pad_maximum_fusion.1), channel_id=1, source_target_pairs={{0,2},{2,0},{4,6},{6,4},{1,3},{3,1},{5,7},{7,5},{8,10},{10,8},{12,... | collective-permute-start | bytes 110600 | tf_op jit(solution)/shard_map/ppermute | solution.py:479

commit v5 on v4

--- a/solution.py
+++ b/solution.py
@@ -117,7 +117,7 @@
 def begin(
     dims, axes, fast,
     v_hbm, config_hbm, offset_hbm, slot_hbm, xi_hbm, strain_hbm, motion_hbm, viscosity_hbm,
-    talk_ref, own_ref, split_ref, matrix_ref, hot_ref, weight_ref, config_ref, offset_ref, viscosity_ref,
+    talk_ref, own_ref, split_ref, matrix_ref, target_ref, weight_ref, config_ref, offset_ref, viscosity_ref,
     v_ref, slot_ref, xi_ref, strain_ref, motion_ref, sems,
 ):
     comps, nodes, cx, cy, cz, nconf, slots, lanes = dims
@@ -131,20 +131,21 @@
 
     for copy in copies[2:5]:
         copy.wait()
-    lane = iota((1, lanes), 1)
-    targets = jnp.concatenate([slot_ref[...], jnp.full((1, lanes - slots), -1, jnp.int32)], axis=1)
+    targets = jnp.concatenate([slot_ref[...]] * 2, axis=1)
+    target_ref[...] = targets
+    lane = iota((1, 128), 1)
+    ends = jnp.full((1, 128), -1, jnp.int32)
     for y in range(blocks):
-        targets = jnp.where(lane == lanes - 2 * blocks + y, y * cz, targets)
-        targets = jnp.where(lane == lanes - blocks + y, (y + 1) * cz - 1, targets)
-    hot = one_hot(targets, cells)
-    hot_ref[...] = hot
+        ends = jnp.where(lane == 128 - 2 * blocks + y, y * cz, ends)
+        ends = jnp.where(lane == 128 - blocks + y, (y + 1) * cz - 1, ends)
+    hot = one_hot(jnp.concatenate([targets, ends], axis=1), cells)
     config = jnp.concatenate([config_ref[y : y + 1, :] for y in range(blocks)], axis=1)
     config = dot(jnp.broadcast_to(config.astype(F32), (16, cells)).astype(BF16), hot)[0:1, :]
 
-    xi = [jnp.concatenate([xi_ref[j], jnp.zeros((1, lanes - slots), F32)], axis=1) for j in range(3)]
+    half = iota((1, lanes), 1) < slots
+    xi = [jnp.concatenate([xi_ref[j]] * 2, axis=1) for j in range(3)]
     (px, dx), (py, dy), (pz, dz) = shapes_of(xi, lanes)
-    whole = py * pz
-    basis = (px * whole, dx * whole, px * dy * pz, px * py * dz)
+    basis = (jnp.where(half, px, dx) * (py * pz), px * jnp.where(half, dy * pz, py * dz))
     for copy in copies[:2] + copies[5:]:
         copy.wait()
     raw = []
@@ -161,35 +162,37 @@
     matrix_ref[...] = matrix
     product = dot(matrix, jnp.concatenate([tripled(*split(p)) for p in basis], axis=1))
     weights = []
-    for j in range(4):
-        weights.append(basis[j] + configured(product[:, j * lanes : (j + 1) * lanes], config, nconf))
+    for j in range(2):
+        weights.append(basis[j] + configured(product[:, j * lanes : (j + 1) * lanes], config[:, :lanes], nconf))
         weight_ref[j * nodes : (j + 1) * nodes, :] = weights[j]
 
     for k in range(comps):
-        own_ref[k : k + 1, :] = jnp.sum(raw[k] * weights[0], axis=0, keepdims=True)
-        for j in range(3):
-            at = 3 + 3 * k + j
-            own_ref[at : at + 1, :] = jnp.sum(raw[k] * weights[1 + j], axis=0, keepdims=True)
+        for j in range(2):
+            sums = jnp.sum(raw[k][:, :lanes] * weights[j], axis=0, keepdims=True)
+            other = pltpu.roll(sums, slots, axis=1)
+            left, right = ((k, 3 + 3 * k), (4 + 3 * k, 5 + 3 * k))[j]
+            own_ref[left : left + 1, :] = jnp.where(half, sums, other)
+            own_ref[right : right + 1, :] = jnp.where(half, other, sums)
     for i in range(9):
-        own_ref[12 + i : 13 + i, 0:slots] = strain_ref[i]
+        own_ref[12 + i : 13 + i, :] = jnp.concatenate([strain_ref[i]] * 2, axis=1)
     for i in range(3):
-        own_ref[21 + i : 22 + i, 0:slots] = motion_ref[i]
+        own_ref[21 + i : 22 + i, :] = jnp.concatenate([motion_ref[i]] * 2, axis=1)
 
     count = comps * nodes // 24
     wide = 2 * blocks
-    ends = jnp.concatenate([r[:, lanes - 128 :] for r in raw], axis=0)
+    ends = jnp.concatenate([r[:, lanes:] for r in raw], axis=0)
     lane = iota((24, 128), 1)
     last = own_ref[:, lanes - 128 :]
     for g in range(count):
         start = 128 - (count - g) * wide
         group = pltpu.roll(ends[24 * g : 24 * (g + 1)], (start + wide) % 128, axis=1)
         last = jnp.where(lane >= start, group, last)
-    last = jnp.concatenate([last, jnp.broadcast_to(config[:, lanes - 128 :], (8, 128))], axis=0)
+    last = jnp.concatenate([last, jnp.broadcast_to(config[:, lanes:], (8, 128))], axis=0)
     if fast:
         last = pltpu.roll(last, lax.axis_index(axes[2]) * slots, axis=1)
-    elif lanes > 128:
-        talk_ref[0:24, : lanes - 128] = own_ref[:, : lanes - 128]
-    talk_ref[:, lanes - 128 :] = last
+    else:
+        talk_ref[0:24, :slots] = own_ref[:, :slots]
+    talk_ref[:, talk_ref.shape[1] - 128 :] = last
 
 
 def local(
@@ -284,8 +287,8 @@
 
 def middle(
     dims, axes, sizes, fast,
-    za_ref, con_ref, viscosity_ref, offset_ref, matrix_ref, config_ref, xa_ref, xb_ref, zb_ref,
-    total_ref,
+    za_ref, con_ref, viscosity_ref, offset_ref, matrix_ref, config_ref, xa_ref, xb_ref, zb_ref, target_ref,
+    total_ref, hot_ref,
 ):
     comps, nodes, cx, cy, cz, nconf, slots, lanes = dims
     blocks = cx * cy
@@ -306,9 +309,10 @@
     count = comps * nodes // 24
     wide = 2 * blocks
     plain = plain_matrix(offset_ref[...])
+    hot_ref[...] = one_hot(jnp.concatenate([target_ref[...]] * 2, axis=1), blocks * cz)
 
     def ends_of(ref):
-        last = ref[:, lanes - 128 :]
+        last = ref[:, ref.shape[1] - 128 :]
         if fast:
             last = pltpu.roll(last, (lax.axis_index(axes[2]) + 1) % 2 * slots, axis=1)
         config = pltpu.roll(last[24:32], wide, axis=1)
@@ -376,6 +380,10 @@
             total_ref[k * nodes : (k + 1) * nodes, y * cz : (y + 1) * cz] = values[y]
 
 
+def outer_blocks(cx, cy):
+    return [y for y in range(cx * cy) if y % cy in (0, cy - 1)]
+
+
 def widen(face, nodes):
     return jnp.concatenate([face[4 * (i // 4) : 4 * (i // 4) + 4] for i in range(nodes // 4)], axis=0)
 
@@ -394,24 +402,48 @@
     return parts + pltpu.roll(parts, 64, axis=1)
 
 
+def rim(
+    dims, axes, sizes, fast,
+    total_ref, yb_ref, ya_ref, matrix_ref, config_ref,
+    rim_ref,
+):
+    comps, nodes, cx, cy, cz, nconf, slots, lanes = dims
+    face = nodes // 4
+    even_y, open_y = place(axes[1], sizes[1])
+    first = 24 if fast else 0
+    b = (iota((nodes, cz), 0) >> 2) & 3
+    matrix = matrix_ref[...]
+    for k in range(comps):
+        rows = slice(first + k * face, first + (k + 1) * face)
+        y_low, y_up = sides(even_y, open_y, ya_ref[rows, :], yb_ref[rows, :])
+        outer = outer_blocks(cx, cy)
+        values = []
+        for y in outer:
+            plane = slice(y // cy * cz, (y // cy + 1) * cz)
+            value = total_ref[k * nodes : (k + 1) * nodes, y * cz : (y + 1) * cz]
+            if y % cy == 0:
+                value = value - jnp.where(b == 0, PENALTY * widen(y_low[:, plane], nodes), 0.0)
+            if y % cy == cy - 1:
+                value = value - jnp.where(b == 3, PENALTY * widen(y_up[:, plane], nodes), 0.0)
+            values.append(value)
+        product = dot(matrix, tripled(*split(jnp.concatenate(values, axis=1))))
+        for i, y in enumerate(outer):
+            at = slice(i * cz, (i + 1) * cz)
+            rim_ref[k * nodes : (k + 1) * nodes, at] = values[i] + configured(product[:, at], config_ref[y : y + 1, :], nconf)
+
+
 def after(
-    dims, axes, sizes, fast,
-    total_ref, yb_ref, *refs,
+    dims, axes, fast,
+    total_ref, *refs,
 ):
-    if fast:
-        got_2, ya_ref, pair_ref, *refs = refs
-        refs = (*refs[:5], pair_ref, ya_ref, got_2, yb_ref, *refs[5:])
-    else:
-        ya_ref, parts_ref, *refs = refs
-        refs = (*refs[:5], parts_ref, *refs[5:])
-    matrix_ref, config_ref, hot_ref, weight_ref, own_ref, *refs = refs
-    if fast:
-        ya_ref, yb_ref = ya_ref.at[24:, :], yb_ref.at[24:, :]
-    *part_refs, out_hbm, deform_hbm, out_ref, deform_ref, sems = refs
     comps, nodes, cx, cy, cz, nconf, slots, lanes = dims
     blocks = cx * cy
-    face = nodes // 4
-    even_y, open_y = place(axes[1], sizes[1])
+    if fast:
+        got_3, got_2, got_1, pair_ref, *refs = refs
+        part_refs = (pair_ref, got_1, got_2, got_3)
+    else:
+        *part_refs, refs = refs[0], refs[1:]
+    rim_ref, hot_ref, weight_ref, own_ref, out_hbm, deform_hbm, out_ref, deform_ref, sems = refs
 
     parts = gather_parts(part_refs, axes) if fast else part_refs[0][...]
     own = [own_ref[i : i + 1, :] for i in range(24)]
@@ -420,49 +452,33 @@
     moved, _, _ = solid(got[0:3], got[3:12], own[12:21], own[21:24])
     for i in range(9):
         deform_ref[i] = moved[i][:, :slots]
-    copies = [pltpu.make_async_copy(deform_ref, deform_hbm, sems.at[4 * comps])]
+    copies = [pltpu.make_async_copy(deform_ref, deform_hbm, sems.at[comps])]
     copies[0].start()
     hot = hot_ref[...]
-    basis = [weight_ref[j * nodes : (j + 1) * nodes, :] for j in range(4)]
-    row = iota((nodes, cz), 0)
-    b = (row >> 2) & 3
-    live = iota((nodes, lanes), 1) < slots
+    half = iota((1, lanes), 1) < slots
     highs, lows = [], []
     for k in range(comps):
-        force = drag[k] * basis[0]
-        for j in range(3):
-            force = force - stress[3 * k + j] * basis[1 + j]
-        high, low = split(jnp.where(live, force, 0.0))
+        force = jnp.where(half, drag[k], -stress[3 * k]) * weight_ref[:nodes, :]
+        force = force - jnp.where(half, stress[3 * k + 1], stress[3 * k + 2]) * weight_ref[nodes:, :]
+        high, low = split(force)
         highs.append(high)
         lows.append(low)
-    spreads = dot(jnp.concatenate(highs + lows, axis=0), hot, ((1,), (1,)))
-
-    config_rows = [config_ref[y : y + 1, :] for y in range(blocks)]
-    matrix = matrix_ref[...]
-    step = nodes * blocks // 4
-    outer = [y for y in range(blocks) if y % cy in (0, cy - 1)]
-    for k in range(comps):
-        rows = slice(k * face, (k + 1) * face)
-        y_low, y_up = sides(even_y, open_y, ya_ref[rows, :], yb_ref[rows, :])
-        values = [total_ref[k * nodes : (k + 1) * nodes, y * cz : (y + 1) * cz] for y in range(blocks)]
-        for y in outer:
-            plane = slice(y // cy * cz, (y // cy + 1) * cz)
-            if y % cy == 0:
-                values[y] = values[y] - jnp.where(b == 0, PENALTY * widen(y_low[:, plane], nodes), 0.0)
-            if y % cy == cy - 1:
-                values[y] = values[y] - jnp.where(b == 3, PENALTY * widen(y_up[:, plane], nodes), 0.0)
-        product = dot(matrix, tripled(*split(jnp.concatenate([values[y] for y in outer], axis=1))))
-        for i, y in enumerate(outer):
-            values[y] = values[y] + configured(product[:, i * cz : (i + 1) * cz], config_rows[y], nconf)
+    pieces = jnp.concatenate([jnp.concatenate(highs, axis=0), jnp.concatenate(lows, axis=0)], axis=1)
+    spreads = dot(pieces, hot, ((1,), (1,)))
+
+    outer = outer_blocks(cx, cy)
+    for k in range(comps):
+        rows = slice(k * nodes, (k + 1) * nodes)
         for y in range(blocks):
             cells = slice(y * cz, (y + 1) * cz)
-            for part in (k, comps + k):
-                values[y] = values[y] - spreads[part * nodes : (part + 1) * nodes, cells]
-            out_ref[pl.ds(k * nodes * blocks + y, nodes, stride=blocks), :] = values[y]
-        for i in range(4 * k, 4 * k + 4):
-            done = slice(i * step, (i + 1) * step)
-            copies.append(pltpu.make_async_copy(out_ref.at[done, :], out_hbm.at[done, :], sems.at[i]))
-            copies[-1].start()
+            if y in outer:
+                value = rim_ref[rows, outer.index(y) * cz : (outer.index(y) + 1) * cz]
+            else:
+                value = total_ref[rows, cells]
+            out_ref[pl.ds(k * nodes * blocks + y, nodes, stride=blocks), :] = value - spreads[rows, cells]
+        done = slice(k * nodes * blocks, (k + 1) * nodes * blocks)
+        copies.append(pltpu.make_async_copy(out_ref.at[done, :], out_hbm.at[done, :], sems.at[k]))
+        copies[-1].start()
     for copy in copies:
         copy.wait()
 
@@ -498,7 +514,8 @@
     slots = slot_cells.shape[-1]
     n_dx, n_dy, n_solid = mesh_sizes
     face_rows = comps * nodes // 4
-    lanes = pl.cdiv(slots + comps * nodes // 24 * 2 * blocks, 128) * 128
+    lanes = 2 * slots
+    talk_lanes = lanes if comps * nodes // 24 * 2 * blocks <= slots == 64 else slots + 128
     dims = (comps, nodes, cx, cy, cz, nconf, slots, lanes)
 
     v = velocity.reshape(comps * nodes * blocks, cz)
@@ -522,16 +539,16 @@
     def estimate(columns):
         return pl.CostEstimate(flops=2 * 6 * nconf * nodes * nodes * columns, bytes_accessed=1_000_000, transcendentals=0)
 
-    fast = (n_dx, n_dy, n_solid, slots, lanes) == (4, 4, 2, 64, 128)
-    talk, own, parted, matrix, hot, weights, config, offsets, visc = pl.pallas_call(
+    fast = (n_dx, n_dy, n_solid, slots, talk_lanes) == (4, 4, 2, 64, 128)
+    talk, own, parted, matrix, targets, weights, config, offsets, visc = pl.pallas_call(
         functools.partial(begin, dims, axes, fast),
         out_shape=(
-            shape(32, lanes),
+            shape(32, talk_lanes),
             shape(24, lanes),
             shape(2 * comps * nodes, cells, dtype=BF16),
             shape(nconf * nodes, 3 * nodes, dtype=BF16),
-            shape(cells, lanes, dtype=BF16),
-            shape(4 * nodes, lanes),
+            shape(1, lanes, dtype=targets.dtype),
+            shape(2 * nodes, lanes),
             shape(*config.shape, dtype=config.dtype),
             shape(*offsets.shape),
             shape(*visc.shape),
@@ -570,42 +587,49 @@
         got_3 = flip(jnp.concatenate([pair, yb, pair[:8]], axis=0), "dy", 3)
         got_2 = flip(jnp.concatenate([pair, yb[:8]], axis=0), "dy", 2)
         got_1 = flip(jnp.concatenate([pair, ya], axis=0), "dy", 1)
-        parts = [got_2, got_1, pair]
-        got_yb = got_3
+        parts = [got_3, got_2, got_1, pair]
+        got_ya, got_yb = got_1, got_3
         got_za, got_zb = got_s, got_s
     else:
         got_xa, got_xb = swap(xa, "dx", 0), swap(xb, "dx", 1)
         got_ya, got_yb = swap(ya, "dy", 0), swap(yb, "dy", 1)
         got_za, got_zb = swap(talk, "solid", 0), swap(talk, "solid", 1)
         got_parts = lax.all_to_all(talk[:24, :slots], ("dy", "solid"), split_axis=1, concat_axis=1, tiled=True)
-        parts = [got_ya, jnp.pad(got_parts, ((0, 0), (0, lanes - slots)))]
-
-    total = pl.pallas_call(
+        parts = [jnp.concatenate([got_parts] * 2, axis=1)]
+
+    total, hot = pl.pallas_call(
         functools.partial(middle, dims, axes, mesh_sizes, fast),
-        out_shape=shape(comps * nodes, cells),
-        in_specs=[vmem] * 9,
+        out_shape=(shape(comps * nodes, cells), shape(cells, 2 * lanes, dtype=BF16)),
+        in_specs=[vmem] * 10,
+        out_specs=(vmem,) * 2,
+        compiler_params=params,
+        cost_estimate=estimate(comps * cells),
+        name="middle",
+    )(got_za, con, visc, offsets, matrix, config, got_xa, got_xb, got_zb, targets)
+
+    rims = pl.pallas_call(
+        functools.partial(rim, dims, axes, mesh_sizes, fast),
+        out_shape=shape(comps * nodes, len(outer_blocks(cx, cy)) * cz),
+        in_specs=[vmem] * 5,
         out_specs=vmem,
         compiler_params=params,
         cost_estimate=estimate(comps * cells),
-        name="middle",
-    )(got_za, con, visc, offsets, matrix, config, got_xa, got_xb, got_zb)
+        name="rim",
+    )(total, got_yb, got_ya, matrix, config)
 
     out, deform = pl.pallas_call(
-        functools.partial(after, dims, axes, mesh_sizes, fast),
-        out_shape=(
-            jax.ShapeDtypeStruct(v.shape, F32),
-            jax.ShapeDtypeStruct((9, 1, slots), F32),
-        ),
-        in_specs=[vmem] * (7 + len(parts)),
+        functools.partial(after, dims, axes, fast),
+        out_shape=(shape(*v.shape), shape(9, 1, slots)),
+        in_specs=[vmem] * (5 + len(parts)),
         out_specs=(hbm, hbm),
         scratch_shapes=[
             pltpu.VMEM(v.shape, F32),
             pltpu.VMEM(strain.shape, F32),
-            pltpu.SemaphoreType.DMA((4 * comps + 1,)),
+            pltpu.SemaphoreType.DMA((comps + 1,)),
         ],
         compiler_params=params,
         name="after",
-    )(total, got_yb, *parts, matrix, config, hot, weights, own)
+    )(total, *parts, rims, hot, weights, own)
     return out.reshape(velocity.shape), deform.reshape(strain_offsets.shape)
 
 

time: 17.9 us -> 17.5 us (0.978)
  waiting for transfers between devices: 2.67 us -> 2.28 us
    ppermute x4, waiting for transfers between devices: 2.66 us -> 2.27 us  [flip(): lax.ppermute(x, axis, [(i, i ^ bits) for i in range(lax.axis_size(axis))])]
    pallas_call x1 -> x2, Pallas kernels: 1.46 us -> 1.49 us  [the longest x1 1.11 us: shards(): pl.pallas_call(functools.partial(after, dims, axes, fast), out_shape=(sha...]
  transfers between devices with their start and end apart: 6 -> 6, of which waited for: 1 -> 2; matrix products, arithmetic and copies ran while one was open for 0% -> 0% of each run, Pallas kernels for 10% -> 13%
where the time goes in v5:
time: 17.5 us; the launch traced here: 17.4 us
  starting transfers between devices  9.16 us (52%)
  Pallas kernels  5.2 us (30%)
  waiting for transfers between devices  2.28 us (13%)
  between operations  0.7 us (4%)
    ppermute x4, starting transfers between devices, flip(): lax.ppermute(x, axis, [(i, i ^ bits) for i in range(lax.axis_size(axis))])  6.05 us
    ppermute x2, starting transfers between devices, swap(): return lax.ppermute(x, axis, pairs + [(j, i) for i, j in pairs])  3.1 us
    ppermute x4, waiting for transfers between devices, flip(): lax.ppermute(x, axis, [(i, i ^ bits) for i in range(lax.axis_size(axis))])  2.27 us
    pallas_call x1, Pallas kernels, shards(): pl.pallas_call(functools.partial(begin, dims, axes, fast), out_shape=(sha...  1.87 us
    pallas_call x1, Pallas kernels, shards(): pl.pallas_call(functools.partial(middle, dims, axes, mesh_sizes, fast), o...  1.18 us
    pallas_call x1, Pallas kernels, shards(): pl.pallas_call(functools.partial(after, dims, axes, fast), out_shape=(sha...  1.11 us
    pallas_call x1, Pallas kernels, shards(): pl.pallas_call(functools.partial(local, dims, axes), out_shape=(shape(2 *...  0.66 us
    pallas_call x1, Pallas kernels, shards(): pl.pallas_call(functools.partial(rim, dims, axes, mesh_sizes, fast), out_...  0.38 us
  transfers between devices with their start and end apart: 6, of which 2 were waited for; matrix products, arithmetic and copies ran while one was open for 0% of the time, Pallas kernels for 13%

profile of v5, /device:TPU:0, one launch (start us, length us, event | category | flops | bytes accessed | tf_op | source)
XLA Modules:
  0.0 17.4 jit_solution(14600559684445608981)
XLA Ops:
  0.6 1.9 %begin.1 = (f32[32,128]{1,0:T(8,128)S(1)}, f32[24,128]{1,0:T(8,128)S(1)}, bf16[384,512]{1,0:T(8,128)(2,1)S(1)}, bf16[512,192]{1,0:T(8,128)(2,1)S(1)}, s32[1,128]...) custom-call(f32[768,128]{1,0:T(8,128)} %bitcast.14, ...), custom_call_target="tpu_custom_call" | custom-call | tf_op jit(solution)/shard_map/begin/pallas_call | solution.py:543
  2.5 3.0 %collective-permute-start = (f32[32,128]{1,0:T(8,128)S(1)}, f32[32,128]{1,0:T(8,128)S(1)}, u32[]{:S(2)}, u32[]{:S(2)}) collective-permute-start(f32[32,128]{1,0:T(8,128)S(1)} %get-tuple-element.20), channel_id=1, source_target_pairs={{0,1},{1,0},{2,3},{3,2},{4,5},{5,4},{6,7},{7,6},{8,9},{9,8},{10,11... | collective-permute-start | bytes 49160 | tf_op jit(solution)/shard_map/ppermute | solution.py:491
  5.5 0.7 %local.1 = (bf16[384,512]{1,0:T(8,128)(2,1)S(1)}, f32[48,512]{1,0:T(8,128)S(1)}, f32[48,512]{1,0:T(8,128)S(1)}, f32[48,128]{1,0:T(8,128)S(1)}, f32[48,128]{1,0:T(8,128)S(1)}) custom-call(bf16[384,512]{1,0:T(8,128)(2,1)S(1)} %get-tuple-element.21.split_ref, f32[512,64]{1,0:T(8,128)S(1)} %get-tuple-element.22.offset_ref, s32[4,128]{1,0:T(4,128)S(1)} %get-tuple-element.23.config_ref), custom_call_target="tpu_custom_call" | custom-call | flops 603979776 | bytes 1000000 | tf_op jit(solution)/shard_map/local/pallas_call | solution.py:570
  6.2 0.1 collective-permute-start.1
  6.3 1.6 %collective-permute-start.2 = (f32[48,512]{1,0:T(8,128)S(1)}, f32[48,512]{1,0:T(8,128)S(1)}, u32[]{:S(2)}, u32[]{:S(2)}) collective-permute-start(f32[48,512]{1,0:T(8,128)S(1)} %get-tuple-element.28), channel_id=1, source_target_pairs={{0,24},{8,16},{16,8},{24,0},{1,25},{9,17},{17,9},{25,1},{2,26},{10... | collective-permute-start | bytes 294920 | tf_op jit(solution)/shard_map/ppermute | solution.py:495
  7.9 0.0 collective-permute-done.za_ref.zb_ref
  7.9 3.7 %collective-permute-start.3 = (f32[80,128]{1,0:T(8,128)S(1)}, f32[80,128]{1,0:T(8,128)S(1)}, u32[]{:S(2)}, u32[]{:S(2)}) collective-permute-start(f32[80,128]{1,0:T(8,128)S(1)} %pad_maximum_fusion), channel_id=1, source_target_pairs={{0,6},{2,4},{4,2},{6,0},{1,7},{3,5},{5,3},{7,1},{8,14},{10,12},{12... | collective-permute-start | bytes 122888 | tf_op jit(solution)/shard_map/ppermute | solution.py:495
  11.6 0.0 collective-permute-start.4
  11.6 0.8 %collective-permute-start.5 = (f32[72,128]{1,0:T(8,128)S(1)}, f32[72,128]{1,0:T(8,128)S(1)}, u32[]{:S(2)}, u32[]{:S(2)}) collective-permute-start(f32[72,128]{1,0:T(8,128)S(1)} %pad_maximum_fusion.1), channel_id=1, source_target_pairs={{0,2},{2,0},{4,6},{6,4},{1,3},{3,1},{5,7},{7,5},{8,10},{10,8},{12,... | collective-permute-start | bytes 110600 | tf_op jit(solution)/shard_map/ppermute | solution.py:495
  12.4 0.0 collective-permute-done.1.xa_ref
  12.4 0.0 collective-permute-done.2.xb_ref
  12.4 1.2 %middle.1 = (f32[192,512]{1,0:T(8,128)S(1)}, bf16[512,256]{1,0:T(8,128)(2,1)S(1)}) custom-call(f32[32,128]{1,0:T(8,128)S(1)} %collective-permute-done.za_ref.zb_ref, bf16[384,512]{1,0:T(8,128)(2,1)S(1)} %get-tuple-element.24.con_ref, f32[4,128]{1,0:T(4,128)S(1)} %get-tuple-element.25.viscosity_ref, f32[512,64]{1,0:T(8,128)S(1)} %get-tuple-element.22.offset_ref, ...), custom_call_target="tpu_custom_call" | custom-call | flops 603979776 | bytes 1000000 | tf_op jit(solution)/shard_map/middle/pallas_call | solution.py:600
  13.6 2.1 %collective-permute-done.5.ya_ref.refs_2_ = f32[72,128]{1,0:T(8,128)S(1)} collective-permute-done((f32[72,128]{1,0:T(8,128)S(1)}, f32[72,128]{1,0:T(8,128)S(1)}, u32[]{:S(2)}, u32[]{:S(2)}) %collective-permute-start.5) | collective-permute-done | bytes 36896 | tf_op jit(solution)/shard_map/ppermute | solution.py:495
  15.7 0.0 collective-permute-done.3.yb_ref.refs_0_
  15.7 0.4 %rim.1.refs_4_ = f32[192,256]{1,0:T(8,128)S(1)} custom-call(f32[192,512]{1,0:T(8,128)S(1)} %get-tuple-element.30.total_ref, f32[80,128]{1,0:T(8,128)S(1)} %collective-permute-done.3.yb_ref.refs_0_, f32[72,128]{1,0:T(8,128)S(1)} %collective-permute-done.5.ya_ref.refs_2_, bf16[512,192]{1,0:T(8,128)(2,1)S(1)} %get-tuple-element.26.matrix_ref, ...), custom_call_target="tpu_custom_call" | custom-call | flops 603979776 | bytes 1000000 | tf_op jit(solution)/shard_map/rim/pallas_call | solution.py:610
  16.0 0.2 %collective-permute-done.4.refs_1_ = f32[32,128]{1,0:T(8,128)S(1)} collective-permute-done((f32[32,128]{1,0:T(8,128)S(1)}, f32[32,128]{1,0:T(8,128)S(1)}, u32[]{:S(2)}, u32[]{:S(2)}) %collective-permute-start.4) | collective-permute-done | bytes 16416 | tf_op jit(solution)/shard_map/ppermute | solution.py:495
  16.3 1.1 %after.1 = (f32[768,128]{1,0:T(8,128)}, f32[9,1,64]{2,1,0:T(1,128)}) custom-call(f32[192,512]{1,0:T(8,128)S(1)} %get-tuple-element.30.total_ref, f32[80,128]{1,0:T(8,128)S(1)} %collective-permute-done.3.yb_ref.refs_0_, f32[32,128]{1,0:T(8,128)S(1)} %collective-permute-done.4.refs_1_, f32[72,128]{1,0:T(8,128)S(1)} %collective-permute-done.5.ya_ref.refs_2_, ...), custom_call_target="tpu_custom_call" | custom-call | tf_op jit(solution)/shard_map/after/pallas_call | solution.py:620
  (7 shorter events, 0.0 us)
Async XLA Ops:
  2.5 5.4 %collective-permute-start = (f32[32,128]{1,0:T(8,128)S(1)}, f32[32,128]{1,0:T(8,128)S(1)}, u32[]{:S(2)}, u32[]{:S(2)}) collective-permute-start(f32[32,128]{1,0:T(8,128)S(1)} %get-tuple-element.20), channel_id=1, source_target_pairs={{0,1},{1,0},{2,3},{3,2},{4,5},{5,4},{6,7},{7,6},{8,9},{9,8},{10,11... | collective-permute-start | bytes 49160 | tf_op jit(solution)/shard_map/ppermute | solution.py:491
  6.2 6.2 %collective-permute-start.1 = (f32[48,512]{1,0:T(8,128)S(1)}, f32[48,512]{1,0:T(8,128)S(1)}, u32[]{:S(2)}, u32[]{:S(2)}) collective-permute-start(f32[48,512]{1,0:T(8,128)S(1)} %get-tuple-element.27), channel_id=1, source_target_pairs={{0,8},{16,24},{8,0},{24,16},{1,9},{17,25},{9,1},{25,17},{2,10},{18... | collective-permute-start | bytes 294920 | tf_op jit(solution)/shard_map/ppermute | solution.py:491
  6.3 6.1 %collective-permute-start.2 = (f32[48,512]{1,0:T(8,128)S(1)}, f32[48,512]{1,0:T(8,128)S(1)}, u32[]{:S(2)}, u32[]{:S(2)}) collective-permute-start(f32[48,512]{1,0:T(8,128)S(1)} %get-tuple-element.28), channel_id=1, source_target_pairs={{0,24},{8,16},{16,8},{24,0},{1,25},{9,17},{17,9},{25,1},{2,26},{10... | collective-permute-start | bytes 294920 | tf_op jit(solution)/shard_map/ppermute | solution.py:495
  7.9 7.7 %collective-permute-start.3 = (f32[80,128]{1,0:T(8,128)S(1)}, f32[80,128]{1,0:T(8,128)S(1)}, u32[]{:S(2)}, u32[]{:S(2)}) collective-permute-start(f32[80,128]{1,0:T(8,128)S(1)} %pad_maximum_fusion), channel_id=1, source_target_pairs={{0,6},{2,4},{4,2},{6,0},{1,7},{3,5},{5,3},{7,1},{8,14},{10,12},{12... | collective-permute-start | bytes 122888 | tf_op jit(solution)/shard_map/ppermute | solution.py:495
  11.6 4.6 %collective-permute-start.4 = (f32[32,128]{1,0:T(8,128)S(1)}, f32[32,128]{1,0:T(8,128)S(1)}, u32[]{:S(2)}, u32[]{:S(2)}) collective-permute-start(f32[32,128]{1,0:T(8,128)S(1)} %pad_maximum_fusion.2), channel_id=1, source_target_pairs={{0,4},{2,6},{4,0},{6,2},{1,5},{3,7},{5,1},{7,3},{8,12},{10,14},{12... | collective-permute-start | bytes 49160 | tf_op jit(solution)/shard_map/ppermute | solution.py:495
  11.6 4.0 %collective-permute-start.5 = (f32[72,128]{1,0:T(8,128)S(1)}, f32[72,128]{1,0:T(8,128)S(1)}, u32[]{:S(2)}, u32[]{:S(2)}) collective-permute-start(f32[72,128]{1,0:T(8,128)S(1)} %pad_maximum_fusion.1), channel_id=1, source_target_pairs={{0,2},{2,0},{4,6},{6,4},{1,3},{3,1},{5,7},{7,5},{8,10},{10,8},{12,... | collective-permute-start | bytes 110600 | tf_op jit(solution)/shard_map/ppermute | solution.py:495

commit v6 on v5

--- a/solution.py
+++ b/solution.py
@@ -85,6 +85,10 @@
     return jnp.concatenate([high, low, high], axis=0)
 
 
+def turned_parts(high, low):
+    return jnp.concatenate([high, high, low], axis=0)
+
+
 def constrain(matrix, columns, config_rows, store, nconf, comps, blocks, lanes):
     step = 2 if blocks % 2 == 0 else 1
     for k in range(comps):
@@ -109,9 +113,14 @@
 
 
 def turned_matrix(offsets, nconf, nodes):
-    turned = jnp.concatenate([offsets[w * nodes : (w + 1) * nodes, :].T for w in range(nconf)], axis=0)
-    high, low = split(turned)
-    return jnp.concatenate([high, high, low], axis=1)
+    blocks = [offsets[w * nodes : (w + 1) * nodes, :] for w in range(nconf)]
+    highs, lows = [], []
+    for block in blocks:
+        high = block.astype(BF16).astype(F32)
+        both = jnp.concatenate([high, block - high], axis=0).T.astype(BF16)
+        highs.append(both)
+        lows.append(both[:, :nodes])
+    return jnp.concatenate([jnp.concatenate(highs, axis=0), jnp.concatenate(lows, axis=0)], axis=1)
 
 
 def begin(
@@ -129,25 +138,34 @@
         sems,
     )
 
-    for copy in copies[2:5]:
+    for copy in copies:
         copy.wait()
     targets = jnp.concatenate([slot_ref[...]] * 2, axis=1)
     target_ref[...] = targets
-    lane = iota((1, 128), 1)
-    ends = jnp.full((1, 128), -1, jnp.int32)
+    wide = 2 * blocks
+    columns = pl.cdiv(slots + wide, 128) * 128
+    lane = iota((1, columns), 1)
+    both = jnp.concatenate([slot_ref[...], jnp.full((1, columns - slots), -1, jnp.int32)], axis=1)
     for y in range(blocks):
-        ends = jnp.where(lane == 128 - 2 * blocks + y, y * cz, ends)
-        ends = jnp.where(lane == 128 - blocks + y, (y + 1) * cz - 1, ends)
-    hot = one_hot(jnp.concatenate([targets, ends], axis=1), cells)
+        both = jnp.where(lane == columns - wide + y, y * cz, both)
+        both = jnp.where(lane == columns - blocks + y, (y + 1) * cz - 1, both)
+    hot = one_hot(both, cells)
     config = jnp.concatenate([config_ref[y : y + 1, :] for y in range(blocks)], axis=1)
     config = dot(jnp.broadcast_to(config.astype(F32), (16, cells)).astype(BF16), hot)[0:1, :]
 
     half = iota((1, lanes), 1) < slots
+
+    def twice(x):
+        if 2 * slots == columns:
+            return jnp.where(iota(x.shape, 1) < slots, x, pltpu.roll(x, slots, axis=1))
+        return jnp.concatenate([x[:, :slots]] * 2, axis=1)
+
+    config_twice = twice(config)
     xi = [jnp.concatenate([xi_ref[j]] * 2, axis=1) for j in range(3)]
     (px, dx), (py, dy), (pz, dz) = shapes_of(xi, lanes)
     basis = (jnp.where(half, px, dx) * (py * pz), px * jnp.where(half, dy * pz, py * dz))
-    for copy in copies[:2] + copies[5:]:
-        copy.wait()
+    matrix = turned_matrix(offset_ref[...], nconf, nodes)
+    matrix_ref[...] = matrix
     raw = []
     for k in range(comps):
         row = 2 * k * nodes
@@ -158,17 +176,16 @@
             split_ref[row + nodes : row + 2 * nodes, at] = low
         both = dot(split_ref[row : row + 2 * nodes, :], hot)
         raw.append(both[:nodes] + both[nodes:])
-    matrix = turned_matrix(offset_ref[...], nconf, nodes)
-    matrix_ref[...] = matrix
-    product = dot(matrix, jnp.concatenate([tripled(*split(p)) for p in basis], axis=1))
+    product = dot(matrix, jnp.concatenate([turned_parts(*split(p)) for p in basis], axis=1))
     weights = []
     for j in range(2):
-        weights.append(basis[j] + configured(product[:, j * lanes : (j + 1) * lanes], config[:, :lanes], nconf))
+        weights.append(basis[j] + configured(product[:, j * lanes : (j + 1) * lanes], config_twice, nconf))
         weight_ref[j * nodes : (j + 1) * nodes, :] = weights[j]
 
     for k in range(comps):
+        value = twice(raw[k])
         for j in range(2):
-            sums = jnp.sum(raw[k][:, :lanes] * weights[j], axis=0, keepdims=True)
+            sums = jnp.sum(value * weights[j], axis=0, keepdims=True)
             other = pltpu.roll(sums, slots, axis=1)
             left, right = ((k, 3 + 3 * k), (4 + 3 * k, 5 + 3 * k))[j]
             own_ref[left : left + 1, :] = jnp.where(half, sums, other)
@@ -179,15 +196,14 @@
         own_ref[21 + i : 22 + i, :] = jnp.concatenate([motion_ref[i]] * 2, axis=1)
 
     count = comps * nodes // 24
-    wide = 2 * blocks
-    ends = jnp.concatenate([r[:, lanes:] for r in raw], axis=0)
+    ends = jnp.concatenate([r[:, columns - 128 :] for r in raw], axis=0)
     lane = iota((24, 128), 1)
     last = own_ref[:, lanes - 128 :]
     for g in range(count):
         start = 128 - (count - g) * wide
         group = pltpu.roll(ends[24 * g : 24 * (g + 1)], (start + wide) % 128, axis=1)
         last = jnp.where(lane >= start, group, last)
-    last = jnp.concatenate([last, jnp.broadcast_to(config[:, lanes:], (8, 128))], axis=0)
+    last = jnp.concatenate([last, jnp.broadcast_to(config[:, columns - 128 :], (8, 128))], axis=0)
     if fast:
         last = pltpu.roll(last, lax.axis_index(axes[2]) * slots, axis=1)
     else:
@@ -373,7 +389,7 @@
             values.append(total)
         inner = [y for y in range(blocks) if 0 < y % cy < cy - 1]
         if inner:
-            product = dot(matrix, tripled(*split(jnp.concatenate([values[y] for y in inner], axis=1))))
+            product = dot(matrix, turned_parts(*split(jnp.concatenate([values[y] for y in inner], axis=1))))
             for i, y in enumerate(inner):
                 values[y] = values[y] + configured(product[:, i * cz : (i + 1) * cz], config_rows[y], nconf)
         for y in range(blocks):
@@ -426,7 +442,7 @@
             if y % cy == cy - 1:
                 value = value - jnp.where(b == 3, PENALTY * widen(y_up[:, plane], nodes), 0.0)
             values.append(value)
-        product = dot(matrix, tripled(*split(jnp.concatenate(values, axis=1))))
+        product = dot(matrix, turned_parts(*split(jnp.concatenate(values, axis=1))))
         for i, y in enumerate(outer):
             at = slice(i * cz, (i + 1) * cz)
             rim_ref[k * nodes : (k + 1) * nodes, at] = values[i] + configured(product[:, at], config_ref[y : y + 1, :], nconf)
@@ -584,7 +600,7 @@
         got_xb = flip(xb, "dx", 3)
         mine = (iota((24, 128), 1) >= 64) == (lax.axis_index("solid") == 1)
         pair = jnp.where(mine, talk[:24], got_s[:24])
-        got_3 = flip(jnp.concatenate([pair, yb, pair[:8]], axis=0), "dy", 3)
+        got_3 = flip(jnp.concatenate([pair, yb], axis=0), "dy", 3)
         got_2 = flip(jnp.concatenate([pair, yb[:8]], axis=0), "dy", 2)
         got_1 = flip(jnp.concatenate([pair, ya], axis=0), "dy", 1)
         parts = [got_3, got_2, got_1, pair]

time: 17.5 us -> 17.4 us (level)
  transfers between devices with their start and end apart: 6 -> 6, of which waited for: 2 -> 3; matrix products, arithmetic and copies ran while one was open for 0% -> 0% of each run, Pallas kernels for 13% -> 13%
where the time goes in v6:
time: 17.4 us; the launch traced here: 17.2 us
  starting transfers between devices  9.16 us (53%)
  Pallas kernels  5.05 us (29%)
  waiting for transfers between devices  2.29 us (13%)
  between operations  0.69 us (4%)
    ppermute x4, starting transfers between devices, flip(): lax.ppermute(x, axis, [(i, i ^ bits) for i in range(lax.axis_size(axis))])  6.06 us
    ppermute x2, starting transfers between devices, swap(): return lax.ppermute(x, axis, pairs + [(j, i) for i, j in pairs])  3.1 us
    ppermute x4, waiting for transfers between devices, flip(): lax.ppermute(x, axis, [(i, i ^ bits) for i in range(lax.axis_size(axis))])  2.29 us
    pallas_call x1, Pallas kernels, shards(): pl.pallas_call(functools.partial(begin, dims, axes, fast), out_shape=(sha...  1.73 us
    pallas_call x1, Pallas kernels, shards(): pl.pallas_call(functools.partial(middle, dims, axes, mesh_sizes, fast), o...  1.17 us
    pallas_call x1, Pallas kernels, shards(): pl.pallas_call(functools.partial(after, dims, axes, fast), out_shape=(sha...  1.11 us
    pallas_call x1, Pallas kernels, shards(): pl.pallas_call(functools.partial(local, dims, axes), out_shape=(shape(2 *...  0.66 us
    pallas_call x1, Pallas kernels, shards(): pl.pallas_call(functools.partial(rim, dims, axes, mesh_sizes, fast), out_...  0.38 us
  transfers between devices with their start and end apart: 6, of which 3 were waited for; matrix products, arithmetic and copies ran while one was open for 0% of the time, Pallas kernels for 13%

profile of v6, /device:TPU:0, one launch (start us, length us, event | category | flops | bytes accessed | tf_op | source)
XLA Modules:
  0.0 17.2 jit_solution(15028787224366502662)
XLA Ops:
  0.6 1.7 %begin.1 = (f32[32,128]{1,0:T(8,128)S(1)}, f32[24,128]{1,0:T(8,128)S(1)}, bf16[384,512]{1,0:T(8,128)(2,1)S(1)}, bf16[512,192]{1,0:T(8,128)(2,1)S(1)}, s32[1,128]...) custom-call(f32[768,128]{1,0:T(8,128)} %bitcast.14, ...), custom_call_target="tpu_custom_call" | custom-call | tf_op jit(solution)/shard_map/begin/pallas_call | solution.py:559
  2.4 3.0 %collective-permute-start = (f32[32,128]{1,0:T(8,128)S(1)}, f32[32,128]{1,0:T(8,128)S(1)}, u32[]{:S(2)}, u32[]{:S(2)}) collective-permute-start(f32[32,128]{1,0:T(8,128)S(1)} %get-tuple-element.20), channel_id=1, source_target_pairs={{0,1},{1,0},{2,3},{3,2},{4,5},{5,4},{6,7},{7,6},{8,9},{9,8},{10,11... | collective-permute-start | bytes 49160 | tf_op jit(solution)/shard_map/ppermute | solution.py:507
  5.4 0.7 %local.1 = (bf16[384,512]{1,0:T(8,128)(2,1)S(1)}, f32[48,512]{1,0:T(8,128)S(1)}, f32[48,512]{1,0:T(8,128)S(1)}, f32[48,128]{1,0:T(8,128)S(1)}, f32[48,128]{1,0:T(8,128)S(1)}) custom-call(bf16[384,512]{1,0:T(8,128)(2,1)S(1)} %get-tuple-element.21.split_ref, f32[512,64]{1,0:T(8,128)S(1)} %get-tuple-element.22.offset_ref, s32[4,128]{1,0:T(4,128)S(1)} %get-tuple-element.23.config_ref), custom_call_target="tpu_custom_call" | custom-call | flops 603979776 | bytes 1000000 | tf_op jit(solution)/shard_map/local/pallas_call | solution.py:586
  6.1 0.1 collective-permute-start.1
  6.2 1.6 %collective-permute-start.2 = (f32[48,512]{1,0:T(8,128)S(1)}, f32[48,512]{1,0:T(8,128)S(1)}, u32[]{:S(2)}, u32[]{:S(2)}) collective-permute-start(f32[48,512]{1,0:T(8,128)S(1)} %get-tuple-element.28), channel_id=1, source_target_pairs={{0,24},{8,16},{16,8},{24,0},{1,25},{9,17},{17,9},{25,1},{2,26},{10... | collective-permute-start | bytes 294920 | tf_op jit(solution)/shard_map/ppermute | solution.py:511
  7.8 0.0 collective-permute-done.za_ref.zb_ref
  7.8 3.7 %collective-permute-start.3 = (f32[72,128]{1,0:T(8,128)S(1)}, f32[72,128]{1,0:T(8,128)S(1)}, u32[]{:S(2)}, u32[]{:S(2)}) collective-permute-start(f32[72,128]{1,0:T(8,128)S(1)} %get-tuple-element.41), channel_id=1, source_target_pairs={{0,6},{2,4},{4,2},{6,0},{1,7},{3,5},{5,3},{7,1},{8,14},{10,12},{12... | collective-permute-start | bytes 110600 | tf_op jit(solution)/shard_map/ppermute | solution.py:511
  11.5 0.0 collective-permute-start.4
  11.5 0.8 %collective-permute-start.5 = (f32[72,128]{1,0:T(8,128)S(1)}, f32[72,128]{1,0:T(8,128)S(1)}, u32[]{:S(2)}, u32[]{:S(2)}) collective-permute-start(f32[72,128]{1,0:T(8,128)S(1)} %get-tuple-element.40), channel_id=1, source_target_pairs={{0,2},{2,0},{4,6},{6,4},{1,3},{3,1},{5,7},{7,5},{8,10},{10,8},{12,... | collective-permute-start | bytes 110600 | tf_op jit(solution)/shard_map/ppermute | solution.py:511
  12.3 0.0 collective-permute-done.1.xa_ref
  12.3 0.0 collective-permute-done.2.xb_ref
  12.3 1.2 %middle.1 = (f32[192,512]{1,0:T(8,128)S(1)}, bf16[512,256]{1,0:T(8,128)(2,1)S(1)}) custom-call(f32[32,128]{1,0:T(8,128)S(1)} %collective-permute-done.za_ref.zb_ref, bf16[384,512]{1,0:T(8,128)(2,1)S(1)} %get-tuple-element.24.con_ref, f32[4,128]{1,0:T(4,128)S(1)} %get-tuple-element.25.viscosity_ref, f32[512,64]{1,0:T(8,128)S(1)} %get-tuple-element.22.offset_ref, ...), custom_call_target="tpu_custom_call" | custom-call | flops 603979776 | bytes 1000000 | tf_op jit(solution)/shard_map/middle/pallas_call | solution.py:616
  13.4 0.2 %collective-permute-done.3.yb_ref.refs_0_ = f32[72,128]{1,0:T(8,128)S(1)} collective-permute-done((f32[72,128]{1,0:T(8,128)S(1)}, f32[72,128]{1,0:T(8,128)S(1)}, u32[]{:S(2)}, u32[]{:S(2)}) %collective-permute-start.3) | collective-permute-done | bytes 36896 | tf_op jit(solution)/shard_map/ppermute | solution.py:511
  13.6 1.8 %collective-permute-done.5.ya_ref.refs_2_ = f32[72,128]{1,0:T(8,128)S(1)} collective-permute-done((f32[72,128]{1,0:T(8,128)S(1)}, f32[72,128]{1,0:T(8,128)S(1)}, u32[]{:S(2)}, u32[]{:S(2)}) %collective-permute-start.5) | collective-permute-done | bytes 36896 | tf_op jit(solution)/shard_map/ppermute | solution.py:511
  15.4 0.4 %rim.1.refs_4_ = f32[192,256]{1,0:T(8,128)S(1)} custom-call(f32[192,512]{1,0:T(8,128)S(1)} %get-tuple-element.30.total_ref, f32[72,128]{1,0:T(8,128)S(1)} %collective-permute-done.3.yb_ref.refs_0_, f32[72,128]{1,0:T(8,128)S(1)} %collective-permute-done.5.ya_ref.refs_2_, bf16[512,192]{1,0:T(8,128)(2,1)S(1)} %get-tuple-element.26.matrix_ref, ...), custom_call_target="tpu_custom_call" | custom-call | flops 603979776 | bytes 1000000 | tf_op jit(solution)/shard_map/rim/pallas_call | solution.py:626
  15.8 0.3 %collective-permute-done.4.refs_1_ = f32[32,128]{1,0:T(8,128)S(1)} collective-permute-done((f32[32,128]{1,0:T(8,128)S(1)}, f32[32,128]{1,0:T(8,128)S(1)}, u32[]{:S(2)}, u32[]{:S(2)}) %collective-permute-start.4) | collective-permute-done | bytes 16416 | tf_op jit(solution)/shard_map/ppermute | solution.py:511
  16.1 1.1 %after.1 = (f32[768,128]{1,0:T(8,128)}, f32[9,1,64]{2,1,0:T(1,128)}) custom-call(f32[192,512]{1,0:T(8,128)S(1)} %get-tuple-element.30.total_ref, f32[72,128]{1,0:T(8,128)S(1)} %collective-permute-done.3.yb_ref.refs_0_, f32[32,128]{1,0:T(8,128)S(1)} %collective-permute-done.4.refs_1_, f32[72,128]{1,0:T(8,128)S(1)} %collective-permute-done.5.ya_ref.refs_2_, ...), custom_call_target="tpu_custom_call" | custom-call | tf_op jit(solution)/shard_map/after/pallas_call | solution.py:636
  (5 shorter events, 0.0 us)
Async XLA Ops:
  2.4 5.4 %collective-permute-start = (f32[32,128]{1,0:T(8,128)S(1)}, f32[32,128]{1,0:T(8,128)S(1)}, u32[]{:S(2)}, u32[]{:S(2)}) collective-permute-start(f32[32,128]{1,0:T(8,128)S(1)} %get-tuple-element.20), channel_id=1, source_target_pairs={{0,1},{1,0},{2,3},{3,2},{4,5},{5,4},{6,7},{7,6},{8,9},{9,8},{10,11... | collective-permute-start | bytes 49160 | tf_op jit(solution)/shard_map/ppermute | solution.py:507
  6.1 6.2 %collective-permute-start.1 = (f32[48,512]{1,0:T(8,128)S(1)}, f32[48,512]{1,0:T(8,128)S(1)}, u32[]{:S(2)}, u32[]{:S(2)}) collective-permute-start(f32[48,512]{1,0:T(8,128)S(1)} %get-tuple-element.27), channel_id=1, source_target_pairs={{0,8},{16,24},{8,0},{24,16},{1,9},{17,25},{9,1},{25,17},{2,10},{18... | collective-permute-start | bytes 294920 | tf_op jit(solution)/shard_map/ppermute | solution.py:507
  6.2 6.1 %collective-permute-start.2 = (f32[48,512]{1,0:T(8,128)S(1)}, f32[48,512]{1,0:T(8,128)S(1)}, u32[]{:S(2)}, u32[]{:S(2)}) collective-permute-start(f32[48,512]{1,0:T(8,128)S(1)} %get-tuple-element.28), channel_id=1, source_target_pairs={{0,24},{8,16},{16,8},{24,0},{1,25},{9,17},{17,9},{25,1},{2,26},{10... | collective-permute-start | bytes 294920 | tf_op jit(solution)/shard_map/ppermute | solution.py:511
  7.8 5.8 %collective-permute-start.3 = (f32[72,128]{1,0:T(8,128)S(1)}, f32[72,128]{1,0:T(8,128)S(1)}, u32[]{:S(2)}, u32[]{:S(2)}) collective-permute-start(f32[72,128]{1,0:T(8,128)S(1)} %get-tuple-element.41), channel_id=1, source_target_pairs={{0,6},{2,4},{4,2},{6,0},{1,7},{3,5},{5,3},{7,1},{8,14},{10,12},{12... | collective-permute-start | bytes 110600 | tf_op jit(solution)/shard_map/ppermute | solution.py:511
  11.5 4.6 %collective-permute-start.4 = (f32[32,128]{1,0:T(8,128)S(1)}, f32[32,128]{1,0:T(8,128)S(1)}, u32[]{:S(2)}, u32[]{:S(2)}) collective-permute-start(f32[32,128]{1,0:T(8,128)S(1)} %pad_maximum_fusion.2), channel_id=1, source_target_pairs={{0,4},{2,6},{4,0},{6,2},{1,5},{3,7},{5,1},{7,3},{8,12},{10,14},{12... | collective-permute-start | bytes 49160 | tf_op jit(solution)/shard_map/ppermute | solution.py:511
  11.5 4.0 %collective-permute-start.5 = (f32[72,128]{1,0:T(8,128)S(1)}, f32[72,128]{1,0:T(8,128)S(1)}, u32[]{:S(2)}, u32[]{:S(2)}) collective-permute-start(f32[72,128]{1,0:T(8,128)S(1)} %get-tuple-element.40), channel_id=1, source_target_pairs={{0,2},{2,0},{4,6},{6,4},{1,3},{3,1},{5,7},{7,5},{8,10},{10,8},{12,... | collective-permute-start | bytes 110600 | tf_op jit(solution)/shard_map/ppermute | solution.py:511

commit v7 on v6

--- a/solution.py
+++ b/solution.py
@@ -126,7 +126,7 @@
 def begin(
     dims, axes, fast,
     v_hbm, config_hbm, offset_hbm, slot_hbm, xi_hbm, strain_hbm, motion_hbm, viscosity_hbm,
-    talk_ref, own_ref, split_ref, matrix_ref, target_ref, weight_ref, config_ref, offset_ref, viscosity_ref,
+    talk_ref, self_ref, own_ref, split_ref, matrix_ref, target_ref, weight_ref, config_ref, offset_ref, viscosity_ref,
     v_ref, slot_ref, xi_ref, strain_ref, motion_ref, sems,
 ):
     comps, nodes, cx, cy, cz, nconf, slots, lanes = dims
@@ -191,24 +191,27 @@
             own_ref[left : left + 1, :] = jnp.where(half, sums, other)
             own_ref[right : right + 1, :] = jnp.where(half, other, sums)
     for i in range(9):
-        own_ref[12 + i : 13 + i, :] = jnp.concatenate([strain_ref[i]] * 2, axis=1)
+        own_ref[16 + i : 17 + i, :] = jnp.concatenate([strain_ref[i]] * 2, axis=1)
     for i in range(3):
-        own_ref[21 + i : 22 + i, :] = jnp.concatenate([motion_ref[i]] * 2, axis=1)
-
-    count = comps * nodes // 24
+        own_ref[25 + i : 26 + i, :] = jnp.concatenate([motion_ref[i]] * 2, axis=1)
+    for i in (12, 28):
+        own_ref[i : i + 4, :] = jnp.zeros((4, lanes), F32)
+
+    count = comps * nodes // 16
     ends = jnp.concatenate([r[:, columns - 128 :] for r in raw], axis=0)
-    lane = iota((24, 128), 1)
-    last = own_ref[:, lanes - 128 :]
+    lane = iota((16, 128), 1)
+    at_end = 128 - wide
+    packed = jnp.broadcast_to(pltpu.roll(config[:, columns - 128 :], (count * wide - at_end) % 128, axis=1), (16, 128))
     for g in range(count):
-        start = 128 - (count - g) * wide
-        group = pltpu.roll(ends[24 * g : 24 * (g + 1)], (start + wide) % 128, axis=1)
-        last = jnp.where(lane >= start, group, last)
-    last = jnp.concatenate([last, jnp.broadcast_to(config[:, columns - 128 :], (8, 128))], axis=0)
+        group = pltpu.roll(ends[16 * g : 16 * (g + 1)], (g * wide - at_end) % 128, axis=1)
+        packed = jnp.where((lane >= g * wide) & (lane < (g + 1) * wide), group, packed)
+    talk_ref[talk_ref.shape[0] - 16 :, :] = packed
     if fast:
-        last = pltpu.roll(last, lax.axis_index(axes[2]) * slots, axis=1)
+        parts = jnp.where(lane < slots, own_ref[0:16, :], own_ref[16:32, :])
+        self_ref[...] = parts
+        talk_ref[0:16, :] = jnp.where(lane & 8 == 0, pltpu.roll(parts, 120, axis=1), pltpu.roll(parts, 8, axis=1))
     else:
-        talk_ref[0:24, :slots] = own_ref[:, :slots]
-    talk_ref[:, talk_ref.shape[1] - 128 :] = last
+        self_ref[...] = jnp.zeros_like(self_ref)
 
 
 def local(
@@ -322,17 +325,15 @@
 
     keep = 1.0 + ends(a) + ends(b) + ends(c)
     lane = iota((nodes, cz), 1)
-    count = comps * nodes // 24
+    count = comps * nodes // 16
     wide = 2 * blocks
     plain = plain_matrix(offset_ref[...])
     hot_ref[...] = one_hot(jnp.concatenate([target_ref[...]] * 2, axis=1), blocks * cz)
 
     def ends_of(ref):
-        last = ref[:, ref.shape[1] - 128 :]
-        if fast:
-            last = pltpu.roll(last, (lax.axis_index(axes[2]) + 1) % 2 * slots, axis=1)
-        config = pltpu.roll(last[24:32], wide, axis=1)
-        groups = [pltpu.roll(last[0:24], (count - g) * wide, axis=1) for g in range(count)]
+        packed = ref[ref.shape[0] - 16 :, :]
+        config = pltpu.roll(packed, (128 - count * wide) % 128, axis=1)
+        groups = [pltpu.roll(packed, (128 - g * wide) % 128, axis=1) for g in range(count)]
         rows = jnp.concatenate(groups, axis=0)
         raw = rows[:nodes]
         spread_config = config[0:1]
@@ -406,16 +407,17 @@
 
 def gather_parts(refs, axes):
     me_y, me_s = lax.axis_index(axes[1]), lax.axis_index(axes[2])
-    me = me_y * 2 + me_s
-    lane = iota((24, 128), 1) >> 3
-    parts = jnp.zeros((24, 128), F32)
-    for flip, ref in enumerate(refs):
-        block = ref[0:24, :]
-        for half in range(2):
-            source = (me_y ^ flip) * 2 + half
-            shift = (source - me) * 8 + (128 - 64 * half)
-            parts = jnp.where(lane == source, pltpu.roll(block, shift & 127, axis=1), parts)
-    return parts + pltpu.roll(parts, 64, axis=1)
+    lane = iota((16, 128), 1)
+    parts = jnp.zeros((16, 128), F32)
+    for bits, ref in enumerate(refs):
+        block = ref[0:16, :]
+        for side in range(2):
+            place = me_y * 2 + (me_s ^ side)
+            source = (me_y ^ bits) * 2 + (me_s ^ side)
+            moved = pltpu.roll(block, ((source - place) * 8) & 127, axis=1)
+            parts = jnp.where((lane & 63) >> 3 == source, moved, parts)
+    other = pltpu.roll(parts, 64, axis=1)
+    return jnp.concatenate([jnp.where(lane < 64, parts, other), jnp.where(lane < 64, other, parts)], axis=0)
 
 
 def rim(
@@ -426,7 +428,7 @@
     comps, nodes, cx, cy, cz, nconf, slots, lanes = dims
     face = nodes // 4
     even_y, open_y = place(axes[1], sizes[1])
-    first = 24 if fast else 0
+    first = 16 if fast else 0
     b = (iota((nodes, cz), 0) >> 2) & 3
     matrix = matrix_ref[...]
     for k in range(comps):
@@ -462,10 +464,10 @@
     rim_ref, hot_ref, weight_ref, own_ref, out_hbm, deform_hbm, out_ref, deform_ref, sems = refs
 
     parts = gather_parts(part_refs, axes) if fast else part_refs[0][...]
-    own = [own_ref[i : i + 1, :] for i in range(24)]
-    got = [parts[i : i + 1, :] for i in range(24)]
-    _, stress, drag = solid(own[0:3], own[3:12], got[12:21], got[21:24])
-    moved, _, _ = solid(got[0:3], got[3:12], own[12:21], own[21:24])
+    own = [own_ref[i : i + 1, :] for i in range(32)]
+    got = [parts[i : i + 1, :] for i in range(32)]
+    _, stress, drag = solid(own[0:3], own[3:12], got[16:25], got[25:28])
+    moved, _, _ = solid(got[0:3], got[3:12], own[16:25], own[25:28])
     for i in range(9):
         deform_ref[i] = moved[i][:, :slots]
     copies = [pltpu.make_async_copy(deform_ref, deform_hbm, sems.at[comps])]
@@ -531,7 +533,6 @@
     n_dx, n_dy, n_solid = mesh_sizes
     face_rows = comps * nodes // 4
     lanes = 2 * slots
-    talk_lanes = lanes if comps * nodes // 24 * 2 * blocks <= slots == 64 else slots + 128
     dims = (comps, nodes, cx, cy, cz, nconf, slots, lanes)
 
     v = velocity.reshape(comps * nodes * blocks, cz)
@@ -555,12 +556,13 @@
     def estimate(columns):
         return pl.CostEstimate(flops=2 * 6 * nconf * nodes * nodes * columns, bytes_accessed=1_000_000, transcendentals=0)
 
-    fast = (n_dx, n_dy, n_solid, slots, talk_lanes) == (4, 4, 2, 64, 128)
-    talk, own, parted, matrix, targets, weights, config, offsets, visc = pl.pallas_call(
+    fast = (n_dx, n_dy, n_solid, slots) == (4, 4, 2, 64)
+    talk, mine, own, parted, matrix, targets, weights, config, offsets, visc = pl.pallas_call(
         functools.partial(begin, dims, axes, fast),
         out_shape=(
-            shape(32, talk_lanes),
-            shape(24, lanes),
+            shape(32 if fast else 16, 128),
+            shape(16, 128),
+            shape(32, lanes),
             shape(2 * comps * nodes, cells, dtype=BF16),
             shape(nconf * nodes, 3 * nodes, dtype=BF16),
             shape(1, lanes, dtype=targets.dtype),
@@ -570,7 +572,7 @@
             shape(*visc.shape),
         ),
         in_specs=[hbm] * 8,
-        out_specs=(vmem,) * 9,
+        out_specs=(vmem,) * 10,
         scratch_shapes=[
             pltpu.VMEM(v.shape, F32),
             pltpu.VMEM(targets.shape, targets.dtype),
@@ -598,8 +600,8 @@
         got_s = swap(talk, "solid", 0)
         got_xa = swap(xa, "dx", 0)
         got_xb = flip(xb, "dx", 3)
-        mine = (iota((24, 128), 1) >= 64) == (lax.axis_index("solid") == 1)
-        pair = jnp.where(mine, talk[:24], got_s[:24])
+        own_side = (iota((16, 128), 1) >> 3) & 1 == lax.axis_index("solid")
+        pair = jnp.where(own_side, mine, got_s[:16])
         got_3 = flip(jnp.concatenate([pair, yb], axis=0), "dy", 3)
         got_2 = flip(jnp.concatenate([pair, yb[:8]], axis=0), "dy", 2)
         got_1 = flip(jnp.concatenate([pair, ya], axis=0), "dy", 1)
@@ -610,7 +612,9 @@
         got_xa, got_xb = swap(xa, "dx", 0), swap(xb, "dx", 1)
         got_ya, got_yb = swap(ya, "dy", 0), swap(yb, "dy", 1)
         got_za, got_zb = swap(talk, "solid", 0), swap(talk, "solid", 1)
-        got_parts = lax.all_to_all(talk[:24, :slots], ("dy", "solid"), split_axis=1, concat_axis=1, tiled=True)
+        sent = jnp.concatenate([own[:12, :slots], own[16:28, :slots]], axis=0)
+        got_parts = lax.all_to_all(sent, ("dy", "solid"), split_axis=1, concat_axis=1, tiled=True)
+        got_parts = jnp.pad(got_parts.reshape(2, 12, slots), ((0, 0), (0, 4), (0, 0))).reshape(32, slots)
         parts = [jnp.concatenate([got_parts] * 2, axis=1)]
 
     total, hot = pl.pallas_call(

time: 17.4 us -> 17.3 us (level)
  no operation moved by 1% of the time
where the time goes in v7:
time: 17.3 us; the launch traced here: 17.2 us
  starting transfers between devices  9.16 us (53%)
  Pallas kernels  4.99 us (29%)
  waiting for transfers between devices  2.31 us (13%)
  between operations  0.69 us (4%)
    ppermute x4, starting transfers between devices, flip(): lax.ppermute(x, axis, [(i, i ^ bits) for i in range(lax.axis_size(axis))])  6.06 us
    ppermute x2, starting transfers between devices, swap(): return lax.ppermute(x, axis, pairs + [(j, i) for i, j in pairs])  3.1 us
    ppermute x4, waiting for transfers between devices, flip(): lax.ppermute(x, axis, [(i, i ^ bits) for i in range(lax.axis_size(axis))])  2.3 us
    pallas_call x1, Pallas kernels, shards(): pl.pallas_call(functools.partial(begin, dims, axes, fast), out_shape=(sha...  1.73 us
    pallas_call x1, Pallas kernels, shards(): pl.pallas_call(functools.partial(middle, dims, axes, mesh_sizes, fast), o...  1.11 us
    pallas_call x1, Pallas kernels, shards(): pl.pallas_call(functools.partial(after, dims, axes, fast), out_shape=(sha...  1.1 us
    pallas_call x1, Pallas kernels, shards(): pl.pallas_call(functools.partial(local, dims, axes), out_shape=(shape(2 *...  0.67 us
    pallas_call x1, Pallas kernels, shards(): pl.pallas_call(functools.partial(rim, dims, axes, mesh_sizes, fast), out_...  0.38 us
  transfers between devices with their start and end apart: 6, of which 3 were waited for; matrix products, arithmetic and copies ran while one was open for 0% of the time, Pallas kernels for 13%

profile of v7, /device:TPU:0, one launch (start us, length us, event | category | flops | bytes accessed | tf_op | source)
XLA Modules:
  0.0 17.2 jit_solution(9154802471111871598)
XLA Ops:
  0.6 1.7 %begin.1 = (f32[32,128]{1,0:T(8,128)S(1)}, f32[16,128]{1,0:T(8,128)S(1)}, f32[32,128]{1,0:T(8,128)S(1)}, bf16[384,512]{1,0:T(8,128)(2,1)S(1)}, bf16[512,192]{1,0...) custom-call(f32[768,128]{1,0:T(8,128)} %bitcast.14, ...), custom_call_target="tpu_custom_call" | custom-call | tf_op jit(solution)/shard_map/begin/pallas_call | solution.py:560
  2.4 3.0 %collective-permute-start = (f32[32,128]{1,0:T(8,128)S(1)}, f32[32,128]{1,0:T(8,128)S(1)}, u32[]{:S(2)}, u32[]{:S(2)}) collective-permute-start(f32[32,128]{1,0:T(8,128)S(1)} %get-tuple-element.21), channel_id=1, source_target_pairs={{0,1},{1,0},{2,3},{3,2},{4,5},{5,4},{6,7},{7,6},{8,9},{9,8},{10,11... | collective-permute-start | bytes 49160 | tf_op jit(solution)/shard_map/ppermute | solution.py:509
  5.4 0.7 %local.1 = (bf16[384,512]{1,0:T(8,128)(2,1)S(1)}, f32[48,512]{1,0:T(8,128)S(1)}, f32[48,512]{1,0:T(8,128)S(1)}, f32[48,128]{1,0:T(8,128)S(1)}, f32[48,128]{1,0:T(8,128)S(1)}) custom-call(bf16[384,512]{1,0:T(8,128)(2,1)S(1)} %get-tuple-element.22.split_ref, f32[512,64]{1,0:T(8,128)S(1)} %get-tuple-element.23.offset_ref, s32[4,128]{1,0:T(4,128)S(1)} %get-tuple-element.24.config_ref), custom_call_target="tpu_custom_call" | custom-call | flops 603979776 | bytes 1000000 | tf_op jit(solution)/shard_map/local/pallas_call | solution.py:588
  6.1 0.1 collective-permute-start.1
  6.2 1.6 %collective-permute-start.2 = (f32[48,512]{1,0:T(8,128)S(1)}, f32[48,512]{1,0:T(8,128)S(1)}, u32[]{:S(2)}, u32[]{:S(2)}) collective-permute-start(f32[48,512]{1,0:T(8,128)S(1)} %get-tuple-element.29), channel_id=1, source_target_pairs={{0,24},{8,16},{16,8},{24,0},{1,25},{9,17},{17,9},{25,1},{2,26},{10... | collective-permute-start | bytes 294920 | tf_op jit(solution)/shard_map/ppermute | solution.py:513
  7.8 0.0 collective-permute-done.za_ref.zb_ref
  7.8 3.7 %collective-permute-start.3 = (f32[64,128]{1,0:T(8,128)S(1)}, f32[64,128]{1,0:T(8,128)S(1)}, u32[]{:S(2)}, u32[]{:S(2)}) collective-permute-start(f32[64,128]{1,0:T(8,128)S(1)} %get-tuple-element.43), channel_id=1, source_target_pairs={{0,6},{2,4},{4,2},{6,0},{1,7},{3,5},{5,3},{7,1},{8,14},{10,12},{12... | collective-permute-start | bytes 98312 | tf_op jit(solution)/shard_map/ppermute | solution.py:513
  11.5 0.0 collective-permute-start.4
  11.5 0.8 %collective-permute-start.5 = (f32[64,128]{1,0:T(8,128)S(1)}, f32[64,128]{1,0:T(8,128)S(1)}, u32[]{:S(2)}, u32[]{:S(2)}) collective-permute-start(f32[64,128]{1,0:T(8,128)S(1)} %get-tuple-element.42), channel_id=1, source_target_pairs={{0,2},{2,0},{4,6},{6,4},{1,3},{3,1},{5,7},{7,5},{8,10},{10,8},{12,... | collective-permute-start | bytes 98312 | tf_op jit(solution)/shard_map/ppermute | solution.py:513
  12.3 0.0 collective-permute-done.1.xa_ref
  12.3 0.0 collective-permute-done.2.xb_ref
  12.3 1.1 %middle.1 = (f32[192,512]{1,0:T(8,128)S(1)}, bf16[512,256]{1,0:T(8,128)(2,1)S(1)}) custom-call(f32[32,128]{1,0:T(8,128)S(1)} %collective-permute-done.za_ref.zb_ref, bf16[384,512]{1,0:T(8,128)(2,1)S(1)} %get-tuple-element.25.con_ref, f32[4,128]{1,0:T(4,128)S(1)} %get-tuple-element.26.viscosity_ref, f32[512,64]{1,0:T(8,128)S(1)} %get-tuple-element.23.offset_ref, ...), custom_call_target="tpu_custom_call" | custom-call | flops 603979776 | bytes 1000000 | tf_op jit(solution)/shard_map/middle/pallas_call | solution.py:620
  13.4 0.2 %collective-permute-done.3.yb_ref.refs_0_ = f32[64,128]{1,0:T(8,128)S(1)} collective-permute-done((f32[64,128]{1,0:T(8,128)S(1)}, f32[64,128]{1,0:T(8,128)S(1)}, u32[]{:S(2)}, u32[]{:S(2)}) %collective-permute-start.3) | collective-permute-done | bytes 32800 | tf_op jit(solution)/shard_map/ppermute | solution.py:513
  13.6 1.8 %collective-permute-done.5.ya_ref.refs_2_ = f32[64,128]{1,0:T(8,128)S(1)} collective-permute-done((f32[64,128]{1,0:T(8,128)S(1)}, f32[64,128]{1,0:T(8,128)S(1)}, u32[]{:S(2)}, u32[]{:S(2)}) %collective-permute-start.5) | collective-permute-done | bytes 32800 | tf_op jit(solution)/shard_map/ppermute | solution.py:513
  15.4 0.4 %rim.1.refs_4_ = f32[192,256]{1,0:T(8,128)S(1)} custom-call(f32[192,512]{1,0:T(8,128)S(1)} %get-tuple-element.31.total_ref, f32[64,128]{1,0:T(8,128)S(1)} %collective-permute-done.3.yb_ref.refs_0_, f32[64,128]{1,0:T(8,128)S(1)} %collective-permute-done.5.ya_ref.refs_2_, bf16[512,192]{1,0:T(8,128)(2,1)S(1)} %get-tuple-element.27.matrix_ref, ...), custom_call_target="tpu_custom_call" | custom-call | flops 603979776 | bytes 1000000 | tf_op jit(solution)/shard_map/rim/pallas_call | solution.py:630
  15.8 0.3 %collective-permute-done.4.refs_1_ = f32[24,128]{1,0:T(8,128)S(1)} collective-permute-done((f32[24,128]{1,0:T(8,128)S(1)}, f32[24,128]{1,0:T(8,128)S(1)}, u32[]{:S(2)}, u32[]{:S(2)}) %collective-permute-start.4) | collective-permute-done | bytes 12320 | tf_op jit(solution)/shard_map/ppermute | solution.py:513
  16.1 1.1 %after.1 = (f32[768,128]{1,0:T(8,128)}, f32[9,1,64]{2,1,0:T(1,128)}) custom-call(f32[192,512]{1,0:T(8,128)S(1)} %get-tuple-element.31.total_ref, f32[64,128]{1,0:T(8,128)S(1)} %collective-permute-done.3.yb_ref.refs_0_, f32[24,128]{1,0:T(8,128)S(1)} %collective-permute-done.4.refs_1_, f32[64,128]{1,0:T(8,128)S(1)} %collective-permute-done.5.ya_ref.refs_2_, ...), custom_call_target="tpu_custom_call" | custom-call | tf_op jit(solution)/shard_map/after/pallas_call | solution.py:640
  (5 shorter events, 0.0 us)
Async XLA Ops:
  2.4 5.4 %collective-permute-start = (f32[32,128]{1,0:T(8,128)S(1)}, f32[32,128]{1,0:T(8,128)S(1)}, u32[]{:S(2)}, u32[]{:S(2)}) collective-permute-start(f32[32,128]{1,0:T(8,128)S(1)} %get-tuple-element.21), channel_id=1, source_target_pairs={{0,1},{1,0},{2,3},{3,2},{4,5},{5,4},{6,7},{7,6},{8,9},{9,8},{10,11... | collective-permute-start | bytes 49160 | tf_op jit(solution)/shard_map/ppermute | solution.py:509
  6.1 6.2 %collective-permute-start.1 = (f32[48,512]{1,0:T(8,128)S(1)}, f32[48,512]{1,0:T(8,128)S(1)}, u32[]{:S(2)}, u32[]{:S(2)}) collective-permute-start(f32[48,512]{1,0:T(8,128)S(1)} %get-tuple-element.28), channel_id=1, source_target_pairs={{0,8},{16,24},{8,0},{24,16},{1,9},{17,25},{9,1},{25,17},{2,10},{18... | collective-permute-start | bytes 294920 | tf_op jit(solution)/shard_map/ppermute | solution.py:509
  6.2 6.1 %collective-permute-start.2 = (f32[48,512]{1,0:T(8,128)S(1)}, f32[48,512]{1,0:T(8,128)S(1)}, u32[]{:S(2)}, u32[]{:S(2)}) collective-permute-start(f32[48,512]{1,0:T(8,128)S(1)} %get-tuple-element.29), channel_id=1, source_target_pairs={{0,24},{8,16},{16,8},{24,0},{1,25},{9,17},{17,9},{25,1},{2,26},{10... | collective-permute-start | bytes 294920 | tf_op jit(solution)/shard_map/ppermute | solution.py:513
  7.8 5.8 %collective-permute-start.3 = (f32[64,128]{1,0:T(8,128)S(1)}, f32[64,128]{1,0:T(8,128)S(1)}, u32[]{:S(2)}, u32[]{:S(2)}) collective-permute-start(f32[64,128]{1,0:T(8,128)S(1)} %get-tuple-element.43), channel_id=1, source_target_pairs={{0,6},{2,4},{4,2},{6,0},{1,7},{3,5},{5,3},{7,1},{8,14},{10,12},{12... | collective-permute-start | bytes 98312 | tf_op jit(solution)/shard_map/ppermute | solution.py:513
  11.5 4.6 %collective-permute-start.4 = (f32[24,128]{1,0:T(8,128)S(1)}, f32[24,128]{1,0:T(8,128)S(1)}, u32[]{:S(2)}, u32[]{:S(2)}) collective-permute-start(f32[24,128]{1,0:T(8,128)S(1)} %pad_maximum_fusion.2), channel_id=1, source_target_pairs={{0,4},{2,6},{4,0},{6,2},{1,5},{3,7},{5,1},{7,3},{8,12},{10,14},{12... | collective-permute-start | bytes 36872 | tf_op jit(solution)/shard_map/ppermute | solution.py:513
  11.5 3.9 %collective-permute-start.5 = (f32[64,128]{1,0:T(8,128)S(1)}, f32[64,128]{1,0:T(8,128)S(1)}, u32[]{:S(2)}, u32[]{:S(2)}) collective-permute-start(f32[64,128]{1,0:T(8,128)S(1)} %get-tuple-element.42), channel_id=1, source_target_pairs={{0,2},{2,0},{4,6},{6,4},{1,3},{3,1},{5,7},{7,5},{8,10},{10,8},{12,... | collective-permute-start | bytes 98312 | tf_op jit(solution)/shard_map/ppermute | solution.py:513

commit v8 on v7

--- a/solution.py
+++ b/solution.py
@@ -411,6 +411,8 @@
     parts = jnp.zeros((16, 128), F32)
     for bits, ref in enumerate(refs):
         block = ref[0:16, :]
+        if bits == 2:
+            block = jnp.concatenate([block[8:], block[:8]], axis=0)
         for side in range(2):
             place = me_y * 2 + (me_s ^ side)
             source = (me_y ^ bits) * 2 + (me_s ^ side)
@@ -603,7 +605,7 @@
         own_side = (iota((16, 128), 1) >> 3) & 1 == lax.axis_index("solid")
         pair = jnp.where(own_side, mine, got_s[:16])
         got_3 = flip(jnp.concatenate([pair, yb], axis=0), "dy", 3)
-        got_2 = flip(jnp.concatenate([pair, yb[:8]], axis=0), "dy", 2)
+        got_2 = flip(jnp.concatenate([pair[8:], pair[:8]], axis=0), "dy", 2)
         got_1 = flip(jnp.concatenate([pair, ya], axis=0), "dy", 1)
         parts = [got_3, got_2, got_1, pair]
         got_ya, got_yb = got_1, got_3

time: 17.3 us -> 17.3 us (level)
  no operation moved by 1% of the time
where the time goes in v8:
time: 17.3 us; the launch traced here: 17.1 us
  starting transfers between devices  9.16 us (53%)
  Pallas kernels  4.99 us (29%)
  waiting for transfers between devices  2.26 us (13%)
  between operations  0.69 us (4%)
    ppermute x4, starting transfers between devices, flip(): lax.ppermute(x, axis, [(i, i ^ bits) for i in range(lax.axis_size(axis))])  6.06 us
    ppermute x2, starting transfers between devices, swap(): return lax.ppermute(x, axis, pairs + [(j, i) for i, j in pairs])  3.1 us
    ppermute x4, waiting for transfers between devices, flip(): lax.ppermute(x, axis, [(i, i ^ bits) for i in range(lax.axis_size(axis))])  2.26 us
    pallas_call x1, Pallas kernels, shards(): pl.pallas_call(functools.partial(begin, dims, axes, fast), out_shape=(sha...  1.73 us
    pallas_call x1, Pallas kernels, shards(): pl.pallas_call(functools.partial(middle, dims, axes, mesh_sizes, fast), o...  1.11 us
    pallas_call x1, Pallas kernels, shards(): pl.pallas_call(functools.partial(after, dims, axes, fast), out_shape=(sha...  1.1 us
    pallas_call x1, Pallas kernels, shards(): pl.pallas_call(functools.partial(local, dims, axes), out_shape=(shape(2 *...  0.67 us
    pallas_call x1, Pallas kernels, shards(): pl.pallas_call(functools.partial(rim, dims, axes, mesh_sizes, fast), out_...  0.38 us
  transfers between devices with their start and end apart: 6, of which 3 were waited for; matrix products, arithmetic and copies ran while one was open for 0% of the time, Pallas kernels for 13%

profile of v8, /device:TPU:0, one launch (start us, length us, event | category | flops | bytes accessed | tf_op | source)
XLA Modules:
  0.0 17.1 jit_solution(15551715594125876732)
XLA Ops:
  0.6 1.7 %begin.1 = (f32[32,128]{1,0:T(8,128)S(1)}, f32[16,128]{1,0:T(8,128)S(1)}, f32[32,128]{1,0:T(8,128)S(1)}, bf16[384,512]{1,0:T(8,128)(2,1)S(1)}, bf16[512,192]{1,0...) custom-call(f32[768,128]{1,0:T(8,128)} %bitcast.14, ...), custom_call_target="tpu_custom_call" | custom-call | tf_op jit(solution)/shard_map/begin/pallas_call | solution.py:562
  2.4 3.0 %collective-permute-start = (f32[32,128]{1,0:T(8,128)S(1)}, f32[32,128]{1,0:T(8,128)S(1)}, u32[]{:S(2)}, u32[]{:S(2)}) collective-permute-start(f32[32,128]{1,0:T(8,128)S(1)} %get-tuple-element.21), channel_id=1, source_target_pairs={{0,1},{1,0},{2,3},{3,2},{4,5},{5,4},{6,7},{7,6},{8,9},{9,8},{10,11... | collective-permute-start | bytes 49160 | tf_op jit(solution)/shard_map/ppermute | solution.py:511
  5.4 0.7 %local.1 = (bf16[384,512]{1,0:T(8,128)(2,1)S(1)}, f32[48,512]{1,0:T(8,128)S(1)}, f32[48,512]{1,0:T(8,128)S(1)}, f32[48,128]{1,0:T(8,128)S(1)}, f32[48,128]{1,0:T(8,128)S(1)}) custom-call(bf16[384,512]{1,0:T(8,128)(2,1)S(1)} %get-tuple-element.22.split_ref, f32[512,64]{1,0:T(8,128)S(1)} %get-tuple-element.23.offset_ref, s32[4,128]{1,0:T(4,128)S(1)} %get-tuple-element.24.config_ref), custom_call_target="tpu_custom_call" | custom-call | flops 603979776 | bytes 1000000 | tf_op jit(solution)/shard_map/local/pallas_call | solution.py:590
  6.1 0.1 collective-permute-start.1
  6.2 1.6 %collective-permute-start.2 = (f32[48,512]{1,0:T(8,128)S(1)}, f32[48,512]{1,0:T(8,128)S(1)}, u32[]{:S(2)}, u32[]{:S(2)}) collective-permute-start(f32[48,512]{1,0:T(8,128)S(1)} %get-tuple-element.29), channel_id=1, source_target_pairs={{0,24},{8,16},{16,8},{24,0},{1,25},{9,17},{17,9},{25,1},{2,26},{10... | collective-permute-start | bytes 294920 | tf_op jit(solution)/shard_map/ppermute | solution.py:515
  7.8 0.0 collective-permute-done.za_ref.zb_ref
  7.8 3.7 %collective-permute-start.3 = (f32[64,128]{1,0:T(8,128)S(1)}, f32[64,128]{1,0:T(8,128)S(1)}, u32[]{:S(2)}, u32[]{:S(2)}) collective-permute-start(f32[64,128]{1,0:T(8,128)S(1)} %get-tuple-element.43), channel_id=1, source_target_pairs={{0,6},{2,4},{4,2},{6,0},{1,7},{3,5},{5,3},{7,1},{8,14},{10,12},{12... | collective-permute-start | bytes 98312 | tf_op jit(solution)/shard_map/ppermute | solution.py:515
  11.5 0.0 collective-permute-start.4
  11.5 0.8 %collective-permute-start.5 = (f32[64,128]{1,0:T(8,128)S(1)}, f32[64,128]{1,0:T(8,128)S(1)}, u32[]{:S(2)}, u32[]{:S(2)}) collective-permute-start(f32[64,128]{1,0:T(8,128)S(1)} %get-tuple-element.42), channel_id=1, source_target_pairs={{0,2},{2,0},{4,6},{6,4},{1,3},{3,1},{5,7},{7,5},{8,10},{10,8},{12,... | collective-permute-start | bytes 98312 | tf_op jit(solution)/shard_map/ppermute | solution.py:515
  12.3 0.0 collective-permute-done.1.xa_ref
  12.3 0.0 collective-permute-done.2.xb_ref
  12.3 1.1 %middle.1 = (f32[192,512]{1,0:T(8,128)S(1)}, bf16[512,256]{1,0:T(8,128)(2,1)S(1)}) custom-call(f32[32,128]{1,0:T(8,128)S(1)} %collective-permute-done.za_ref.zb_ref, bf16[384,512]{1,0:T(8,128)(2,1)S(1)} %get-tuple-element.25.con_ref, f32[4,128]{1,0:T(4,128)S(1)} %get-tuple-element.26.viscosity_ref, f32[512,64]{1,0:T(8,128)S(1)} %get-tuple-element.23.offset_ref, ...), custom_call_target="tpu_custom_call" | custom-call | flops 603979776 | bytes 1000000 | tf_op jit(solution)/shard_map/middle/pallas_call | solution.py:622
  13.4 0.2 %collective-permute-done.3.yb_ref.refs_0_ = f32[64,128]{1,0:T(8,128)S(1)} collective-permute-done((f32[64,128]{1,0:T(8,128)S(1)}, f32[64,128]{1,0:T(8,128)S(1)}, u32[]{:S(2)}, u32[]{:S(2)}) %collective-permute-start.3) | collective-permute-done | bytes 32800 | tf_op jit(solution)/shard_map/ppermute | solution.py:515
  13.6 1.8 %collective-permute-done.5.ya_ref.refs_2_ = f32[64,128]{1,0:T(8,128)S(1)} collective-permute-done((f32[64,128]{1,0:T(8,128)S(1)}, f32[64,128]{1,0:T(8,128)S(1)}, u32[]{:S(2)}, u32[]{:S(2)}) %collective-permute-start.5) | collective-permute-done | bytes 32800 | tf_op jit(solution)/shard_map/ppermute | solution.py:515
  15.4 0.4 %rim.1.refs_4_ = f32[192,256]{1,0:T(8,128)S(1)} custom-call(f32[192,512]{1,0:T(8,128)S(1)} %get-tuple-element.31.total_ref, f32[64,128]{1,0:T(8,128)S(1)} %collective-permute-done.3.yb_ref.refs_0_, f32[64,128]{1,0:T(8,128)S(1)} %collective-permute-done.5.ya_ref.refs_2_, bf16[512,192]{1,0:T(8,128)(2,1)S(1)} %get-tuple-element.27.matrix_ref, ...), custom_call_target="tpu_custom_call" | custom-call | flops 603979776 | bytes 1000000 | tf_op jit(solution)/shard_map/rim/pallas_call | solution.py:632
  15.8 0.2 %collective-permute-done.4.refs_1_ = f32[16,128]{1,0:T(8,128)S(1)} collective-permute-done((f32[16,128]{1,0:T(8,128)S(1)}, f32[16,128]{1,0:T(8,128)S(1)}, u32[]{:S(2)}, u32[]{:S(2)}) %collective-permute-start.4) | collective-permute-done | bytes 8224 | tf_op jit(solution)/shard_map/ppermute | solution.py:515
  16.0 1.1 %after.1 = (f32[768,128]{1,0:T(8,128)}, f32[9,1,64]{2,1,0:T(1,128)}) custom-call(f32[192,512]{1,0:T(8,128)S(1)} %get-tuple-element.31.total_ref, f32[64,128]{1,0:T(8,128)S(1)} %collective-permute-done.3.yb_ref.refs_0_, f32[16,128]{1,0:T(8,128)S(1)} %collective-permute-done.4.refs_1_, f32[64,128]{1,0:T(8,128)S(1)} %collective-permute-done.5.ya_ref.refs_2_, ...), custom_call_target="tpu_custom_call" | custom-call | tf_op jit(solution)/shard_map/after/pallas_call | solution.py:642
  (5 shorter events, 0.0 us)
Async XLA Ops:
  2.4 5.4 %collective-permute-start = (f32[32,128]{1,0:T(8,128)S(1)}, f32[32,128]{1,0:T(8,128)S(1)}, u32[]{:S(2)}, u32[]{:S(2)}) collective-permute-start(f32[32,128]{1,0:T(8,128)S(1)} %get-tuple-element.21), channel_id=1, source_target_pairs={{0,1},{1,0},{2,3},{3,2},{4,5},{5,4},{6,7},{7,6},{8,9},{9,8},{10,11... | collective-permute-start | bytes 49160 | tf_op jit(solution)/shard_map/ppermute | solution.py:511
  6.1 6.2 %collective-permute-start.1 = (f32[48,512]{1,0:T(8,128)S(1)}, f32[48,512]{1,0:T(8,128)S(1)}, u32[]{:S(2)}, u32[]{:S(2)}) collective-permute-start(f32[48,512]{1,0:T(8,128)S(1)} %get-tuple-element.28), channel_id=1, source_target_pairs={{0,8},{16,24},{8,0},{24,16},{1,9},{17,25},{9,1},{25,17},{2,10},{18... | collective-permute-start | bytes 294920 | tf_op jit(solution)/shard_map/ppermute | solution.py:511
  6.2 6.1 %collective-permute-start.2 = (f32[48,512]{1,0:T(8,128)S(1)}, f32[48,512]{1,0:T(8,128)S(1)}, u32[]{:S(2)}, u32[]{:S(2)}) collective-permute-start(f32[48,512]{1,0:T(8,128)S(1)} %get-tuple-element.29), channel_id=1, source_target_pairs={{0,24},{8,16},{16,8},{24,0},{1,25},{9,17},{17,9},{25,1},{2,26},{10... | collective-permute-start | bytes 294920 | tf_op jit(solution)/shard_map/ppermute | solution.py:515
  7.8 5.8 %collective-permute-start.3 = (f32[64,128]{1,0:T(8,128)S(1)}, f32[64,128]{1,0:T(8,128)S(1)}, u32[]{:S(2)}, u32[]{:S(2)}) collective-permute-start(f32[64,128]{1,0:T(8,128)S(1)} %get-tuple-element.43), channel_id=1, source_target_pairs={{0,6},{2,4},{4,2},{6,0},{1,7},{3,5},{5,3},{7,1},{8,14},{10,12},{12... | collective-permute-start | bytes 98312 | tf_op jit(solution)/shard_map/ppermute | solution.py:515
  11.5 4.5 %collective-permute-start.4 = (f32[16,128]{1,0:T(8,128)S(1)}, f32[16,128]{1,0:T(8,128)S(1)}, u32[]{:S(2)}, u32[]{:S(2)}) collective-permute-start(f32[16,128]{1,0:T(8,128)S(1)} %pad_maximum_fusion.2), channel_id=1, source_target_pairs={{0,4},{2,6},{4,0},{6,2},{1,5},{3,7},{5,1},{7,3},{8,12},{10,14},{12... | collective-permute-start | bytes 24584 | tf_op jit(solution)/shard_map/ppermute | solution.py:515
  11.5 3.9 %collective-permute-start.5 = (f32[64,128]{1,0:T(8,128)S(1)}, f32[64,128]{1,0:T(8,128)S(1)}, u32[]{:S(2)}, u32[]{:S(2)}) collective-permute-start(f32[64,128]{1,0:T(8,128)S(1)} %get-tuple-element.42), channel_id=1, source_target_pairs={{0,2},{2,0},{4,6},{6,4},{1,3},{3,1},{5,7},{7,5},{8,10},{10,8},{12,... | collective-permute-start | bytes 98312 | tf_op jit(solution)/shard_map/ppermute | solution.py:515

commit v9 on v8

--- a/solution.py
+++ b/solution.py
@@ -127,18 +127,18 @@
     dims, axes, fast,
     v_hbm, config_hbm, offset_hbm, slot_hbm, xi_hbm, strain_hbm, motion_hbm, viscosity_hbm,
     talk_ref, self_ref, own_ref, split_ref, matrix_ref, target_ref, weight_ref, config_ref, offset_ref, viscosity_ref,
-    v_ref, slot_ref, xi_ref, strain_ref, motion_ref, sems,
+    v_ref, slot_ref, xi_ref, strain_ref, motion_ref, hot_ref, parts_ref, basis_ref, sems,
 ):
     comps, nodes, cx, cy, cz, nconf, slots, lanes = dims
     blocks = cx * cy
     cells = blocks * cz
     copies = fetch(
-        [(v_hbm, v_ref), (offset_hbm, offset_ref), (slot_hbm, slot_ref), (config_hbm, config_ref), (xi_hbm, xi_ref),
+        [(slot_hbm, slot_ref), (config_hbm, config_ref), (xi_hbm, xi_ref), (v_hbm, v_ref), (offset_hbm, offset_ref),
          (strain_hbm, strain_ref), (motion_hbm, motion_ref), (viscosity_hbm, viscosity_ref)],
         sems,
     )
 
-    for copy in copies:
+    for copy in copies[:3]:
         copy.wait()
     targets = jnp.concatenate([slot_ref[...]] * 2, axis=1)
     target_ref[...] = targets
@@ -150,6 +150,7 @@
         both = jnp.where(lane == columns - wide + y, y * cz, both)
         both = jnp.where(lane == columns - blocks + y, (y + 1) * cz - 1, both)
     hot = one_hot(both, cells)
+    hot_ref[...] = hot
     config = jnp.concatenate([config_ref[y : y + 1, :] for y in range(blocks)], axis=1)
     config = dot(jnp.broadcast_to(config.astype(F32), (16, cells)).astype(BF16), hot)[0:1, :]
 
@@ -164,6 +165,11 @@
     xi = [jnp.concatenate([xi_ref[j]] * 2, axis=1) for j in range(3)]
     (px, dx), (py, dy), (pz, dz) = shapes_of(xi, lanes)
     basis = (jnp.where(half, px, dx) * (py * pz), px * jnp.where(half, dy * pz, py * dz))
+    for j in range(2):
+        basis_ref[j * nodes : (j + 1) * nodes, :] = basis[j]
+        parts_ref[:, j * lanes : (j + 1) * lanes] = turned_parts(*split(basis[j]))
+    for copy in copies[3:]:
+        copy.wait()
     matrix = turned_matrix(offset_ref[...], nconf, nodes)
     matrix_ref[...] = matrix
     raw = []
@@ -174,12 +180,12 @@
             at = slice(y * cz, (y + 1) * cz)
             split_ref[row : row + nodes, at] = high
             split_ref[row + nodes : row + 2 * nodes, at] = low
-        both = dot(split_ref[row : row + 2 * nodes, :], hot)
+        both = dot(split_ref[row : row + 2 * nodes, :], hot_ref[...])
         raw.append(both[:nodes] + both[nodes:])
-    product = dot(matrix, jnp.concatenate([turned_parts(*split(p)) for p in basis], axis=1))
+    product = dot(matrix, parts_ref[...])
     weights = []
     for j in range(2):
-        weights.append(basis[j] + configured(product[:, j * lanes : (j + 1) * lanes], config_twice, nconf))
+        weights.append(basis_ref[j * nodes : (j + 1) * nodes, :] + configured(product[:, j * lanes : (j + 1) * lanes], config_twice, nconf))
         weight_ref[j * nodes : (j + 1) * nodes, :] = weights[j]
 
     for k in range(comps):
@@ -581,6 +587,9 @@
             pltpu.VMEM(xi.shape, F32),
             pltpu.VMEM(strain.shape, F32),
             pltpu.VMEM(motion.shape, F32),
+            pltpu.VMEM((cells, pl.cdiv(slots + 2 * blocks, 128) * 128), BF16),
+            pltpu.VMEM((3 * nodes, 2 * lanes), BF16),
+            pltpu.VMEM((2 * nodes, lanes), F32),
             pltpu.SemaphoreType.DMA((8,)),
         ],
         compiler_params=params,

time: 17.3 us -> 17.3 us (level)
  no operation moved by 1% of the time
where the time goes in v9:
time: 17.3 us; the launch traced here: 17.1 us
  starting transfers between devices  9.16 us (53%)
  Pallas kernels  4.97 us (29%)
  waiting for transfers between devices  2.27 us (13%)
  between operations  0.69 us (4%)
    ppermute x4, starting transfers between devices, flip(): lax.ppermute(x, axis, [(i, i ^ bits) for i in range(lax.axis_size(axis))])  6.06 us
    ppermute x2, starting transfers between devices, swap(): return lax.ppermute(x, axis, pairs + [(j, i) for i, j in pairs])  3.1 us
    ppermute x4, waiting for transfers between devices, flip(): lax.ppermute(x, axis, [(i, i ^ bits) for i in range(lax.axis_size(axis))])  2.26 us
    pallas_call x1, Pallas kernels, shards(): pl.pallas_call(functools.partial(begin, dims, axes, fast), out_shape=(sha...  1.71 us
    pallas_call x1, Pallas kernels, shards(): pl.pallas_call(functools.partial(middle, dims, axes, mesh_sizes, fast), o...  1.11 us
    pallas_call x1, Pallas kernels, shards(): pl.pallas_call(functools.partial(after, dims, axes, fast), out_shape=(sha...  1.1 us
    pallas_call x1, Pallas kernels, shards(): pl.pallas_call(functools.partial(local, dims, axes), out_shape=(shape(2 *...  0.67 us
    pallas_call x1, Pallas kernels, shards(): pl.pallas_call(functools.partial(rim, dims, axes, mesh_sizes, fast), out_...  0.37 us
  transfers between devices with their start and end apart: 6, of which 3 were waited for; matrix products, arithmetic and copies ran while one was open for 0% of the time, Pallas kernels for 13%

profile of v9, /device:TPU:0, one launch (start us, length us, event | category | flops | bytes accessed | tf_op | source)
XLA Modules:
  0.0 17.1 jit_solution(6020557868953669819)
XLA Ops:
  0.6 1.7 %begin.1 = (f32[32,128]{1,0:T(8,128)S(1)}, f32[16,128]{1,0:T(8,128)S(1)}, f32[32,128]{1,0:T(8,128)S(1)}, bf16[384,512]{1,0:T(8,128)(2,1)S(1)}, bf16[512,192]{1,0...) custom-call(f32[768,128]{1,0:T(8,128)} %bitcast.14, ...), custom_call_target="tpu_custom_call" | custom-call | tf_op jit(solution)/shard_map/begin/pallas_call | solution.py:568
  2.4 3.0 %collective-permute-start = (f32[32,128]{1,0:T(8,128)S(1)}, f32[32,128]{1,0:T(8,128)S(1)}, u32[]{:S(2)}, u32[]{:S(2)}) collective-permute-start(f32[32,128]{1,0:T(8,128)S(1)} %get-tuple-element.21), channel_id=1, source_target_pairs={{0,1},{1,0},{2,3},{3,2},{4,5},{5,4},{6,7},{7,6},{8,9},{9,8},{10,11... | collective-permute-start | bytes 49160 | tf_op jit(solution)/shard_map/ppermute | solution.py:517
  5.4 0.7 %local.1 = (bf16[384,512]{1,0:T(8,128)(2,1)S(1)}, f32[48,512]{1,0:T(8,128)S(1)}, f32[48,512]{1,0:T(8,128)S(1)}, f32[48,128]{1,0:T(8,128)S(1)}, f32[48,128]{1,0:T(8,128)S(1)}) custom-call(bf16[384,512]{1,0:T(8,128)(2,1)S(1)} %get-tuple-element.22.split_ref, f32[512,64]{1,0:T(8,128)S(1)} %get-tuple-element.23.offset_ref, s32[4,128]{1,0:T(4,128)S(1)} %get-tuple-element.24.config_ref), custom_call_target="tpu_custom_call" | custom-call | flops 603979776 | bytes 1000000 | tf_op jit(solution)/shard_map/local/pallas_call | solution.py:599
  6.1 0.1 collective-permute-start.1
  6.1 1.6 %collective-permute-start.2 = (f32[48,512]{1,0:T(8,128)S(1)}, f32[48,512]{1,0:T(8,128)S(1)}, u32[]{:S(2)}, u32[]{:S(2)}) collective-permute-start(f32[48,512]{1,0:T(8,128)S(1)} %get-tuple-element.29), channel_id=1, source_target_pairs={{0,24},{8,16},{16,8},{24,0},{1,25},{9,17},{17,9},{25,1},{2,26},{10... | collective-permute-start | bytes 294920 | tf_op jit(solution)/shard_map/ppermute | solution.py:521
  7.8 0.0 collective-permute-done.za_ref.zb_ref
  7.8 3.7 %collective-permute-start.3 = (f32[64,128]{1,0:T(8,128)S(1)}, f32[64,128]{1,0:T(8,128)S(1)}, u32[]{:S(2)}, u32[]{:S(2)}) collective-permute-start(f32[64,128]{1,0:T(8,128)S(1)} %get-tuple-element.43), channel_id=1, source_target_pairs={{0,6},{2,4},{4,2},{6,0},{1,7},{3,5},{5,3},{7,1},{8,14},{10,12},{12... | collective-permute-start | bytes 98312 | tf_op jit(solution)/shard_map/ppermute | solution.py:521
  11.5 0.0 collective-permute-start.4
  11.5 0.8 %collective-permute-start.5 = (f32[64,128]{1,0:T(8,128)S(1)}, f32[64,128]{1,0:T(8,128)S(1)}, u32[]{:S(2)}, u32[]{:S(2)}) collective-permute-start(f32[64,128]{1,0:T(8,128)S(1)} %get-tuple-element.42), channel_id=1, source_target_pairs={{0,2},{2,0},{4,6},{6,4},{1,3},{3,1},{5,7},{7,5},{8,10},{10,8},{12,... | collective-permute-start | bytes 98312 | tf_op jit(solution)/shard_map/ppermute | solution.py:521
  12.3 0.0 collective-permute-done.1.xa_ref
  12.3 0.0 collective-permute-done.2.xb_ref
  12.3 1.1 %middle.1 = (f32[192,512]{1,0:T(8,128)S(1)}, bf16[512,256]{1,0:T(8,128)(2,1)S(1)}) custom-call(f32[32,128]{1,0:T(8,128)S(1)} %collective-permute-done.za_ref.zb_ref, bf16[384,512]{1,0:T(8,128)(2,1)S(1)} %get-tuple-element.25.con_ref, f32[4,128]{1,0:T(4,128)S(1)} %get-tuple-element.26.viscosity_ref, f32[512,64]{1,0:T(8,128)S(1)} %get-tuple-element.23.offset_ref, ...), custom_call_target="tpu_custom_call" | custom-call | flops 603979776 | bytes 1000000 | tf_op jit(solution)/shard_map/middle/pallas_call | solution.py:631
  13.4 0.2 %collective-permute-done.3.yb_ref.refs_0_ = f32[64,128]{1,0:T(8,128)S(1)} collective-permute-done((f32[64,128]{1,0:T(8,128)S(1)}, f32[64,128]{1,0:T(8,128)S(1)}, u32[]{:S(2)}, u32[]{:S(2)}) %collective-permute-start.3) | collective-permute-done | bytes 32800 | tf_op jit(solution)/shard_map/ppermute | solution.py:521
  13.6 1.8 %collective-permute-done.5.ya_ref.refs_2_ = f32[64,128]{1,0:T(8,128)S(1)} collective-permute-done((f32[64,128]{1,0:T(8,128)S(1)}, f32[64,128]{1,0:T(8,128)S(1)}, u32[]{:S(2)}, u32[]{:S(2)}) %collective-permute-start.5) | collective-permute-done | bytes 32800 | tf_op jit(solution)/shard_map/ppermute | solution.py:521
  15.4 0.4 %rim.1.refs_4_ = f32[192,256]{1,0:T(8,128)S(1)} custom-call(f32[192,512]{1,0:T(8,128)S(1)} %get-tuple-element.31.total_ref, f32[64,128]{1,0:T(8,128)S(1)} %collective-permute-done.3.yb_ref.refs_0_, f32[64,128]{1,0:T(8,128)S(1)} %collective-permute-done.5.ya_ref.refs_2_, bf16[512,192]{1,0:T(8,128)(2,1)S(1)} %get-tuple-element.27.matrix_ref, ...), custom_call_target="tpu_custom_call" | custom-call | flops 603979776 | bytes 1000000 | tf_op jit(solution)/shard_map/rim/pallas_call | solution.py:641
  15.8 0.3 %collective-permute-done.4.refs_1_ = f32[16,128]{1,0:T(8,128)S(1)} collective-permute-done((f32[16,128]{1,0:T(8,128)S(1)}, f32[16,128]{1,0:T(8,128)S(1)}, u32[]{:S(2)}, u32[]{:S(2)}) %collective-permute-start.4) | collective-permute-done | bytes 8224 | tf_op jit(solution)/shard_map/ppermute | solution.py:521
  16.0 1.1 %after.1 = (f32[768,128]{1,0:T(8,128)}, f32[9,1,64]{2,1,0:T(1,128)}) custom-call(f32[192,512]{1,0:T(8,128)S(1)} %get-tuple-element.31.total_ref, f32[64,128]{1,0:T(8,128)S(1)} %collective-permute-done.3.yb_ref.refs_0_, f32[16,128]{1,0:T(8,128)S(1)} %collective-permute-done.4.refs_1_, f32[64,128]{1,0:T(8,128)S(1)} %collective-permute-done.5.ya_ref.refs_2_, ...), custom_call_target="tpu_custom_call" | custom-call | tf_op jit(solution)/shard_map/after/pallas_call | solution.py:651
  (5 shorter events, 0.0 us)
Async XLA Ops:
  2.4 5.4 %collective-permute-start = (f32[32,128]{1,0:T(8,128)S(1)}, f32[32,128]{1,0:T(8,128)S(1)}, u32[]{:S(2)}, u32[]{:S(2)}) collective-permute-start(f32[32,128]{1,0:T(8,128)S(1)} %get-tuple-element.21), channel_id=1, source_target_pairs={{0,1},{1,0},{2,3},{3,2},{4,5},{5,4},{6,7},{7,6},{8,9},{9,8},{10,11... | collective-permute-start | bytes 49160 | tf_op jit(solution)/shard_map/ppermute | solution.py:517
  6.1 6.2 %collective-permute-start.1 = (f32[48,512]{1,0:T(8,128)S(1)}, f32[48,512]{1,0:T(8,128)S(1)}, u32[]{:S(2)}, u32[]{:S(2)}) collective-permute-start(f32[48,512]{1,0:T(8,128)S(1)} %get-tuple-element.28), channel_id=1, source_target_pairs={{0,8},{16,24},{8,0},{24,16},{1,9},{17,25},{9,1},{25,17},{2,10},{18... | collective-permute-start | bytes 294920 | tf_op jit(solution)/shard_map/ppermute | solution.py:517
  6.1 6.1 %collective-permute-start.2 = (f32[48,512]{1,0:T(8,128)S(1)}, f32[48,512]{1,0:T(8,128)S(1)}, u32[]{:S(2)}, u32[]{:S(2)}) collective-permute-start(f32[48,512]{1,0:T(8,128)S(1)} %get-tuple-element.29), channel_id=1, source_target_pairs={{0,24},{8,16},{16,8},{24,0},{1,25},{9,17},{17,9},{25,1},{2,26},{10... | collective-permute-start | bytes 294920 | tf_op jit(solution)/shard_map/ppermute | solution.py:521
  7.8 5.8 %collective-permute-start.3 = (f32[64,128]{1,0:T(8,128)S(1)}, f32[64,128]{1,0:T(8,128)S(1)}, u32[]{:S(2)}, u32[]{:S(2)}) collective-permute-start(f32[64,128]{1,0:T(8,128)S(1)} %get-tuple-element.43), channel_id=1, source_target_pairs={{0,6},{2,4},{4,2},{6,0},{1,7},{3,5},{5,3},{7,1},{8,14},{10,12},{12... | collective-permute-start | bytes 98312 | tf_op jit(solution)/shard_map/ppermute | solution.py:521
  11.5 4.5 %collective-permute-start.4 = (f32[16,128]{1,0:T(8,128)S(1)}, f32[16,128]{1,0:T(8,128)S(1)}, u32[]{:S(2)}, u32[]{:S(2)}) collective-permute-start(f32[16,128]{1,0:T(8,128)S(1)} %pad_maximum_fusion.2), channel_id=1, source_target_pairs={{0,4},{2,6},{4,0},{6,2},{1,5},{3,7},{5,1},{7,3},{8,12},{10,14},{12... | collective-permute-start | bytes 24584 | tf_op jit(solution)/shard_map/ppermute | solution.py:521
  11.5 3.9 %collective-permute-start.5 = (f32[64,128]{1,0:T(8,128)S(1)}, f32[64,128]{1,0:T(8,128)S(1)}, u32[]{:S(2)}, u32[]{:S(2)}) collective-permute-start(f32[64,128]{1,0:T(8,128)S(1)} %get-tuple-element.42), channel_id=1, source_target_pairs={{0,2},{2,0},{4,6},{6,4},{1,3},{3,1},{5,7},{7,5},{8,10},{10,8},{12,... | collective-permute-start | bytes 98312 | tf_op jit(solution)/shard_map/ppermute | solution.py:521

commit v10 on v8

--- a/solution.py
+++ b/solution.py
@@ -125,8 +125,8 @@
 
 def begin(
     dims, axes, fast,
-    v_hbm, config_hbm, offset_hbm, slot_hbm, xi_hbm, strain_hbm, motion_hbm, viscosity_hbm,
-    talk_ref, self_ref, own_ref, split_ref, matrix_ref, target_ref, weight_ref, config_ref, offset_ref, viscosity_ref,
+    v_hbm, config_hbm, offset_hbm, slot_hbm, xi_hbm, strain_hbm, motion_hbm,
+    talk_ref, self_ref, own_ref, split_ref, matrix_ref, target_ref, weight_ref, config_ref, offset_ref,
     v_ref, slot_ref, xi_ref, strain_ref, motion_ref, sems,
 ):
     comps, nodes, cx, cy, cz, nconf, slots, lanes = dims
@@ -134,7 +134,7 @@
     cells = blocks * cz
     copies = fetch(
         [(v_hbm, v_ref), (offset_hbm, offset_ref), (slot_hbm, slot_ref), (config_hbm, config_ref), (xi_hbm, xi_ref),
-         (strain_hbm, strain_ref), (motion_hbm, motion_ref), (viscosity_hbm, viscosity_ref)],
+         (strain_hbm, strain_ref), (motion_hbm, motion_ref)],
         sems,
     )
 
@@ -306,9 +306,11 @@
 
 def middle(
     dims, axes, sizes, fast,
-    za_ref, con_ref, viscosity_ref, offset_ref, matrix_ref, config_ref, xa_ref, xb_ref, zb_ref, target_ref,
+    za_ref, con_ref, viscosity_hbm, offset_ref, matrix_ref, config_ref, xa_ref, xb_ref, zb_ref, target_ref,
     total_ref, hot_ref,
+    viscosity_ref, sems,
 ):
+    copies = fetch([(viscosity_hbm, viscosity_ref)], sems)
     comps, nodes, cx, cy, cz, nconf, slots, lanes = dims
     blocks = cx * cy
     face = nodes // 4
@@ -350,6 +352,7 @@
     config_rows = [config_ref[y : y + 1, :] for y in range(blocks)]
     matrix = matrix_ref[...]
 
+    copies[0].wait()
     for k in range(comps):
         pair = con_ref[2 * k * nodes : 2 * (k + 1) * nodes, :]
         ops = dot(table, pair)
@@ -559,7 +562,7 @@
         return pl.CostEstimate(flops=2 * 6 * nconf * nodes * nodes * columns, bytes_accessed=1_000_000, transcendentals=0)
 
     fast = (n_dx, n_dy, n_solid, slots) == (4, 4, 2, 64)
-    talk, mine, own, parted, matrix, targets, weights, config, offsets, visc = pl.pallas_call(
+    talk, mine, own, parted, matrix, targets, weights, config, offsets = pl.pallas_call(
         functools.partial(begin, dims, axes, fast),
         out_shape=(
             shape(32 if fast else 16, 128),
@@ -571,21 +574,20 @@
             shape(2 * nodes, lanes),
             shape(*config.shape, dtype=config.dtype),
             shape(*offsets.shape),
-            shape(*visc.shape),
         ),
-        in_specs=[hbm] * 8,
-        out_specs=(vmem,) * 10,
+        in_specs=[hbm] * 7,
+        out_specs=(vmem,) * 9,
         scratch_shapes=[
             pltpu.VMEM(v.shape, F32),
             pltpu.VMEM(targets.shape, targets.dtype),
             pltpu.VMEM(xi.shape, F32),
             pltpu.VMEM(strain.shape, F32),
             pltpu.VMEM(motion.shape, F32),
-            pltpu.SemaphoreType.DMA((8,)),
+            pltpu.SemaphoreType.DMA((7,)),
         ],
         compiler_params=params,
         name="begin",
-    )(*(pltpu.with_memory_space_constraint(x, pltpu.HBM) for x in (v, config, offsets, targets, xi, strain, motion, visc)))
+    )(*(pltpu.with_memory_space_constraint(x, pltpu.HBM) for x in (v, config, offsets, targets, xi, strain, motion)))
 
     con, xa, xb, ya, yb = pl.pallas_call(
         functools.partial(local, dims, axes),
@@ -622,12 +624,13 @@
     total, hot = pl.pallas_call(
         functools.partial(middle, dims, axes, mesh_sizes, fast),
         out_shape=(shape(comps * nodes, cells), shape(cells, 2 * lanes, dtype=BF16)),
-        in_specs=[vmem] * 10,
+        in_specs=[vmem] * 2 + [hbm] + [vmem] * 7,
+        scratch_shapes=[pltpu.VMEM(visc.shape, F32), pltpu.SemaphoreType.DMA((1,))],
         out_specs=(vmem,) * 2,
         compiler_params=params,
         cost_estimate=estimate(comps * cells),
         name="middle",
-    )(got_za, con, visc, offsets, matrix, config, got_xa, got_xb, got_zb, targets)
+    )(got_za, con, pltpu.with_memory_space_constraint(visc, pltpu.HBM), offsets, matrix, config, got_xa, got_xb, got_zb, targets)
 
     rims = pl.pallas_call(
         functools.partial(rim, dims, axes, mesh_sizes, fast),

time: 17.3 us -> 17.3 us (level)
  waiting for transfers between devices: 2.26 us -> 1.67 us
  Pallas kernels: 4.99 us -> 5.56 us
    ppermute x4, waiting for transfers between devices: 2.26 us -> 1.66 us  [flip(): lax.ppermute(x, axis, [(i, i ^ bits) for i in range(lax.axis_size(axis))])]
    pallas_call x1, Pallas kernels: 1.11 us -> 1.7 us  [shards(): pl.pallas_call(functools.partial(middle, dims, axes, mesh_sizes, fast), o...]
  transfers between devices with their start and end apart: 6 -> 6, of which waited for: 3 -> 2; matrix products, arithmetic and copies ran while one was open for 0% -> 0% of each run, Pallas kernels for 13% -> 16%
where the time goes in v10:
time: 17.3 us; the launch traced here: 17.1 us
  starting transfers between devices  9.16 us (53%)
  Pallas kernels  5.56 us (32%)
  waiting for transfers between devices  1.67 us (10%)
  between operations  0.71 us (4%)
    ppermute x4, starting transfers between devices, flip(): lax.ppermute(x, axis, [(i, i ^ bits) for i in range(lax.axis_size(axis))])  6.06 us
    ppermute x2, starting transfers between devices, swap(): return lax.ppermute(x, axis, pairs + [(j, i) for i, j in pairs])  3.1 us
    pallas_call x1, Pallas kernels, shards(): pl.pallas_call(functools.partial(begin, dims, axes, fast), out_shape=(sha...  1.72 us
    pallas_call x1, Pallas kernels, shards(): pl.pallas_call(functools.partial(middle, dims, axes, mesh_sizes, fast), o...  1.7 us
    ppermute x4, waiting for transfers between devices, flip(): lax.ppermute(x, axis, [(i, i ^ bits) for i in range(lax.axis_size(axis))])  1.66 us
    pallas_call x1, Pallas kernels, shards(): pl.pallas_call(functools.partial(after, dims, axes, fast), out_shape=(sha...  1.1 us
    pallas_call x1, Pallas kernels, shards(): pl.pallas_call(functools.partial(local, dims, axes), out_shape=(shape(2 *...  0.67 us
    pallas_call x1, Pallas kernels, shards(): pl.pallas_call(functools.partial(rim, dims, axes, mesh_sizes, fast), out_...  0.38 us
  transfers between devices with their start and end apart: 6, of which 2 were waited for; matrix products, arithmetic and copies ran while one was open for 0% of the time, Pallas kernels for 16%

profile of v10, /device:TPU:0, one launch (start us, length us, event | category | flops | bytes accessed | tf_op | source)
XLA Modules:
  0.0 17.1 jit_solution(13835873492620013027)
XLA Ops:
  0.6 1.7 %begin.1 = (f32[32,128]{1,0:T(8,128)S(1)}, f32[16,128]{1,0:T(8,128)S(1)}, f32[32,128]{1,0:T(8,128)S(1)}, bf16[384,512]{1,0:T(8,128)(2,1)S(1)}, bf16[512,192]{1,0...) custom-call(f32[768,128]{1,0:T(8,128)} %bitcast.14, ...), custom_call_target="tpu_custom_call" | custom-call | tf_op jit(solution)/shard_map/begin/pallas_call | solution.py:565
  2.4 3.0 %collective-permute-start = (f32[32,128]{1,0:T(8,128)S(1)}, f32[32,128]{1,0:T(8,128)S(1)}, u32[]{:S(2)}, u32[]{:S(2)}) collective-permute-start(f32[32,128]{1,0:T(8,128)S(1)} %get-tuple-element.20), channel_id=1, source_target_pairs={{0,1},{1,0},{2,3},{3,2},{4,5},{5,4},{6,7},{7,6},{8,9},{9,8},{10,11... | collective-permute-start | bytes 49160 | tf_op jit(solution)/shard_map/ppermute | solution.py:514
  5.4 0.7 %local.1 = (bf16[384,512]{1,0:T(8,128)(2,1)S(1)}, f32[48,512]{1,0:T(8,128)S(1)}, f32[48,512]{1,0:T(8,128)S(1)}, f32[48,128]{1,0:T(8,128)S(1)}, f32[48,128]{1,0:T(8,128)S(1)}) custom-call(bf16[384,512]{1,0:T(8,128)(2,1)S(1)} %get-tuple-element.21.split_ref, f32[512,64]{1,0:T(8,128)S(1)} %get-tuple-element.22.offset_ref, s32[4,128]{1,0:T(4,128)S(1)} %get-tuple-element.23.config_ref), custom_call_target="tpu_custom_call" | custom-call | flops 603979776 | bytes 1000000 | tf_op jit(solution)/shard_map/local/pallas_call | solution.py:592
  6.1 0.1 collective-permute-start.1
  6.1 1.6 %collective-permute-start.2 = (f32[48,512]{1,0:T(8,128)S(1)}, f32[48,512]{1,0:T(8,128)S(1)}, u32[]{:S(2)}, u32[]{:S(2)}) collective-permute-start(f32[48,512]{1,0:T(8,128)S(1)} %get-tuple-element.27), channel_id=1, source_target_pairs={{0,24},{8,16},{16,8},{24,0},{1,25},{9,17},{17,9},{25,1},{2,26},{10... | collective-permute-start | bytes 294920 | tf_op jit(solution)/shard_map/ppermute | solution.py:518
  7.8 0.0 collective-permute-done.za_ref.zb_ref
  7.8 3.7 %collective-permute-start.3 = (f32[64,128]{1,0:T(8,128)S(1)}, f32[64,128]{1,0:T(8,128)S(1)}, u32[]{:S(2)}, u32[]{:S(2)}) collective-permute-start(f32[64,128]{1,0:T(8,128)S(1)} %get-tuple-element.41), channel_id=1, source_target_pairs={{0,6},{2,4},{4,2},{6,0},{1,7},{3,5},{5,3},{7,1},{8,14},{10,12},{12... | collective-permute-start | bytes 98312 | tf_op jit(solution)/shard_map/ppermute | solution.py:518
  11.5 0.0 collective-permute-start.4
  11.5 0.8 %collective-permute-start.5 = (f32[64,128]{1,0:T(8,128)S(1)}, f32[64,128]{1,0:T(8,128)S(1)}, u32[]{:S(2)}, u32[]{:S(2)}) collective-permute-start(f32[64,128]{1,0:T(8,128)S(1)} %get-tuple-element.40), channel_id=1, source_target_pairs={{0,2},{2,0},{4,6},{6,4},{1,3},{3,1},{5,7},{7,5},{8,10},{10,8},{12,... | collective-permute-start | bytes 98312 | tf_op jit(solution)/shard_map/ppermute | solution.py:518
  12.3 0.0 collective-permute-done.1.xa_ref
  12.3 0.0 collective-permute-done.2.xb_ref
  12.3 1.7 %middle.1 = (f32[192,512]{1,0:T(8,128)S(1)}, bf16[512,256]{1,0:T(8,128)(2,1)S(1)}) custom-call(f32[32,128]{1,0:T(8,128)S(1)} %collective-permute-done.za_ref.zb_ref, bf16[384,512]{1,0:T(8,128)(2,1)S(1)} %get-tuple-element.24.con_ref, f32[4,128]{1,0:T(4,128)} %bitcast.23, f32[512,64]{1,0:T(8,128)S(1)} %get-tuple-element.22.offset_ref, ...), custom_call_target="tpu_custom_call" | custom-call | flops 603979776 | bytes 1000000 | tf_op jit(solution)/shard_map/middle/pallas_call | solution.py:624
  14.0 0.0 collective-permute-done.3.yb_ref.refs_0_
  14.0 1.4 %collective-permute-done.5.ya_ref.refs_2_ = f32[64,128]{1,0:T(8,128)S(1)} collective-permute-done((f32[64,128]{1,0:T(8,128)S(1)}, f32[64,128]{1,0:T(8,128)S(1)}, u32[]{:S(2)}, u32[]{:S(2)}) %collective-permute-start.5) | collective-permute-done | bytes 32800 | tf_op jit(solution)/shard_map/ppermute | solution.py:518
  15.4 0.4 %rim.1.refs_4_ = f32[192,256]{1,0:T(8,128)S(1)} custom-call(f32[192,512]{1,0:T(8,128)S(1)} %get-tuple-element.29.total_ref, f32[64,128]{1,0:T(8,128)S(1)} %collective-permute-done.3.yb_ref.refs_0_, f32[64,128]{1,0:T(8,128)S(1)} %collective-permute-done.5.ya_ref.refs_2_, bf16[512,192]{1,0:T(8,128)(2,1)S(1)} %get-tuple-element.25.matrix_ref, ...), custom_call_target="tpu_custom_call" | custom-call | flops 603979776 | bytes 1000000 | tf_op jit(solution)/shard_map/rim/pallas_call | solution.py:635
  15.8 0.2 %collective-permute-done.4.refs_1_ = f32[16,128]{1,0:T(8,128)S(1)} collective-permute-done((f32[16,128]{1,0:T(8,128)S(1)}, f32[16,128]{1,0:T(8,128)S(1)}, u32[]{:S(2)}, u32[]{:S(2)}) %collective-permute-start.4) | collective-permute-done | bytes 8224 | tf_op jit(solution)/shard_map/ppermute | solution.py:518
  16.0 1.1 %after.1 = (f32[768,128]{1,0:T(8,128)}, f32[9,1,64]{2,1,0:T(1,128)}) custom-call(f32[192,512]{1,0:T(8,128)S(1)} %get-tuple-element.29.total_ref, f32[64,128]{1,0:T(8,128)S(1)} %collective-permute-done.3.yb_ref.refs_0_, f32[16,128]{1,0:T(8,128)S(1)} %collective-permute-done.4.refs_1_, f32[64,128]{1,0:T(8,128)S(1)} %collective-permute-done.5.ya_ref.refs_2_, ...), custom_call_target="tpu_custom_call" | custom-call | tf_op jit(solution)/shard_map/after/pallas_call | solution.py:645
  (5 shorter events, 0.0 us)
Async XLA Ops:
  2.4 5.4 %collective-permute-start = (f32[32,128]{1,0:T(8,128)S(1)}, f32[32,128]{1,0:T(8,128)S(1)}, u32[]{:S(2)}, u32[]{:S(2)}) collective-permute-start(f32[32,128]{1,0:T(8,128)S(1)} %get-tuple-element.20), channel_id=1, source_target_pairs={{0,1},{1,0},{2,3},{3,2},{4,5},{5,4},{6,7},{7,6},{8,9},{9,8},{10,11... | collective-permute-start | bytes 49160 | tf_op jit(solution)/shard_map/ppermute | solution.py:514
  6.1 6.2 %collective-permute-start.1 = (f32[48,512]{1,0:T(8,128)S(1)}, f32[48,512]{1,0:T(8,128)S(1)}, u32[]{:S(2)}, u32[]{:S(2)}) collective-permute-start(f32[48,512]{1,0:T(8,128)S(1)} %get-tuple-element.26), channel_id=1, source_target_pairs={{0,8},{16,24},{8,0},{24,16},{1,9},{17,25},{9,1},{25,17},{2,10},{18... | collective-permute-start | bytes 294920 | tf_op jit(solution)/shard_map/ppermute | solution.py:514
  6.1 6.1 %collective-permute-start.2 = (f32[48,512]{1,0:T(8,128)S(1)}, f32[48,512]{1,0:T(8,128)S(1)}, u32[]{:S(2)}, u32[]{:S(2)}) collective-permute-start(f32[48,512]{1,0:T(8,128)S(1)} %get-tuple-element.27), channel_id=1, source_target_pairs={{0,24},{8,16},{16,8},{24,0},{1,25},{9,17},{17,9},{25,1},{2,26},{10... | collective-permute-start | bytes 294920 | tf_op jit(solution)/shard_map/ppermute | solution.py:518
  7.8 6.2 %collective-permute-start.3 = (f32[64,128]{1,0:T(8,128)S(1)}, f32[64,128]{1,0:T(8,128)S(1)}, u32[]{:S(2)}, u32[]{:S(2)}) collective-permute-start(f32[64,128]{1,0:T(8,128)S(1)} %get-tuple-element.41), channel_id=1, source_target_pairs={{0,6},{2,4},{4,2},{6,0},{1,7},{3,5},{5,3},{7,1},{8,14},{10,12},{12... | collective-permute-start | bytes 98312 | tf_op jit(solution)/shard_map/ppermute | solution.py:518
  11.5 4.5 %collective-permute-start.4 = (f32[16,128]{1,0:T(8,128)S(1)}, f32[16,128]{1,0:T(8,128)S(1)}, u32[]{:S(2)}, u32[]{:S(2)}) collective-permute-start(f32[16,128]{1,0:T(8,128)S(1)} %pad_maximum_fusion.2), channel_id=1, source_target_pairs={{0,4},{2,6},{4,0},{6,2},{1,5},{3,7},{5,1},{7,3},{8,12},{10,14},{12... | collective-permute-start | bytes 24584 | tf_op jit(solution)/shard_map/ppermute | solution.py:518
  11.5 3.9 %collective-permute-start.5 = (f32[64,128]{1,0:T(8,128)S(1)}, f32[64,128]{1,0:T(8,128)S(1)}, u32[]{:S(2)}, u32[]{:S(2)}) collective-permute-start(f32[64,128]{1,0:T(8,128)S(1)} %get-tuple-element.40), channel_id=1, source_target_pairs={{0,2},{2,0},{4,6},{6,4},{1,3},{3,1},{5,7},{7,5},{8,10},{10,8},{12,... | collective-permute-start | bytes 98312 | tf_op jit(solution)/shard_map/ppermute | solution.py:518

commit v11 on v8

--- a/solution.py
+++ b/solution.py
@@ -182,6 +182,15 @@
         weights.append(basis[j] + configured(product[:, j * lanes : (j + 1) * lanes], config_twice, nconf))
         weight_ref[j * nodes : (j + 1) * nodes, :] = weights[j]
 
+    count = comps * nodes // 16
+    ends = jnp.concatenate([r[:, columns - 128 :] for r in raw], axis=0)
+    lane = iota((16, 128), 1)
+    at_end = 128 - wide
+    packed = jnp.broadcast_to(pltpu.roll(config[:, columns - 128 :], (count * wide - at_end) % 128, axis=1), (16, 128))
+    for g in range(count):
+        group = pltpu.roll(ends[16 * g : 16 * (g + 1)], (g * wide - at_end) % 128, axis=1)
+        packed = jnp.where((lane >= g * wide) & (lane < (g + 1) * wide), group, packed)
+    talk_ref[talk_ref.shape[0] - 16 :, :] = packed
     for k in range(comps):
         value = twice(raw[k])
         for j in range(2):
@@ -197,15 +206,6 @@
     for i in (12, 28):
         own_ref[i : i + 4, :] = jnp.zeros((4, lanes), F32)
 
-    count = comps * nodes // 16
-    ends = jnp.concatenate([r[:, columns - 128 :] for r in raw], axis=0)
-    lane = iota((16, 128), 1)
-    at_end = 128 - wide
-    packed = jnp.broadcast_to(pltpu.roll(config[:, columns - 128 :], (count * wide - at_end) % 128, axis=1), (16, 128))
-    for g in range(count):
-        group = pltpu.roll(ends[16 * g : 16 * (g + 1)], (g * wide - at_end) % 128, axis=1)
-        packed = jnp.where((lane >= g * wide) & (lane < (g + 1) * wide), group, packed)
-    talk_ref[talk_ref.shape[0] - 16 :, :] = packed
     if fast:
         parts = jnp.where(lane < slots, own_ref[0:16, :], own_ref[16:32, :])
         self_ref[...] = parts

time: 17.3 us -> 17.3 us (level)
  no operation moved by 1% of the time
where the time goes in v11:
time: 17.3 us; the launch traced here: 17.1 us
  starting transfers between devices  9.16 us (53%)
  Pallas kernels  4.99 us (29%)
  waiting for transfers between devices  2.26 us (13%)
  between operations  0.69 us (4%)
    ppermute x4, starting transfers between devices, flip(): lax.ppermute(x, axis, [(i, i ^ bits) for i in range(lax.axis_size(axis))])  6.06 us
    ppermute x2, starting transfers between devices, swap(): return lax.ppermute(x, axis, pairs + [(j, i) for i, j in pairs])  3.1 us
    ppermute x4, waiting for transfers between devices, flip(): lax.ppermute(x, axis, [(i, i ^ bits) for i in range(lax.axis_size(axis))])  2.26 us
    pallas_call x1, Pallas kernels, shards(): pl.pallas_call(functools.partial(begin, dims, axes, fast), out_shape=(sha...  1.73 us
    pallas_call x1, Pallas kernels, shards(): pl.pallas_call(functools.partial(middle, dims, axes, mesh_sizes, fast), o...  1.11 us
    pallas_call x1, Pallas kernels, shards(): pl.pallas_call(functools.partial(after, dims, axes, fast), out_shape=(sha...  1.1 us
    pallas_call x1, Pallas kernels, shards(): pl.pallas_call(functools.partial(local, dims, axes), out_shape=(shape(2 *...  0.67 us
    pallas_call x1, Pallas kernels, shards(): pl.pallas_call(functools.partial(rim, dims, axes, mesh_sizes, fast), out_...  0.38 us
  transfers between devices with their start and end apart: 6, of which 3 were waited for; matrix products, arithmetic and copies ran while one was open for 0% of the time, Pallas kernels for 13%

profile of v11, /device:TPU:0, one launch (start us, length us, event | category | flops | bytes accessed | tf_op | source)
XLA Modules:
  0.0 17.1 jit_solution(12722701122459380402)
XLA Ops:
  0.6 1.7 %begin.1 = (f32[32,128]{1,0:T(8,128)S(1)}, f32[16,128]{1,0:T(8,128)S(1)}, f32[32,128]{1,0:T(8,128)S(1)}, bf16[384,512]{1,0:T(8,128)(2,1)S(1)}, bf16[512,192]{1,0...) custom-call(f32[768,128]{1,0:T(8,128)} %bitcast.14, ...), custom_call_target="tpu_custom_call" | custom-call | tf_op jit(solution)/shard_map/begin/pallas_call | solution.py:562
  2.4 3.0 %collective-permute-start = (f32[32,128]{1,0:T(8,128)S(1)}, f32[32,128]{1,0:T(8,128)S(1)}, u32[]{:S(2)}, u32[]{:S(2)}) collective-permute-start(f32[32,128]{1,0:T(8,128)S(1)} %get-tuple-element.21), channel_id=1, source_target_pairs={{0,1},{1,0},{2,3},{3,2},{4,5},{5,4},{6,7},{7,6},{8,9},{9,8},{10,11... | collective-permute-start | bytes 49160 | tf_op jit(solution)/shard_map/ppermute | solution.py:511
  5.4 0.7 %local.1 = (bf16[384,512]{1,0:T(8,128)(2,1)S(1)}, f32[48,512]{1,0:T(8,128)S(1)}, f32[48,512]{1,0:T(8,128)S(1)}, f32[48,128]{1,0:T(8,128)S(1)}, f32[48,128]{1,0:T(8,128)S(1)}) custom-call(bf16[384,512]{1,0:T(8,128)(2,1)S(1)} %get-tuple-element.22.split_ref, f32[512,64]{1,0:T(8,128)S(1)} %get-tuple-element.23.offset_ref, s32[4,128]{1,0:T(4,128)S(1)} %get-tuple-element.24.config_ref), custom_call_target="tpu_custom_call" | custom-call | flops 603979776 | bytes 1000000 | tf_op jit(solution)/shard_map/local/pallas_call | solution.py:590
  6.1 0.1 collective-permute-start.1
  6.2 1.6 %collective-permute-start.2 = (f32[48,512]{1,0:T(8,128)S(1)}, f32[48,512]{1,0:T(8,128)S(1)}, u32[]{:S(2)}, u32[]{:S(2)}) collective-permute-start(f32[48,512]{1,0:T(8,128)S(1)} %get-tuple-element.29), channel_id=1, source_target_pairs={{0,24},{8,16},{16,8},{24,0},{1,25},{9,17},{17,9},{25,1},{2,26},{10... | collective-permute-start | bytes 294920 | tf_op jit(solution)/shard_map/ppermute | solution.py:515
  7.8 0.0 collective-permute-done.za_ref.zb_ref
  7.8 3.7 %collective-permute-start.3 = (f32[64,128]{1,0:T(8,128)S(1)}, f32[64,128]{1,0:T(8,128)S(1)}, u32[]{:S(2)}, u32[]{:S(2)}) collective-permute-start(f32[64,128]{1,0:T(8,128)S(1)} %get-tuple-element.43), channel_id=1, source_target_pairs={{0,6},{2,4},{4,2},{6,0},{1,7},{3,5},{5,3},{7,1},{8,14},{10,12},{12... | collective-permute-start | bytes 98312 | tf_op jit(solution)/shard_map/ppermute | solution.py:515
  11.5 0.0 collective-permute-start.4
  11.5 0.8 %collective-permute-start.5 = (f32[64,128]{1,0:T(8,128)S(1)}, f32[64,128]{1,0:T(8,128)S(1)}, u32[]{:S(2)}, u32[]{:S(2)}) collective-permute-start(f32[64,128]{1,0:T(8,128)S(1)} %get-tuple-element.42), channel_id=1, source_target_pairs={{0,2},{2,0},{4,6},{6,4},{1,3},{3,1},{5,7},{7,5},{8,10},{10,8},{12,... | collective-permute-start | bytes 98312 | tf_op jit(solution)/shard_map/ppermute | solution.py:515
  12.3 0.0 collective-permute-done.1.xa_ref
  12.3 0.0 collective-permute-done.2.xb_ref
  12.3 1.1 %middle.1 = (f32[192,512]{1,0:T(8,128)S(1)}, bf16[512,256]{1,0:T(8,128)(2,1)S(1)}) custom-call(f32[32,128]{1,0:T(8,128)S(1)} %collective-permute-done.za_ref.zb_ref, bf16[384,512]{1,0:T(8,128)(2,1)S(1)} %get-tuple-element.25.con_ref, f32[4,128]{1,0:T(4,128)S(1)} %get-tuple-element.26.viscosity_ref, f32[512,64]{1,0:T(8,128)S(1)} %get-tuple-element.23.offset_ref, ...), custom_call_target="tpu_custom_call" | custom-call | flops 603979776 | bytes 1000000 | tf_op jit(solution)/shard_map/middle/pallas_call | solution.py:622
  13.4 0.2 %collective-permute-done.3.yb_ref.refs_0_ = f32[64,128]{1,0:T(8,128)S(1)} collective-permute-done((f32[64,128]{1,0:T(8,128)S(1)}, f32[64,128]{1,0:T(8,128)S(1)}, u32[]{:S(2)}, u32[]{:S(2)}) %collective-permute-start.3) | collective-permute-done | bytes 32800 | tf_op jit(solution)/shard_map/ppermute | solution.py:515
  13.6 1.8 %collective-permute-done.5.ya_ref.refs_2_ = f32[64,128]{1,0:T(8,128)S(1)} collective-permute-done((f32[64,128]{1,0:T(8,128)S(1)}, f32[64,128]{1,0:T(8,128)S(1)}, u32[]{:S(2)}, u32[]{:S(2)}) %collective-permute-start.5) | collective-permute-done | bytes 32800 | tf_op jit(solution)/shard_map/ppermute | solution.py:515
  15.4 0.4 %rim.1.refs_4_ = f32[192,256]{1,0:T(8,128)S(1)} custom-call(f32[192,512]{1,0:T(8,128)S(1)} %get-tuple-element.31.total_ref, f32[64,128]{1,0:T(8,128)S(1)} %collective-permute-done.3.yb_ref.refs_0_, f32[64,128]{1,0:T(8,128)S(1)} %collective-permute-done.5.ya_ref.refs_2_, bf16[512,192]{1,0:T(8,128)(2,1)S(1)} %get-tuple-element.27.matrix_ref, ...), custom_call_target="tpu_custom_call" | custom-call | flops 603979776 | bytes 1000000 | tf_op jit(solution)/shard_map/rim/pallas_call | solution.py:632
  15.8 0.2 %collective-permute-done.4.refs_1_ = f32[16,128]{1,0:T(8,128)S(1)} collective-permute-done((f32[16,128]{1,0:T(8,128)S(1)}, f32[16,128]{1,0:T(8,128)S(1)}, u32[]{:S(2)}, u32[]{:S(2)}) %collective-permute-start.4) | collective-permute-done | bytes 8224 | tf_op jit(solution)/shard_map/ppermute | solution.py:515
  16.0 1.1 %after.1 = (f32[768,128]{1,0:T(8,128)}, f32[9,1,64]{2,1,0:T(1,128)}) custom-call(f32[192,512]{1,0:T(8,128)S(1)} %get-tuple-element.31.total_ref, f32[64,128]{1,0:T(8,128)S(1)} %collective-permute-done.3.yb_ref.refs_0_, f32[16,128]{1,0:T(8,128)S(1)} %collective-permute-done.4.refs_1_, f32[64,128]{1,0:T(8,128)S(1)} %collective-permute-done.5.ya_ref.refs_2_, ...), custom_call_target="tpu_custom_call" | custom-call | tf_op jit(solution)/shard_map/after/pallas_call | solution.py:642
  (5 shorter events, 0.0 us)
Async XLA Ops:
  2.4 5.4 %collective-permute-start = (f32[32,128]{1,0:T(8,128)S(1)}, f32[32,128]{1,0:T(8,128)S(1)}, u32[]{:S(2)}, u32[]{:S(2)}) collective-permute-start(f32[32,128]{1,0:T(8,128)S(1)} %get-tuple-element.21), channel_id=1, source_target_pairs={{0,1},{1,0},{2,3},{3,2},{4,5},{5,4},{6,7},{7,6},{8,9},{9,8},{10,11... | collective-permute-start | bytes 49160 | tf_op jit(solution)/shard_map/ppermute | solution.py:511
  6.1 6.2 %collective-permute-start.1 = (f32[48,512]{1,0:T(8,128)S(1)}, f32[48,512]{1,0:T(8,128)S(1)}, u32[]{:S(2)}, u32[]{:S(2)}) collective-permute-start(f32[48,512]{1,0:T(8,128)S(1)} %get-tuple-element.28), channel_id=1, source_target_pairs={{0,8},{16,24},{8,0},{24,16},{1,9},{17,25},{9,1},{25,17},{2,10},{18... | collective-permute-start | bytes 294920 | tf_op jit(solution)/shard_map/ppermute | solution.py:511
  6.2 6.1 %collective-permute-start.2 = (f32[48,512]{1,0:T(8,128)S(1)}, f32[48,512]{1,0:T(8,128)S(1)}, u32[]{:S(2)}, u32[]{:S(2)}) collective-permute-start(f32[48,512]{1,0:T(8,128)S(1)} %get-tuple-element.29), channel_id=1, source_target_pairs={{0,24},{8,16},{16,8},{24,0},{1,25},{9,17},{17,9},{25,1},{2,26},{10... | collective-permute-start | bytes 294920 | tf_op jit(solution)/shard_map/ppermute | solution.py:515
  7.8 5.8 %collective-permute-start.3 = (f32[64,128]{1,0:T(8,128)S(1)}, f32[64,128]{1,0:T(8,128)S(1)}, u32[]{:S(2)}, u32[]{:S(2)}) collective-permute-start(f32[64,128]{1,0:T(8,128)S(1)} %get-tuple-element.43), channel_id=1, source_target_pairs={{0,6},{2,4},{4,2},{6,0},{1,7},{3,5},{5,3},{7,1},{8,14},{10,12},{12... | collective-permute-start | bytes 98312 | tf_op jit(solution)/shard_map/ppermute | solution.py:515
  11.5 4.5 %collective-permute-start.4 = (f32[16,128]{1,0:T(8,128)S(1)}, f32[16,128]{1,0:T(8,128)S(1)}, u32[]{:S(2)}, u32[]{:S(2)}) collective-permute-start(f32[16,128]{1,0:T(8,128)S(1)} %pad_maximum_fusion.2), channel_id=1, source_target_pairs={{0,4},{2,6},{4,0},{6,2},{1,5},{3,7},{5,1},{7,3},{8,12},{10,14},{12... | collective-permute-start | bytes 24584 | tf_op jit(solution)/shard_map/ppermute | solution.py:515
  11.5 3.9 %collective-permute-start.5 = (f32[64,128]{1,0:T(8,128)S(1)}, f32[64,128]{1,0:T(8,128)S(1)}, u32[]{:S(2)}, u32[]{:S(2)}) collective-permute-start(f32[64,128]{1,0:T(8,128)S(1)} %get-tuple-element.42), channel_id=1, source_target_pairs={{0,2},{2,0},{4,6},{6,4},{1,3},{3,1},{5,7},{7,5},{8,10},{10,8},{12,... | collective-permute-start | bytes 98312 | tf_op jit(solution)/shard_map/ppermute | solution.py:515
